TPU v7x, 512 devices: a whole 4x4x16 slice. The times are simulated.
512 devices in a mesh: rep: 64 (over z, x), tp: 8 (over y, core).
Axes of the slice: x: 4, y: 4, z: 16, core: 2. Of those that a mesh axis runs over, the one named last changes fastest.
Arguments:
- first_hidden_rows: bfloat16 [8192, 3072], P('rep', 'tp'), may hold values from -40 to 40
- norm_scale: float32 [3072], P('tp'), may hold values from 0.1 to 1.9
- projection_weight: bfloat16 [3072, 3072], P('tp'), may hold values from -0.109375 to 0.109375
- down_weights: bfloat16 [256, 3072, 64], P('rep', 'tp'), may hold values from -0.109375 to 0.109375
- up_weights: bfloat16 [256, 64, 3072], P('rep', None, 'tp'), may hold values from -0.75 to 0.75
- requests: int32 [64, 64], replicated, may hold values from 0 to 255, as said below
Outputs:
- drafted: bfloat16 [2, 8192, 3072], P(None, 'rep', 'tp')
Inputs may be any that keep to these rules, and one draw needn't show every extreme that they name: `requests`: adapter a is held by replica group a // 4. Each row g names adapters of every holding group, 1 entries for each of them.
All inputs are finite; a program needn't handle non-finite values.
Results may differ from a plain program's by a relative error of at most 0.019.
Values may be sent and summed in bfloat16 or wider, within the bound.
No kernel may reach another device: no remote copies, remote signals or barrier semaphores. Data moves between devices by JAX's collectives and lax.ppermute only.
A program may use at most 64 MiB of HBM per device.

v0:
```python
import jax
import jax.numpy as jnp
from jax import lax
from jax.sharding import PartitionSpec as P

DRAFT = 2


EPSILON = 1e-06


def rank_total(partial_value):
    return lax.psum(partial_value.astype(jnp.bfloat16), "tp").astype(jnp.float32)


def normed(current, norm_scale, full_width):
    squares = lax.psum(jnp.sum(current * current, axis=1), "tp")
    factor = lax.rsqrt(squares / full_width + EPSILON)
    return (current * factor[:, None] * norm_scale[None, :]).astype(jnp.bfloat16)


def shards(first_hidden_rows, norm_scale, projection_weight, down_weights, up_weights, requests):
    groups = lax.axis_size("rep")
    feature_portion = first_hidden_rows.shape[1]
    full_width = feature_portion * lax.axis_size("tp")
    kept_adapters = down_weights.shape[0]
    rank_span = down_weights.shape[2]
    req_count = requests.shape[1]
    local_rows = first_hidden_rows.shape[0]
    block_rows = local_rows // req_count
    slot_count = req_count // groups
    owners = requests // kept_adapters
    later_pos = lax.broadcasted_iota(jnp.int32, (req_count, req_count), 0)
    other_pos = lax.broadcasted_iota(jnp.int32, (req_count, req_count), 1)
    earlier = other_pos < later_pos
    slot_of = jnp.sum(
        ((owners[:, :, None] == owners[:, None, :]) & earlier[None, :, :]).astype(jnp.int32), axis=2
    )
    myself = lax.axis_index("rep")
    my_flat = jnp.take(owners, myself, axis=0) * slot_count + jnp.take(slot_of, myself, axis=0)
    slot_ids = jnp.arange(slot_count, dtype=jnp.int32)
    matches = (owners[:, None, :] == myself) & (slot_of[:, None, :] == slot_ids[None, :, None])
    adapter_found = jnp.any(matches, axis=2).astype(jnp.bfloat16)
    local_index = jnp.sum(jnp.where(matches, requests[:, None, :] % kept_adapters, 0), axis=2)
    picked_down = jnp.take(down_weights, local_index, axis=0) * adapter_found[:, :, None, None]
    picked_up = jnp.take(up_weights, local_index, axis=0) * adapter_found[:, :, None, None]
    got_a, got_b = (
        lax.all_to_all(picked_down, "rep", split_axis=0, concat_axis=0, tiled=True),
        lax.all_to_all(picked_up, "rep", split_axis=0, concat_axis=0, tiled=True),
    )
    mine_a = jnp.take(
        got_a.reshape(groups * slot_count, feature_portion, rank_span), my_flat, axis=0
    )
    mine_b = jnp.take(
        got_b.reshape(groups * slot_count, rank_span, feature_portion), my_flat, axis=0
    )
    draft_states = first_hidden_rows
    outputs = []
    for draft_step in range(DRAFT):
        widened_output = draft_states.astype(jnp.float32)
        normalized_rows = normed(widened_output, norm_scale, full_width)
        partial_value = jnp.dot(
            normalized_rows, projection_weight, preferred_element_type=jnp.float32
        )
        base_output = lax.psum_scatter(
            partial_value.astype(jnp.bfloat16), "tp", scatter_dimension=1, tiled=True
        ).astype(jnp.float32)
        blocks = normalized_rows.reshape(req_count, block_rows, feature_portion)
        rank_part = jnp.einsum("jbd,jdr->jbr", blocks, mine_a, preferred_element_type=jnp.float32)
        rank_rows = rank_total(rank_part).astype(jnp.bfloat16)
        adapter_update = jnp.einsum(
            "jbr,jrd->jbd", rank_rows, mine_b, preferred_element_type=jnp.float32
        ).astype(jnp.bfloat16)
        draft_states = (
            widened_output
            + base_output
            + adapter_update.reshape(local_rows, feature_portion).astype(jnp.float32)
        ).astype(jnp.bfloat16)
        outputs.append(draft_states)
    return jnp.stack(outputs)


def solution(mesh):
    return jax.shard_map(
        shards,
        mesh=mesh,
        in_specs=(
            P("rep", "tp"),
            P("tp"),
            P("tp", None),
            P("rep", "tp", None),
            P("rep", None, "tp"),
            P(),
        ),
        out_specs=P(None, "rep", "tp"),
        check_vma=False,
    )
```

profile of v0, /device:TPU:1, one launch (start us, length us, event | category | flops | bytes accessed | tf_op | source)
XLA Modules:
  0.0 392.3 jit_solution(18235282135278220102)
XLA Ops:
  6.5 0.0 copy-start
  6.5 0.0 copy-start.1
  6.6 1.0 add_select_fusion.1
  7.5 1.9 convert_reduce_fusion
  9.4 0.9 fusion.36
  10.3 0.9 fusion.24
  11.2 0.0 copy-done.1
  11.2 2.7 gather_fusion
  13.9 4.1 %fusion.1 = bf16[64,1,384,64]{2,3,1,0:T(8,128)(2,1)} fusion(bf16[64,384,64]{1,2,0:T(8,128)(2,1)} %gather_fusion, pred[64]{0:T(512)(128)(4,1)S(1)} %compare_and_fusion.1, bf16[64]{0:T(256)(128)(2,1)S(1)} %convert_element_type.75), kind=kLoop, calls=%fused_computation.9 | loop fusion | flops 3145728 | bytes 6291648 | tf_op jit(solution)/shard_map/mul | solution.py:45
  18.0 0.0 copy-start.2
  18.0 19.5 %all-to-all-start = ((bf16[64,1,384,64]{2,3,1,0:T(8,128)(2,1)}), bf16[64,1,384,64]{2,3,1,0:T(8,128)(2,1)}, u32[]{:S(2)}, u32[]{:S(2)}) async-start(bf16[64,1,384,64]{2,3,1,0:T(8,128)(2,1)} %fusion.1), calls=%async_computation | async-start | bytes 6291456 | tf_op jit(solution)/shard_map/all_to_all | solution.py:48
  37.5 0.0 copy-done.2
  37.5 2.6 gather_fusion.2
  40.1 4.0 %fusion = bf16[64,1,64,384]{3,2,1,0:T(8,128)(2,1)} fusion(bf16[64,64,384]{2,1,0:T(8,128)(2,1)} %gather_fusion.2, pred[64]{0:T(512)(128)(4,1)S(1)} %compare_and_fusion.1, bf16[64]{0:T(256)(128)(2,1)S(1)} %convert_element_type.75), kind=kLoop, calls=%fused_computation.7 | loop fusion | flops 3145728 | bytes 6291648 | tf_op jit(solution)/shard_map/mul | solution.py:46
  44.2 0.0 copy-start.3
  44.2 0.0 copy-start.4
  44.2 133.4 %all-to-all-done = bf16[64,1,384,64]{2,3,1,0:T(8,128)(2,1)} async-done(((bf16[64,1,384,64]{2,3,1,0:T(8,128)(2,1)}), bf16[64,1,384,64]{2,3,1,0:T(8,128)(2,1)}, u32[]{:S(2)}, u32[]{:S(2)}) %all-to-all-start) | async-done | bytes 3145760 | tf_op jit(solution)/shard_map/all_to_all | solution.py:48
  177.6 10.5 %all-to-all-start.1 = ((bf16[64,1,64,384]{3,2,1,0:T(8,128)(2,1)}), bf16[64,1,64,384]{3,2,1,0:T(8,128)(2,1)}, u32[]{:S(2)}, u32[]{:S(2)}) async-start(bf16[64,1,64,384]{3,2,1,0:T(8,128)(2,1)} %fusion), calls=%async_computation.1 | async-start | bytes 6291456 | tf_op jit(solution)/shard_map/all_to_all | solution.py:49
  188.1 0.0 reduce-scatter.7.cloned.1.call-start
  188.1 0.0 copy-done.3
  188.2 0.1 fusion.12
  188.3 13.8 %psum.28 = f32[128]{0:T(128)S(1)} all-reduce(f32[128]{0:T(128)S(1)} %fusion.12), channel_id=1, replica_groups=mesh['rep'=64,'tp'=8] {'tp'}, use_global_device_ids=true, to_apply=%region_1.2 | all-reduce | flops 128 | bytes 1024 | tf_op jit(solution)/shard_map/psum | solution.py:17
  202.1 0.0 copy-done.4
  202.1 0.1 fusion.14
  202.2 0.0 copy-done
  202.2 0.6 convolution_convert_fusion.1
  202.8 1.2 copy.7
  204.0 0.0 reduce-scatter.7.cloned.1.call-update
  204.0 0.0 reduce-scatter.9.cloned.1.call-start
  204.1 38.1 %reduce-scatter.7.cloned.1.call-done = bf16[384,128]{1,0:T(8,128)(2,1)} async-done(((bf16[3072,128]{1,0:T(8,128)(2,1)}), bf16[384,128]{1,0:T(8,128)(2,1)}) %reduce-scatter.7.cloned.1.call-update) | async-done | bytes 98320
  242.3 1.0 copy.8
  243.3 4.6 %gather_fusion.1 = bf16[64,384,64]{1,2,0:T(8,128)(2,1)} fusion(bf16[64,384,64]{1,2,0:T(8,128)(2,1)} %bitcast.5, s32[1024]{0:T(1024)S(1)} %pad_clamp_fusion), kind=kCustom, calls=%fused_computation.1 | custom fusion | bytes 6291712 | tf_op jit(solution)/shard_map/jit(_take)/gather | solution.py:51
  247.9 3.1 fusion.10
  251.0 25.1 %psum.29 = bf16[64,2,64]{2,1,0:T(2,128)(2,1)S(1)} all-reduce(bf16[64,2,64]{2,1,0:T(2,128)(2,1)S(1)} %fusion.10), channel_id=1, replica_groups=mesh['rep'=64,'tp'=8] {'tp'}, use_global_device_ids=true, to_apply=%region_6.8 | all-reduce | flops 8192 | bytes 32768 | tf_op jit(solution)/shard_map/psum | solution.py:13
  276.1 50.2 %all-to-all-done.1 = bf16[64,1,64,384]{3,2,1,0:T(8,128)(2,1)} async-done(((bf16[64,1,64,384]{3,2,1,0:T(8,128)(2,1)}), bf16[64,1,64,384]{3,2,1,0:T(8,128)(2,1)}, u32[]{:S(2)}, u32[]{:S(2)}) %all-to-all-start.1) | async-done | bytes 3145760 | tf_op jit(solution)/shard_map/all_to_all | solution.py:49
  326.3 4.5 %gather_fusion.3 = bf16[64,64,384]{2,1,0:T(8,128)(2,1)} fusion(bf16[64,64,384]{2,1,0:T(8,128)(2,1)} %bitcast.7, s32[1024]{0:T(1024)S(1)} %pad_clamp_fusion), kind=kCustom, calls=%fused_computation.3 | custom fusion | bytes 6291712 | tf_op jit(solution)/shard_map/jit(_take)/gather | solution.py:54
  330.9 2.6 fusion.7
  333.5 0.1 reshape.159
  333.6 0.1 fusion.17
  333.8 19.7 %psum.30 = f32[128]{0:T(128)S(1)} all-reduce(f32[128]{0:T(128)S(1)} %get-tuple-element.17), channel_id=1, replica_groups=mesh['rep'=64,'tp'=8] {'tp'}, use_global_device_ids=true, to_apply=%region_8.10 | all-reduce | flops 128 | bytes 1024 | tf_op jit(solution)/shard_map/psum | solution.py:17
  353.5 0.1 fusion.19
  353.6 0.6 convolution_convert_fusion
  354.2 1.2 copy.9
  355.3 0.0 reduce-scatter.9.cloned.1.call-update
  355.4 3.1 fusion.11
  358.5 20.6 %psum.31 = bf16[64,2,64]{2,1,0:T(2,128)(2,1)S(1)} all-reduce(bf16[64,2,64]{2,1,0:T(2,128)(2,1)S(1)} %fusion.11), channel_id=1, replica_groups=mesh['rep'=64,'tp'=8] {'tp'}, use_global_device_ids=true, to_apply=%region_10.12 | all-reduce | flops 8192 | bytes 32768 | tf_op jit(solution)/shard_map/psum | solution.py:13
  379.1 2.6 fusion.9
  381.7 0.1 reshape.160
  381.9 1.9 reduce-scatter.9.cloned.1.call-done
  383.7 1.0 copy.10
  384.8 0.7 pad_maximum_fusion
  (12 shorter events, 0.2 us)
Async XLA Ops:
  6.5 195.7 %copy-start = (bf16[384,3072]{1,0:T(8,128)(2,1)S(1)}, bf16[384,3072]{1,0:T(8,128)(2,1)}, u32[]{:S(2)}) copy-start(bf16[384,3072]{1,0:T(8,128)(2,1)} %param.10) | copy-start | bytes 7077892
  6.5 4.7 %copy-start.1 = (bf16[4,384,64]{1,2,0:T(8,128)(2,1)S(1)}, bf16[4,384,64]{1,2,0:T(8,128)(2,1)}, u32[]{:S(2)}) copy-start(bf16[4,384,64]{1,2,0:T(8,128)(2,1)} %param.11) | copy-start | bytes 589828
  18.0 19.5 %copy-start.2 = (bf16[4,64,384]{2,1,0:T(8,128)(2,1)S(1)}, bf16[4,64,384]{2,1,0:T(8,128)(2,1)}, u32[]{:S(2)}) copy-start(bf16[4,64,384]{2,1,0:T(8,128)(2,1)} %param.12) | copy-start | bytes 589828
  18.0 159.6 %all-to-all-start = ((bf16[64,1,384,64]{2,3,1,0:T(8,128)(2,1)}), bf16[64,1,384,64]{2,3,1,0:T(8,128)(2,1)}, u32[]{:S(2)}, u32[]{:S(2)}) async-start(bf16[64,1,384,64]{2,3,1,0:T(8,128)(2,1)} %fusion.1), calls=%async_computation | async-start | bytes 6291456 | tf_op jit(solution)/shard_map/all_to_all | solution.py:48
  44.2 144.0 %copy-start.3 = (bf16[128,384]{1,0:T(8,128)(2,1)S(1)}, bf16[128,384]{1,0:T(8,128)(2,1)}, u32[]{:S(2)}) copy-start(bf16[128,384]{1,0:T(8,128)(2,1)} %param.8) | copy-start | bytes 294916
  44.2 158.0 %copy-start.4 = (f32[384]{0:T(512)S(1)}, f32[384]{0:T(512)}, u32[]{:S(2)}) copy-start(f32[384]{0:T(512)} %param.9) | copy-start | bytes 4612
  177.6 148.7 %all-to-all-start.1 = ((bf16[64,1,64,384]{3,2,1,0:T(8,128)(2,1)}), bf16[64,1,64,384]{3,2,1,0:T(8,128)(2,1)}, u32[]{:S(2)}, u32[]{:S(2)}) async-start(bf16[64,1,64,384]{3,2,1,0:T(8,128)(2,1)} %fusion), calls=%async_computation.1 | async-start | bytes 6291456 | tf_op jit(solution)/shard_map/all_to_all | solution.py:49
  188.1 54.2 %reduce-scatter.7.cloned.1.call-start = ((), (), s32[]{:S(2)}) async-start(), calls=%async_computation.4 | async-start | bytes 884736
  204.0 179.7 %reduce-scatter.9.cloned.1.call-start = ((), (), s32[]{:S(2)}) async-start(), calls=%async_computation.5 | async-start | bytes 884736
Sparse Core Ops, SparseCore 0:
  204.1 38.0 reduce-scatter.6
  355.5 28.2 reduce-scatter.8
where the time goes:
time: 394 us; the launch traced here: 392 us
  waiting for transfers between devices  224 us (57%)
  blocking collectives  79.2 us (20%)
  starting transfers between devices  30 us (8%)
  local copies, waits for them, and re-layouts  19.1 us (5%)
  other arithmetic  14 us (4%)
  between operations  13.6 us (3%)
  matrix products  12.7 us (3%)
    all_to_all x1, waiting for transfers between devices, shards(): lax.all_to_all(picked_down, 'rep', split_axis=0, concat_axis=0, tiled=True)  133 us
    all_to_all x1, waiting for transfers between devices, shards(): lax.all_to_all(picked_up, 'rep', split_axis=0, concat_axis=0, tiled=True)  50.2 us
    psum x2, blocking collectives, rank_total(): lax.psum(partial_value.astype(jnp.bfloat16), 'tp').astype(jnp.float32)  45.7 us
    unnamed x4, waiting for transfers between devices  40 us
    psum x2, blocking collectives, normed(): squares = lax.psum(jnp.sum(current * current, axis=1), 'tp')  33.5 us
    all_to_all x1, starting transfers between devices, shards(): lax.all_to_all(picked_down, 'rep', split_axis=0, concat_axis=0, tiled=True)  19.5 us
    all_to_all x1, starting transfers between devices, shards(): lax.all_to_all(picked_up, 'rep', split_axis=0, concat_axis=0, tiled=True)  10.5 us
  transfers between devices with their start and end apart: 4, of which 4 were waited for; matrix products, arithmetic and copies ran while one was open for 6% of the time, Pallas kernels for 0%

commit v1 on v0

v1 whole, which is shorter than its diff:
```python
import jax
import jax.numpy as jnp
from jax import lax
from jax.sharding import PartitionSpec as P

DRAFT = 2

EPSILON = 1e-06


def shards(first_hidden_rows, norm_scale, projection_weight, down_weights, up_weights, requests):
    groups = lax.axis_size("rep")
    tp = lax.axis_size("tp")
    rows, width = first_hidden_rows.shape
    full_width = width * tp
    kept, _, rank = down_weights.shape
    req_count = requests.shape[1]
    block_rows = rows // req_count
    bf16, f32 = jnp.bfloat16, jnp.float32

    me = lax.axis_index("rep")
    owners = requests // kept
    my_owner = jnp.take(owners, me, axis=0)
    to_holder = (my_owner[None, :] == jnp.arange(groups, dtype=jnp.int32)[:, None]).astype(bf16)
    held = jnp.sum(jnp.where(owners == me, requests % kept, 0), axis=1)
    row_adapter = jnp.repeat(held, block_rows)

    def move(blocks):
        return lax.all_to_all(blocks, "rep", split_axis=0, concat_axis=0, tiled=True)

    blocks = first_hidden_rows.reshape(req_count, block_rows * width)
    sent = jnp.dot(to_holder, blocks, preferred_element_type=f32).astype(bf16)
    states = move(sent).reshape(rows, width)
    down = jnp.transpose(down_weights, (1, 0, 2)).reshape(width, kept * rank)
    up = up_weights.reshape(kept * rank, width)
    mask = row_adapter[:, None] == jnp.arange(kept, dtype=jnp.int32)[None, :]
    outputs = []
    for step in range(DRAFT):
        wide = states.astype(f32)
        squares = jnp.sum(wide * wide, axis=1)
        scaled = (wide * norm_scale[None, :]).astype(bf16)
        partial = jnp.dot(scaled, projection_weight, preferred_element_type=f32).astype(bf16)
        ranks = jnp.dot(scaled, down, preferred_element_type=f32).reshape(rows, kept, rank)
        ranks = jnp.sum(jnp.where(mask[:, :, None], ranks, 0.0), axis=1).astype(bf16)
        high = squares.astype(bf16)
        low = (squares - high.astype(f32)).astype(bf16)
        extra = jnp.concatenate(
            [ranks, high[:, None], low[:, None], jnp.zeros((rows, 128 - rank - 2), bf16)], axis=1
        )
        sends = jnp.concatenate(
            [
                jnp.transpose(partial.reshape(rows, tp, width), (1, 0, 2)),
                jnp.broadcast_to(extra[None], (tp, rows, 128)),
            ],
            axis=2,
        )
        got = lax.all_to_all(sends, "tp", split_axis=0, concat_axis=0, tiled=True)
        total = jnp.sum(got.astype(f32), axis=0)
        mean = (total[:, width + rank] + total[:, width + rank + 1]) / full_width
        factor = lax.rsqrt(mean + EPSILON)[:, None]
        base = total[:, :width] * factor
        rank_rows = (total[:, width : width + rank] * factor).astype(bf16)
        spread = jnp.where(mask[:, :, None], rank_rows[:, None, :], 0).reshape(rows, kept * rank)
        delta = jnp.dot(spread, up, preferred_element_type=f32).astype(bf16)
        states = (wide + base + delta.astype(f32)).astype(bf16)
        home = move(states.reshape(req_count, block_rows * width))
        back = jnp.dot(to_holder.T, home, preferred_element_type=f32).astype(bf16)
        outputs.append(back.reshape(rows, width))
    return jnp.stack(outputs)


def solution(mesh):
    return jax.shard_map(
        shards,
        mesh=mesh,
        in_specs=(
            P("rep", "tp"),
            P("tp"),
            P("tp", None),
            P("rep", "tp", None),
            P("rep", None, "tp"),
            P(),
        ),
        out_specs=P(None, "rep", "tp"),
        check_vma=False,
    )
```

time: 394 us -> 127 us (0.32)
  waiting for transfers between devices: 224 us -> 47.3 us
  blocking collectives: 79.2 us -> 22.1 us
  between operations: 13.6 us -> 0.37 us
  local copies, waits for them, and re-layouts: 19.1 us -> 8.49 us
  matrix products: 12.7 us -> 3.75 us
  other arithmetic: 14 us -> 9.46 us
  starting transfers between devices: 30 us -> 34.4 us
    all_to_all x2 -> x4, waiting for transfers between devices: 184 us -> 47.3 us  [the longest x3 37.2 us: move(): lax.all_to_all(blocks, 'rep', split_axis=0, concat_axis=0, tiled=True)]
    psum x4 -> x0, blocking collectives: 79.2 us -> none  [the longest x2 45.7 us: rank_total(): lax.psum(partial_value.astype(jnp.bfloat16), 'tp').astype(jnp.float32)]
    unnamed x4 -> x0, waiting for transfers between devices: 40 us -> none
    all_to_all x0 -> x1, blocking collectives: none -> 22.1 us  [shards(): got = lax.all_to_all(sends, 'tp', split_axis=0, concat_axis=0, tiled=True)]
    gather x4 -> x0, local copies, waits for them, and re-layouts: 14.4 us -> none  [the longest x1 4.57 us: shards(): jnp.take(got_a.reshape(groups * slot_count, feature_portion, rank_span),...]
    dot_general x6 -> x9, matrix products: 12.7 us -> 3.75 us  [the longest x2 1.54 us: shards(): delta = jnp.dot(spread, up, preferred_element_type=f32).astype(bf16)]
    mul x2 -> x0, other arithmetic: 8.14 us -> none  [the longest x1 4.11 us: shards(): jnp.take(down_weights, local_index, axis=0)]
    all_to_all x2 -> x4, starting transfers between devices: 30 us -> 34.4 us  [the longest x3 29.9 us: move(): lax.all_to_all(blocks, 'rep', split_axis=0, concat_axis=0, tiled=True)]
  transfers between devices with their start and end apart: 4 -> 4, of which waited for: 4 -> 4; matrix products, arithmetic and copies ran while one was open for 6% -> 8% of each run, Pallas kernels for 0% -> 0%
where the time goes in v1:
time: 127 us; the launch traced here: 126 us
  waiting for transfers between devices  47.3 us (37%)
  starting transfers between devices  34.4 us (27%)
  blocking collectives  22.1 us (17%)
  other arithmetic  9.46 us (7%)
  local copies, waits for them, and re-layouts  8.49 us (7%)
  matrix products  3.75 us (3%)
    all_to_all x3, waiting for transfers between devices, move(): lax.all_to_all(blocks, 'rep', split_axis=0, concat_axis=0, tiled=True)  37.2 us
    all_to_all x3, starting transfers between devices, move(): lax.all_to_all(blocks, 'rep', split_axis=0, concat_axis=0, tiled=True)  29.9 us
    all_to_all x1, blocking collectives, shards(): got = lax.all_to_all(sends, 'tp', split_axis=0, concat_axis=0, tiled=True)  22.1 us
    all_to_all x1, waiting for transfers between devices, shards(): got = lax.all_to_all(sends, 'tp', split_axis=0, concat_axis=0, tiled=True)  10.2 us
    unnamed x18, local copies, waits for them, and re-layouts  4.66 us
    all_to_all x1, starting transfers between devices, shards(): got = lax.all_to_all(sends, 'tp', split_axis=0, concat_axis=0, tiled=True)  4.5 us
    all_to_all x3, other arithmetic, move(): lax.all_to_all(blocks, 'rep', split_axis=0, concat_axis=0, tiled=True)  4.37 us
  transfers between devices with their start and end apart: 4, of which 4 were waited for; matrix products, arithmetic and copies ran while one was open for 8% of the time, Pallas kernels for 0%

profile of v1, /device:TPU:1, one launch (start us, length us, event | category | flops | bytes accessed | tf_op | source)
XLA Modules:
  0.0 125.9 jit_solution(7028336983110507616)
XLA Ops:
  0.0 0.0 copy-start
  0.0 0.0 copy-start.3
  0.0 0.0 copy-start.4
  0.0 1.1 fusion.39
  1.1 0.9 reshape.117
  2.0 0.2 fusion.8
  2.2 0.5 broadcast.101
  2.7 0.6 reduce.8
  3.3 0.7 reshape.161
  4.0 19.1 %all-to-all-start = ((bf16[64,2,384]{2,1,0:T(2,128)(2,1)}), bf16[64,2,384]{2,1,0:T(2,128)(2,1)S(1)}, u32[]{:S(2)}, u32[]{:S(2)}) async-start(bf16[64,2,384]{2,1,0:T(2,128)(2,1)} %reshape.161), calls=%async_computation | async-start | bytes 196608 | tf_op jit(solution)/shard_map/all_to_all | solution.py:29
  23.1 0.7 mul.71
  23.8 0.1 broadcast_in_dim.92
  23.9 0.1 eq.45
  24.0 0.1 pad.15.clone
  24.1 13.5 %all-to-all-done = bf16[64,2,384]{2,1,0:T(2,128)(2,1)S(1)} async-done(((bf16[64,2,384]{2,1,0:T(2,128)(2,1)}), bf16[64,2,384]{2,1,0:T(2,128)(2,1)S(1)}, u32[]{:S(2)}, u32[]{:S(2)}) %all-to-all-start) | async-done | bytes 98336 | tf_op jit(solution)/shard_map/all_to_all | solution.py:29
  37.6 0.1 reshape.162
  37.7 0.5 convert_reduce_fusion.2
  38.3 0.1 multiply_reduce_fusion
  38.4 0.6 fusion.17
  39.0 0.0 copy-done.4
  39.0 0.2 fusion.9
  39.2 0.1 maximum_maximum_fusion
  39.3 0.1 copy.61
  39.5 0.0 copy-done
  39.5 0.0 copy-done.3
  39.5 0.6 convolution_convert_fusion.1
  40.1 0.1 copy.85
  40.2 0.1 pad_maximum_fusion
  40.3 0.0 copy-start.2
  40.3 22.1 %all_to_all.45 = bf16[8,128,512]{2,1,0:T(8,128)(2,1)S(1)} all-to-all(bf16[8,128,512]{2,1,0:T(8,128)(2,1)S(1)} %pad_maximum_fusion), channel_id=1, replica_groups=mesh['rep'=64,'tp'=8] {'tp'}, dimensions={0} | all-to-all | bytes 2097152 | tf_op jit(solution)/shard_map/all_to_all | solution.py:57
  62.4 0.1 convert_reduce_fusion.1
  62.6 0.2 fusion.33
  62.8 0.1 copy.70
  62.9 0.0 copy-done.2
  62.9 0.3 fusion.12
  63.2 0.2 fusion.10
  63.5 0.6 convolution_convert_fusion
  64.0 0.1 maximum_maximum_fusion.1
  64.1 0.1 copy.65
  64.2 0.1 copy.84
  64.4 1.1 pad_maximum_fusion.1
  65.5 4.5 %all-to-all-start.3 = ((bf16[8,128,512]{2,1,0:T(8,128)(2,1)}), bf16[8,128,512]{2,1,0:T(8,128)(2,1)S(1)}, u32[]{:S(2)}, u32[]{:S(2)}) async-start(bf16[8,128,512]{2,1,0:T(8,128)(2,1)} %pad_maximum_fusion.1), calls=%async_computation.3 | async-start | bytes 2097152 | tf_op jit(solution)/shard_map/all_to_all | solution.py:57
  70.0 0.7 all_to_all.38
  70.7 2.7 %reduce.10 = bf16[64,768]{1,0:T(8,128)(2,1)} reduce(bf16[64,1,768]{2,1,0:T(2,128)(2,1)} %all_to_all.38, bf16[]{:T(256)} %broadcast.101), dimensions={1}, to_apply=%all_to_all.38.reduce_sub_computation | reduce | bytes 196610 | tf_op jit(solution)/shard_map/all_to_all | solution.py:29
  73.4 1.6 %reshape.165 = bf16[64,2,384]{2,1,0:T(2,128)(2,1)} reshape(bf16[64,768]{1,0:T(8,128)(2,1)} %reduce.10) | data formatting | bytes 196608
  74.9 10.2 %all-to-all-done.3 = bf16[8,128,512]{2,1,0:T(8,128)(2,1)S(1)} async-done(((bf16[8,128,512]{2,1,0:T(8,128)(2,1)}), bf16[8,128,512]{2,1,0:T(8,128)(2,1)S(1)}, u32[]{:S(2)}, u32[]{:S(2)}) %all-to-all-start.3) | async-done | bytes 1048608 | tf_op jit(solution)/shard_map/all_to_all | solution.py:57
  85.1 5.4 %all-to-all-start.2 = ((bf16[64,2,384]{2,1,0:T(2,128)(2,1)}), bf16[64,2,384]{2,1,0:T(2,128)(2,1)}, u32[]{:S(2)}, u32[]{:S(2)}) async-start(bf16[64,2,384]{2,1,0:T(2,128)(2,1)} %reshape.165), calls=%async_computation.2 | async-start | bytes 196608 | tf_op jit(solution)/shard_map/all_to_all | solution.py:29
  90.5 0.1 convert_reduce_fusion
  90.7 0.0 copy-start.1
  90.7 0.2 fusion.29
  90.9 0.5 copy-done.1
  91.4 0.1 copy.71
  91.5 1.2 fusion.7
  92.8 1.1 reduce.9
  93.9 0.7 reshape.163
  94.6 10.4 %all-to-all-done.2 = bf16[64,2,384]{2,1,0:T(2,128)(2,1)} async-done(((bf16[64,2,384]{2,1,0:T(2,128)(2,1)}), bf16[64,2,384]{2,1,0:T(2,128)(2,1)}, u32[]{:S(2)}, u32[]{:S(2)}) %all-to-all-start.2) | async-done | bytes 98336 | tf_op jit(solution)/shard_map/all_to_all | solution.py:29
  105.0 5.4 %all-to-all-start.4 = ((bf16[64,2,384]{2,1,0:T(2,128)(2,1)}), bf16[64,2,384]{2,1,0:T(2,128)(2,1)S(1)}, u32[]{:S(2)}, u32[]{:S(2)}) async-start(bf16[64,2,384]{2,1,0:T(2,128)(2,1)} %reshape.163), calls=%async_computation.4 | async-start | bytes 196608 | tf_op jit(solution)/shard_map/all_to_all | solution.py:29
  110.4 1.0 reshape.166
  111.3 0.2 convolution_convert_fusion.3
  111.6 13.3 %all-to-all-done.4 = bf16[64,2,384]{2,1,0:T(2,128)(2,1)S(1)} async-done(((bf16[64,2,384]{2,1,0:T(2,128)(2,1)}), bf16[64,2,384]{2,1,0:T(2,128)(2,1)S(1)}, u32[]{:S(2)}, u32[]{:S(2)}) %all-to-all-start.4) | async-done | bytes 98336 | tf_op jit(solution)/shard_map/all_to_all | solution.py:29
  124.9 0.1 reshape.164
  124.9 0.2 convolution_convert_fusion.2
  125.2 0.7 pad_maximum_fusion.2
  (19 shorter events, 0.4 us)
Async XLA Ops:
  0.0 39.5 %copy-start = (bf16[384,3072]{1,0:T(8,128)(2,1)S(1)}, bf16[384,3072]{1,0:T(8,128)(2,1)}, u32[]{:S(2)}) copy-start(bf16[384,3072]{1,0:T(8,128)(2,1)} %param.8) | copy-start | bytes 7077892
  0.0 39.5 %copy-start.3 = (f32[384]{0:T(512)S(1)}, f32[384]{0:T(512)}, u32[]{:S(2)}) copy-start(f32[384]{0:T(512)} %param.7) | copy-start | bytes 4612
  0.0 39.0 %copy-start.4 = (bf16[4,384,64]{1,2,0:T(8,128)(2,1)S(1)}, bf16[4,384,64]{1,2,0:T(8,128)(2,1)}, u32[]{:S(2)}) copy-start(bf16[4,384,64]{1,2,0:T(8,128)(2,1)} %param.9) | copy-start | bytes 589828
  4.0 33.6 %all-to-all-start = ((bf16[64,2,384]{2,1,0:T(2,128)(2,1)}), bf16[64,2,384]{2,1,0:T(2,128)(2,1)S(1)}, u32[]{:S(2)}, u32[]{:S(2)}) async-start(bf16[64,2,384]{2,1,0:T(2,128)(2,1)} %reshape.161), calls=%async_computation | async-start | bytes 196608 | tf_op jit(solution)/shard_map/all_to_all | solution.py:29
  40.3 22.6 %copy-start.2 = (bf16[4,64,384]{2,1,0:T(8,128)(2,1)S(1)}, bf16[4,64,384]{2,1,0:T(8,128)(2,1)}, u32[]{:S(2)}) copy-start(bf16[4,64,384]{2,1,0:T(8,128)(2,1)} %param.10) | copy-start | bytes 589828
  65.5 19.6 %all-to-all-start.3 = ((bf16[8,128,512]{2,1,0:T(8,128)(2,1)}), bf16[8,128,512]{2,1,0:T(8,128)(2,1)S(1)}, u32[]{:S(2)}, u32[]{:S(2)}) async-start(bf16[8,128,512]{2,1,0:T(8,128)(2,1)} %pad_maximum_fusion.1), calls=%async_computation.3 | async-start | bytes 2097152 | tf_op jit(solution)/shard_map/all_to_all | solution.py:57
  85.1 19.9 %all-to-all-start.2 = ((bf16[64,2,384]{2,1,0:T(2,128)(2,1)}), bf16[64,2,384]{2,1,0:T(2,128)(2,1)}, u32[]{:S(2)}, u32[]{:S(2)}) async-start(bf16[64,2,384]{2,1,0:T(2,128)(2,1)} %reshape.165), calls=%async_computation.2 | async-start | bytes 196608 | tf_op jit(solution)/shard_map/all_to_all | solution.py:29
  90.7 0.7 copy-start.1
  105.0 19.9 %all-to-all-start.4 = ((bf16[64,2,384]{2,1,0:T(2,128)(2,1)}), bf16[64,2,384]{2,1,0:T(2,128)(2,1)S(1)}, u32[]{:S(2)}, u32[]{:S(2)}) async-start(bf16[64,2,384]{2,1,0:T(2,128)(2,1)} %reshape.163), calls=%async_computation.4 | async-start | bytes 196608 | tf_op jit(solution)/shard_map/all_to_all | solution.py:29

commit v2 on v1

v2 whole, which is shorter than its diff:
```python
import jax
import jax.numpy as jnp
from jax import lax
from jax.sharding import Mesh, PartitionSpec as P

DRAFT = 2

EPSILON = 1e-06


def pieces(values, count):
    found = []
    for _ in range(count):
        piece = lax.reduce_precision(values, 8, 7)
        found.append(piece.astype(jnp.bfloat16))
        values = values - piece
    return found


def shards(first_hidden_rows, norm_scale, projection_weight, down_weights, up_weights, requests):
    groups = lax.axis_size("rep")
    chips = lax.axis_size("y")
    cores = lax.axis_size("c")
    rows, width = first_hidden_rows.shape
    chip_width = width * cores
    full_width = chip_width * chips
    kept, _, rank = down_weights.shape
    req_count = requests.shape[1]
    block_rows = rows // req_count
    bf16, f32 = jnp.bfloat16, jnp.float32

    me = lax.axis_index("rep")
    core = lax.axis_index("c")
    owners = requests // kept
    my_owner = lax.dynamic_index_in_dim(owners, me, 0, keepdims=False)
    source_row = jnp.arange(rows, dtype=jnp.int32)
    target_row = jnp.repeat(my_owner * block_rows, block_rows) + source_row % block_rows
    to_holder = (target_row[None, :] == source_row[:, None]).astype(bf16)
    held = jnp.sum(jnp.where(owners == me, requests % kept, 0), axis=1)
    mask = held[:, None] == jnp.arange(kept, dtype=jnp.int32)[None, :]

    sent = jnp.dot(to_holder, first_hidden_rows, preferred_element_type=f32).astype(bf16)
    states = lax.all_to_all(
        sent.reshape(rows, 1, width), ("rep", "c"), split_axis=0, concat_axis=0, tiled=True
    ).reshape(groups, chip_width)

    sibling = [(i, cores - 1 - i) for i in range(cores)]
    down = jnp.transpose(down_weights, (0, 2, 1)).reshape(kept * rank, width)
    up = up_weights.reshape(kept * rank, width)
    gains = jnp.stack(pieces(norm_scale, 3) + [jnp.zeros((width,), bf16)] * 13)
    other_weight = lax.ppermute(projection_weight, "c", sibling)
    others = lax.ppermute(jnp.concatenate([down, up, gains]), "c", sibling)
    other_down, other_up = others[: kept * rank], others[kept * rank : 2 * kept * rank]
    other_scale = jnp.sum(others[2 * kept * rank :].astype(f32), axis=0)
    first = core == 0

    def halves(values):
        low, high = values[:, :width], values[:, width:]
        return jnp.where(first, low, high), jnp.where(first, high, low)

    def whole(mine, other):
        return jnp.concatenate(
            [jnp.where(first, mine, other), jnp.where(first, other, mine)], axis=1
        )

    scale = whole(norm_scale[None], other_scale[None])
    count = groups
    outputs = []
    for step in range(DRAFT):
        wide = states.astype(f32)
        squares = jnp.sum(wide * wide, axis=1)
        mine, other = halves((wide * scale).astype(bf16))
        partial = (
            jnp.dot(mine, projection_weight, preferred_element_type=f32)
            + jnp.dot(other, other_weight, preferred_element_type=f32)
        ).astype(bf16)
        contract = (((1,), (1,)), ((), ()))
        ranks = lax.dot_general(mine, down, contract, preferred_element_type=f32) + lax.dot_general(
            other, other_down, contract, preferred_element_type=f32
        )
        ranks = jnp.sum(
            jnp.where(mask[:, :, None], ranks.reshape(count, kept, rank), 0.0), axis=1
        ).astype(bf16)
        extra = jnp.concatenate(
            [ranks]
            + [piece[:, None] for piece in pieces(squares, 2)]
            + [jnp.zeros((count, 128 - rank - 2), bf16)],
            axis=1,
        )
        sends = jnp.concatenate(
            [
                jnp.transpose(partial.reshape(count, chips, chip_width), (1, 0, 2)),
                jnp.broadcast_to(extra[None], (chips, count, 128)),
            ],
            axis=2,
        )
        got = lax.all_to_all(sends, "y", split_axis=0, concat_axis=0, tiled=True)
        total = jnp.sum(got.astype(f32), axis=0)
        mean = (total[:, chip_width + rank] + total[:, chip_width + rank + 1]) / full_width
        factor = lax.rsqrt(mean + EPSILON)[:, None]
        rank_rows = (total[:, chip_width : chip_width + rank] * factor).astype(bf16)
        spread = jnp.where(mask[:, :, None], rank_rows[:, None, :], 0).reshape(count, kept * rank)
        delta = whole(
            jnp.dot(spread, up, preferred_element_type=f32),
            jnp.dot(spread, other_up, preferred_element_type=f32),
        ).astype(bf16)
        states = (wide + total[:, :chip_width] * factor + delta.astype(f32)).astype(bf16)
        outputs.append(states.reshape(count, cores, 1, width))
    back = jnp.concatenate(outputs, axis=2).reshape(count * cores, DRAFT, width)
    home = lax.all_to_all(back, ("rep", "c"), split_axis=0, concat_axis=0, tiled=True)
    from_holder = (target_row[:, None] == source_row[None, :]).astype(bf16)
    result = jnp.dot(
        from_holder, home.reshape(rows, DRAFT * width), preferred_element_type=f32
    ).astype(bf16)
    return jnp.transpose(result.reshape(rows, DRAFT, width), (1, 0, 2))


def solution(mesh):
    chip_mesh = Mesh(mesh.devices.reshape(mesh.shape["rep"], -1, 2), ("rep", "y", "c"))
    tp = ("y", "c")
    return jax.shard_map(
        shards,
        mesh=chip_mesh,
        in_specs=(
            P("rep", tp),
            P(tp),
            P(tp, None),
            P("rep", tp, None),
            P("rep", None, tp),
            P(),
        ),
        out_specs=P(None, "rep", tp),
        check_vma=False,
    )
```

time: 127 us -> 115 us (0.906)
  waiting for transfers between devices: 47.3 us -> 12.9 us
  blocking collectives: 22.1 us -> 42.1 us
  starting transfers between devices: 34.4 us -> 28.7 us
  matrix products: 3.75 us -> 8.86 us
  local copies, waits for them, and re-layouts: 8.49 us -> 11.1 us
    all_to_all x4 -> x2, waiting for transfers between devices: 47.3 us -> 12.9 us  [the longest x1 6.88 us: shards(): got = lax.all_to_all(sends, 'y', split_axis=0, concat_axis=0, tiled=True)]
    all_to_all x1 -> x2, blocking collectives: 22.1 us -> 42.1 us  [the longest x1 30 us: shards(): lax.all_to_all(back, ('rep', 'c'), split_axis=0, concat_axis=0, tiled=True)]
    all_to_all x4 -> x2, starting transfers between devices: 34.4 us -> 24 us  [the longest x1 20.4 us: shards(): lax.all_to_all(sent.reshape(rows, 1, width), ('rep', 'c'), split_axis=0,...]
    dot_general x9 -> x14, matrix products: 3.75 us -> 8.86 us  [the longest x2 4.41 us: shards(): jnp.dot(other, other_weight, preferred_element_type=f32)]
    ppermute x0 -> x2, starting transfers between devices: none -> 4.71 us  [the longest x1 2.8 us: shards(): other_weight = lax.ppermute(projection_weight, 'c', sibling)]
    all_to_all x3 -> x0, other arithmetic: 4.37 us -> none  [move(): lax.all_to_all(blocks, 'rep', split_axis=0, concat_axis=0, tiled=True)]
    concatenate x3 -> x6, local copies, waits for them, and re-layouts: 0.3 us -> 4.55 us  [the longest x3 4.39 us: shards(): others = lax.ppermute(jnp.concatenate([down, up, gains]), 'c', sibling)]
    unnamed x18 -> x28, local copies, waits for them, and re-layouts: 4.66 us -> 2.18 us
  transfers between devices with their start and end apart: 4 -> 4, of which waited for: 4 -> 2; matrix products, arithmetic and copies ran while one was open for 8% -> 10% of each run, Pallas kernels for 0% -> 0%
where the time goes in v2:
time: 115 us; the launch traced here: 114 us
  blocking collectives  42.1 us (37%)
  starting transfers between devices  28.7 us (25%)
  waiting for transfers between devices  12.9 us (11%)
  local copies, waits for them, and re-layouts  11.1 us (10%)
  other arithmetic  9.24 us (8%)
  matrix products  8.86 us (8%)
    all_to_all x1, blocking collectives, shards(): lax.all_to_all(back, ('rep', 'c'), split_axis=0, concat_axis=0, tiled=True)  30 us
    all_to_all x1, starting transfers between devices, shards(): lax.all_to_all(sent.reshape(rows, 1, width), ('rep', 'c'), split_axis=0,...  20.4 us
    all_to_all x1, blocking collectives, shards(): got = lax.all_to_all(sends, 'y', split_axis=0, concat_axis=0, tiled=True)  12.2 us
    all_to_all x1, waiting for transfers between devices, shards(): got = lax.all_to_all(sends, 'y', split_axis=0, concat_axis=0, tiled=True)  6.88 us
    all_to_all x1, waiting for transfers between devices, shards(): lax.all_to_all(sent.reshape(rows, 1, width), ('rep', 'c'), split_axis=0,...  6.02 us
    dot_general x2, matrix products, shards(): jnp.dot(other, other_weight, preferred_element_type=f32)  4.41 us
    concatenate x3, local copies, waits for them, and re-layouts, shards(): others = lax.ppermute(jnp.concatenate([down, up, gains]), 'c', sibling)  4.39 us
    all_to_all x1, starting transfers between devices, shards(): got = lax.all_to_all(sends, 'y', split_axis=0, concat_axis=0, tiled=True)  3.6 us
  transfers between devices with their start and end apart: 4, of which 2 were waited for; matrix products, arithmetic and copies ran while one was open for 10% of the time, Pallas kernels for 0%

profile of v2, /device:TPU:1, one launch (start us, length us, event | category | flops | bytes accessed | tf_op | source)
XLA Modules:
  0.0 113.5 jit_solution(15627912063207352680)
XLA Ops:
  0.0 1.0 add_select_fusion.1
  1.2 0.1 reshape.154
  1.3 0.2 fusion.2
  1.5 0.4 copy-done.9
  1.9 0.5 broadcast.116
  2.4 0.7 reduce.10
  3.1 0.8 reshape.171
  3.9 20.4 %all-to-all-start = ((bf16[128,2,192]{2,1,0:T(2,128)(2,1)}), bf16[128,2,192]{2,1,0:T(2,128)(2,1)S(1)}, u32[]{:S(2)}, u32[]{:S(2)}) async-start(bf16[128,2,192]{2,1,0:T(2,128)(2,1)} %reshape.171), calls=%async_computation | async-start | bytes 262144 | tf_op jit(solution)/shard_map/all_to_all | solution.py:43
  24.3 2.8 %collective-permute-start.1 = (bf16[384,3072]{1,0:T(8,128)(2,1)}, bf16[384,3072]{1,0:T(8,128)(2,1)}, u32[]{:S(2)}, u32[]{:S(2)}) collective-permute-start(bf16[384,3072]{1,0:T(8,128)(2,1)} %param.8), channel_id=1, source_target_pairs={{0,1},{1,0},{2,3},{3,2},{4,5},{5,4},{6,7},{7,6},{8,9},{9,8},{10,11... | collective-permute-start | bytes 7077896 | tf_op jit(solution)/shard_map/ppermute | solution.py:51
  27.1 0.7 fusion.40
  27.9 4.4 %concatenate.42 = bf16[528,384]{1,0:T(8,128)(2,1)} concatenate(bf16[256,384]{1,0:T(8,128)(2,1)} %bitcast.52, bf16[256,384]{1,0:T(8,128)(2,1)} %bitcast.55, bf16[1,384]{1,0:T(2,128)(2,1)S(1)} %stack.9, bf16[1,384]{1,0:T(2,128)(2,1)S(1)} %stack.10, bf16[1,384]{1,0:T(2,128)(2,1)S(1)} %stack.11, bf16[1,384]{1,0:T(2,128)(2,1)S(1)} %stack_broadcast_in_dim.3, ...), dimensions={0} | concatenate | bytes 811008 | tf_op jit(solution)/shard_map/concatenate | solution.py:52
  32.2 1.9 %collective-permute-start = (bf16[528,384]{1,0:T(8,128)(2,1)}, bf16[528,384]{1,0:T(8,128)(2,1)S(1)}, u32[]{:S(2)}, u32[]{:S(2)}) collective-permute-start(bf16[528,384]{1,0:T(8,128)(2,1)} %concatenate.42), channel_id=1, source_target_pairs={{0,1},{1,0},{2,3},{3,2},{4,5},{5,4},{6,7},{7,6},{8,9},{9,8},{10,11... | collective-permute-start | bytes 1216520 | tf_op jit(solution)/shard_map/ppermute | solution.py:52
  34.2 0.1 iota_compare_fusion.4
  34.3 0.1 pad.17.clone
  34.3 6.0 %all-to-all-done = bf16[128,2,192]{2,1,0:T(2,128)(2,1)S(1)} async-done(((bf16[128,2,192]{2,1,0:T(2,128)(2,1)}), bf16[128,2,192]{2,1,0:T(2,128)(2,1)S(1)}, u32[]{:S(2)}, u32[]{:S(2)}) %all-to-all-start) | async-done | bytes 98336 | tf_op jit(solution)/shard_map/all_to_all | solution.py:43
  40.4 0.2 reshape.172
  40.5 1.6 %fusion.10 = (f32[128]{0:T(128)S(1)}, f32[128,384]{1,0:T(8,128)}) fusion(bf16[128,1,384]{2,1,0:T(2,128)(2,1)S(1)} %reshape.172), kind=kLoop, calls=%fused_computation.33 | loop fusion | flops 147328 | bytes 295424 | tf_op jit(solution)/shard_map/reduce_sum | solution.py:71
  42.1 1.0 reshape.164
  43.1 0.1 reduce_sum.87
  43.3 0.1 reduce_sum.88
  43.4 0.1 copy.25
  43.5 0.1 copy.26
  43.8 0.2 fusion.35
  44.0 0.2 convolution_add_fusion.3
  44.2 0.8 reshape.159
  44.9 1.1 select_reduce_fusion.1
  46.0 0.1 maximum_maximum_fusion
  46.1 0.5 fusion.36
  46.7 2.2 %fusion = bf16[64,3072]{1,0:T(8,128)(2,1)S(1)} fusion(f32[64,3072]{1,0:T(8,128)S(1)} %fusion.36, bf16[384,3072]{1,0:T(8,128)(2,1)} %collective-permute-done.1, pred[]{:T(512)S(6)} %eq.62, bf16[64,768]{1,0:T(8,128)(2,1)S(1)} %multiply_convert_fusion), kind=kOutput, calls=%fused_computation.2 | convolution fusion | flops 151412736 | bytes 3637249 | tf_op jit(solution)/shard_map/dot_general | solution.py:75
  49.0 12.2 %all_to_all.20 = bf16[4,64,896]{2,1,0:T(8,128)(2,1)S(1)} all-to-all(bf16[4,64,896]{2,1,0:T(8,128)(2,1)S(1)} %pad_maximum_fusion), channel_id=1, replica_groups=mesh['rep'=64,'y'=4,'c'=2] {'y'}, dimensions={0} | all-to-all | bytes 917504 | tf_op jit(solution)/shard_map/all_to_all | solution.py:97
  61.3 0.2 fusion.30
  61.5 0.5 copy-done.4
  61.9 0.1 fusion.26
  62.0 0.1 broadcast_select_fusion.1
  62.2 0.3 copy-done.8
  62.4 0.8 convolution_bitcast_fusion.1
  63.3 0.1 select_n.127
  63.4 1.0 select_convert_fusion.3
  64.4 1.0 fusion.3
  65.4 0.5 fusion.38
  65.9 0.2 fusion.37
  66.2 2.2 %fusion.1 = bf16[64,3072]{1,0:T(8,128)(2,1)S(1)} fusion(f32[64,3072]{1,0:T(8,128)S(1)} %fusion.38, bf16[384,3072]{1,0:T(8,128)(2,1)} %collective-permute-done.1, pred[]{:T(512)S(6)} %eq.62, bf16[64,768]{1,0:T(8,128)(2,1)S(1)} %get-tuple-element.7), kind=kOutput, calls=%fused_computation.3 | convolution fusion | flops 151412736 | bytes 3637249 | tf_op jit(solution)/shard_map/dot_general | solution.py:75
  68.4 0.2 convolution_add_fusion.2
  68.6 0.1 reshape.161
  68.8 0.2 select_reduce_fusion
  68.9 0.1 fusion.4
  69.1 0.1 copy.29
  69.2 0.1 copy.30
  69.3 0.1 maximum_maximum_fusion.1
  69.4 0.8 pad_maximum_fusion.1
  70.2 3.6 %all-to-all-start.2 = ((bf16[4,64,896]{2,1,0:T(8,128)(2,1)}), bf16[4,64,896]{2,1,0:T(8,128)(2,1)S(1)}, u32[]{:S(2)}, u32[]{:S(2)}) async-start(bf16[4,64,896]{2,1,0:T(8,128)(2,1)} %pad_maximum_fusion.1), calls=%async_computation.2 | async-start | bytes 917504 | tf_op jit(solution)/shard_map/all_to_all | solution.py:97
  73.9 6.9 %all-to-all-done.2 = bf16[4,64,896]{2,1,0:T(8,128)(2,1)S(1)} async-done(((bf16[4,64,896]{2,1,0:T(8,128)(2,1)}), bf16[4,64,896]{2,1,0:T(8,128)(2,1)S(1)}, u32[]{:S(2)}, u32[]{:S(2)}) %all-to-all-start.2) | async-done | bytes 458784 | tf_op jit(solution)/shard_map/all_to_all | solution.py:97
  80.8 0.2 fusion.25
  81.0 0.1 fusion.21
  81.1 0.2 broadcast_select_fusion
  81.2 0.2 convolution_bitcast_fusion
  81.5 0.1 select_n.134
  81.6 0.2 select_convert_fusion.1
  81.7 0.1 fusion.6
  81.9 0.5 pad_maximum_fusion.2
  82.4 30.0 %all_to_all.21 = bf16[128,2,384]{2,1,0:T(2,128)(2,1)S(1)} all-to-all(bf16[128,2,384]{2,1,0:T(2,128)(2,1)S(1)} %pad_maximum_fusion.2), channel_id=1, replica_groups=mesh['rep'=64,'y'=4,'c'=2] {'rep','c'}, dimensions={0} | all-to-all | bytes 393216 | tf_op jit(solution)/shard_map/all_to_all | solution.py:110
  112.3 0.2 copy.34
  112.6 0.2 convolution_convert_fusion
  112.8 0.7 copy.48
  (52 shorter events, 0.6 us)
Async XLA Ops:
  0.0 1.3 %copy-start = (bf16[128,384]{1,0:T(8,128)(2,1)S(1)}, bf16[128,384]{1,0:T(8,128)(2,1)}, u32[]{:S(2)}) copy-start(bf16[128,384]{1,0:T(8,128)(2,1)} %param.6) | copy-start | bytes 294916
  0.0 46.1 %copy-start.1 = (bf16[384,3072]{1,0:T(8,128)(2,1)S(1)}, bf16[384,3072]{1,0:T(8,128)(2,1)}, u32[]{:S(2)}) copy-start(bf16[384,3072]{1,0:T(8,128)(2,1)} %param.8) | copy-start | bytes 7077892
  0.0 43.7 %copy-start.7 = (f32[384]{0:T(512)S(1)}, f32[384]{0:T(512)}, u32[]{:S(2)}) copy-start(f32[384]{0:T(512)} %param.7) | copy-start | bytes 4612
  0.0 43.7 %copy-start.2 = (bf16[4,384,64]{1,2,0:T(8,128)(2,1)S(1)}, bf16[4,384,64]{1,2,0:T(8,128)(2,1)}, u32[]{:S(2)}) copy-start(bf16[4,384,64]{1,2,0:T(8,128)(2,1)} %param.9) | copy-start | bytes 589828
  1.3 0.6 copy-start.9
  3.9 36.5 %all-to-all-start = ((bf16[128,2,192]{2,1,0:T(2,128)(2,1)}), bf16[128,2,192]{2,1,0:T(2,128)(2,1)S(1)}, u32[]{:S(2)}, u32[]{:S(2)}) async-start(bf16[128,2,192]{2,1,0:T(2,128)(2,1)} %reshape.171), calls=%async_computation | async-start | bytes 262144 | tf_op jit(solution)/shard_map/all_to_all | solution.py:43
  24.3 22.4 %collective-permute-start.1 = (bf16[384,3072]{1,0:T(8,128)(2,1)}, bf16[384,3072]{1,0:T(8,128)(2,1)}, u32[]{:S(2)}, u32[]{:S(2)}) collective-permute-start(bf16[384,3072]{1,0:T(8,128)(2,1)} %param.8), channel_id=1, source_target_pairs={{0,1},{1,0},{2,3},{3,2},{4,5},{5,4},{6,7},{7,6},{8,9},{9,8},{10,11... | collective-permute-start | bytes 7077896 | tf_op jit(solution)/shard_map/ppermute | solution.py:51
  32.2 11.4 %collective-permute-start = (bf16[528,384]{1,0:T(8,128)(2,1)}, bf16[528,384]{1,0:T(8,128)(2,1)S(1)}, u32[]{:S(2)}, u32[]{:S(2)}) collective-permute-start(bf16[528,384]{1,0:T(8,128)(2,1)} %concatenate.42), channel_id=1, source_target_pairs={{0,1},{1,0},{2,3},{3,2},{4,5},{5,4},{6,7},{7,6},{8,9},{9,8},{10,11... | collective-permute-start | bytes 1216520 | tf_op jit(solution)/shard_map/ppermute | solution.py:52
  34.2 27.8 %copy-start.5 = (pred[64,4]{1,0:T(8,128)(4,1)}, pred[64,4]{1,0:T(8,128)(4,1)S(1)}, u32[]{:S(2)}) copy-start(pred[64,4]{1,0:T(8,128)(4,1)S(1)} %iota_compare_fusion.4) | copy-start | bytes 772
  34.3 12.3 %copy-start.11 = (bf16[128]{0:T(256)(128)(2,1)}, bf16[128]{0:T(256)(128)(2,1)S(1)}, u32[]{:S(2)}) copy-start(bf16[128]{0:T(256)(128)(2,1)S(1)} %pad.17.clone) | copy-start | bytes 772
  48.9 13.5 %copy-start.3 = (bf16[4,64,384]{2,1,0:T(8,128)(2,1)S(1)}, bf16[4,64,384]{2,1,0:T(8,128)(2,1)}, u32[]{:S(2)}) copy-start(bf16[4,64,384]{2,1,0:T(8,128)(2,1)} %param.10) | copy-start | bytes 589828
  61.3 0.7 copy-start.4
  61.9 0.5 copy-start.8
  66.2 2.6 %copy-start.6 = (pred[64,4]{1,0:T(8,128)(4,1)S(1)}, pred[64,4]{1,0:T(8,128)(4,1)}, u32[]{:S(2)}) copy-start(pred[64,4]{1,0:T(8,128)(4,1)} %copy-done.5) | copy-start | bytes 772
  66.2 3.1 %copy-start.12 = (bf16[128]{0:T(256)(128)(2,1)S(1)}, bf16[128]{0:T(256)(128)(2,1)}, u32[]{:S(2)}) copy-start(bf16[128]{0:T(256)(128)(2,1)} %copy-done.11) | copy-start | bytes 772
  70.2 42.3 %copy-start.10 = (s32[128]{0:T(128)S(1)}, s32[128]{0:T(128)}, u32[]{:S(2)}) copy-start(s32[128]{0:T(128)} %copy-done.9) | copy-start | bytes 1540
  70.2 10.5 %all-to-all-start.2 = ((bf16[4,64,896]{2,1,0:T(8,128)(2,1)}), bf16[4,64,896]{2,1,0:T(8,128)(2,1)S(1)}, u32[]{:S(2)}, u32[]{:S(2)}) async-start(bf16[4,64,896]{2,1,0:T(8,128)(2,1)} %pad_maximum_fusion.1), calls=%async_computation.2 | async-start | bytes 917504 | tf_op jit(solution)/shard_map/all_to_all | solution.py:97

commit v3 on v1

v3 whole, which is shorter than its diff:
```python
import functools

import jax
import jax.numpy as jnp
from jax import lax
from jax.experimental import pallas as pl
from jax.experimental.pallas import tpu as pltpu
from jax.sharding import Mesh, PartitionSpec as P

DRAFT = 2
LANES = 128
EPSILON = 1e-06

bf16, f32, i32 = jnp.bfloat16, jnp.float32, jnp.int32


def iota(shape, dim):
    return lax.broadcasted_iota(i32, shape, dim)


def mm(left, right):
    return jnp.dot(left, right, preferred_element_type=f32)


def mm_t(left, right):
    return lax.dot_general(left, right, (((1,), (1,)), ((), ())), preferred_element_type=f32)


def holder_rows(my_requests, kept, blocks):
    rows = 2 * blocks
    repeat = (iota((blocks, rows), 1) // 2 == iota((blocks, rows), 0)).astype(bf16)
    owner = jnp.broadcast_to((my_requests // kept).astype(f32).astype(bf16), (8, blocks))
    return mm(owner, repeat)[:1].astype(i32) * 2 + iota((1, rows), 1) % 2


def held_column(requests, me, kept):
    return jnp.sum(jnp.where(requests // kept == me, requests % kept, 0), axis=1, keepdims=True)


def permute_in(kept, requests_ref, x_ref, sent_ref):
    me = lax.axis_index("rep")
    blocks = requests_ref.shape[1]
    target = holder_rows(requests_ref[pl.ds(me, 1), :], kept, blocks)
    pick = (target == iota((2 * blocks, 2 * blocks), 0)).astype(bf16)
    sent_ref[...] = mm(pick, x_ref[...]).astype(bf16)


def permute_out(kept, requests_ref, home_ref, out_ref):
    me = lax.axis_index("rep")
    blocks = requests_ref.shape[1]
    width = out_ref.shape[2]
    target = holder_rows(requests_ref[pl.ds(me, 1), :], kept, blocks)
    pick = (target == iota((2 * blocks, 2 * blocks), 0)).astype(bf16)
    for step in range(DRAFT):
        out_ref[step] = lax.dot_general(
            pick,
            home_ref[:, step * width : (step + 1) * width],
            (((0,), (0,)), ((), ())),
            preferred_element_type=f32,
        ).astype(bf16)


def products(low, high, held, kept, weights, message_ref):
    weight, other_weight, down, other_down, scale, other_scale = weights
    first = lax.axis_index("c") == 0
    count, width = low.shape
    rank_cols = down.shape[0]
    rank = rank_cols // kept
    chips, _, packed = message_ref.shape
    chip_width = packed - LANES
    squares = jnp.sum(low * low, axis=1, keepdims=True) + jnp.sum(
        high * high, axis=1, keepdims=True
    )
    mine = (jnp.where(first, low, high) * scale[...]).astype(bf16)
    other = (jnp.where(first, high, low) * other_scale[...]).astype(bf16)
    for chip in range(chips):
        cols = pl.ds(chip * chip_width, chip_width)
        message_ref[chip, :, :chip_width] = (
            mm(mine, weight[:, cols]) + mm(other, other_weight[:, cols])
        ).astype(bf16)
    ranks = (mm_t(mine, down[...]) + mm_t(other, other_down[...])).astype(bf16)
    ranks = jnp.where(iota((count, rank_cols), 1) // rank == held, ranks, 0).astype(bf16)
    fold = iota((rank_cols, LANES), 0) % rank == iota((rank_cols, LANES), 1)
    extra = mm(ranks, fold.astype(bf16))
    top = squares.astype(bf16).astype(f32)
    lane = iota((count, LANES), 1)
    extra = jnp.where(lane == rank, top, extra)
    extra = jnp.where(lane == rank + 1, squares - top, extra).astype(bf16)
    for chip in range(chips):
        message_ref[chip, :, chip_width:] = extra


def update(low, high, held, kept, got_ref, up, other_up):
    first = lax.axis_index("c") == 0
    count, width = low.shape
    rank_cols = up.shape[0]
    rank = rank_cols // kept
    chips, _, packed = got_ref.shape
    chip_width = packed - LANES

    def total(start, stop):
        value = got_ref[0, :, start:stop].astype(f32)
        for chip in range(1, chips):
            value += got_ref[chip, :, start:stop].astype(f32)
        return value

    extra = total(chip_width, packed)
    lane = iota((count, LANES), 1)
    is_square = (lane == rank) | (lane == rank + 1)
    mean = jnp.sum(jnp.where(is_square, extra, 0.0), axis=1, keepdims=True) / (chip_width * chips)
    factor = lax.rsqrt(mean + EPSILON)
    ranks = jnp.where(lane < rank, extra * factor, 0.0).astype(bf16)
    unfold = iota((LANES, rank_cols), 1) % rank == iota((LANES, rank_cols), 0)
    spread = mm(ranks, unfold.astype(bf16))
    spread = jnp.where(iota((count, rank_cols), 1) // rank == held, spread, 0.0).astype(bf16)
    mine, other = mm(spread, up[...]), mm(spread, other_up[...])
    low_delta = jnp.where(first, mine, other).astype(bf16).astype(f32)
    high_delta = jnp.where(first, other, mine).astype(bf16).astype(f32)
    low = (low + total(0, width) * factor + low_delta).astype(bf16)
    high = (high + total(width, chip_width) * factor + high_delta).astype(bf16)
    return low, high


def row_pick(rows, core):
    return (iota((rows // 2, rows), 1) == 2 * iota((rows // 2, rows), 0) + core).astype(bf16)


def first_products(kept, requests_ref, x_ref, *refs):
    weights, message_ref = refs[:-1], refs[-1]
    held = held_column(requests_ref[...], lax.axis_index("rep"), kept)
    low, high = (mm(row_pick(x_ref.shape[0], core), x_ref[...]) for core in range(2))
    products(low, high, held, kept, weights, message_ref)


def next_products(kept, requests_ref, x_ref, got_ref, up, other_up, *refs):
    weights, (message_ref, state_ref) = refs[:-2], refs[-2:]
    held = held_column(requests_ref[...], lax.axis_index("rep"), kept)
    low, high = (mm(row_pick(x_ref.shape[0], core), x_ref[...]) for core in range(2))
    low, high = update(low, high, held, kept, got_ref, up, other_up)
    width = x_ref.shape[1]
    state_ref[:, :width] = low
    state_ref[:, width:] = high
    products(low.astype(f32), high.astype(f32), held, kept, weights, message_ref)


def last_update(kept, requests_ref, state_ref, got_ref, up, other_up, back_ref):
    held = held_column(requests_ref[...], lax.axis_index("rep"), kept)
    width = up.shape[1]
    rows = back_ref.shape[0]
    old = (state_ref[:, :width], state_ref[:, width:])
    new = update(old[0].astype(f32), old[1].astype(f32), held, kept, got_ref, up, other_up)
    for step, (low, high) in enumerate((old, new)):
        back_ref[:, step * width : (step + 1) * width] = sum(
            lax.dot_general(
                row_pick(rows, core), half, (((0,), (0,)), ((), ())), preferred_element_type=f32
            )
            for core, half in enumerate((low, high))
        ).astype(bf16)


def call(kernel, outs, *operands):
    spec = pl.BlockSpec(memory_space=pltpu.VMEM)
    return pl.pallas_call(
        kernel,
        out_shape=[jax.ShapeDtypeStruct(shape, bf16) for shape in outs],
        in_specs=[spec] * len(operands),
        out_specs=[spec] * len(outs),
        compiler_params=pltpu.CompilerParams(vmem_limit_bytes=24 * 2**20),
    )(*[pltpu.with_memory_space_constraint(operand, pltpu.VMEM) for operand in operands])


def shards(first_hidden_rows, norm_scale, projection_weight, down_weights, up_weights, requests):
    groups = lax.axis_size("rep")
    chips = lax.axis_size("y")
    cores = lax.axis_size("c")
    rows, width = first_hidden_rows.shape
    chip_width = width * cores
    kept, _, rank = down_weights.shape

    (sent,) = call(
        functools.partial(permute_in, kept), [(rows, width)], requests, first_hidden_rows
    )
    got = lax.all_to_all(
        sent.reshape(rows, 2, width // 2), ("rep", "c"), split_axis=0, concat_axis=0, tiled=True
    ).reshape(rows, width)

    sibling = [(i, cores - 1 - i) for i in range(cores)]
    down = jnp.transpose(down_weights, (0, 2, 1)).reshape(kept * rank, width)
    up = up_weights.reshape(kept * rank, width)
    scale = norm_scale[None]
    other_weight, other_down, other_up, other_scale = (
        lax.ppermute(value, "c", sibling) for value in (projection_weight, down, up, scale)
    )
    weights = (projection_weight, other_weight, down, other_down, scale, other_scale)

    def exchange(message):
        return lax.all_to_all(message, "y", split_axis=0, concat_axis=0, tiled=True)

    message_shape = (chips, groups, chip_width + LANES)
    (message,) = call(
        functools.partial(first_products, kept), [message_shape], requests, got, *weights
    )
    message, state = call(
        functools.partial(next_products, kept),
        [message_shape, (groups, chip_width)],
        requests,
        got,
        exchange(message),
        up,
        other_up,
        *weights,
    )
    (back,) = call(
        functools.partial(last_update, kept),
        [(rows, DRAFT * width)],
        requests,
        state,
        exchange(message),
        up,
        other_up,
    )
    home = lax.all_to_all(
        back.reshape(rows, DRAFT, width), ("rep", "c"), split_axis=0, concat_axis=0, tiled=True
    ).reshape(rows, DRAFT * width)
    (result,) = call(
        functools.partial(permute_out, kept), [(DRAFT, rows, width)], requests, home
    )
    return result


def solution(mesh):
    chip_mesh = Mesh(mesh.devices.reshape(mesh.shape["rep"], -1, 2), ("rep", "y", "c"))
    tp = ("y", "c")
    return jax.shard_map(
        shards,
        mesh=chip_mesh,
        in_specs=(
            P("rep", tp),
            P(tp),
            P(tp, None),
            P("rep", tp, None),
            P("rep", None, tp),
            P(),
        ),
        out_specs=P(None, "rep", tp),
        check_vma=False,
    )
```

time: 127 us -> 107 us (0.84)
  waiting for transfers between devices: 47.3 us -> 15.6 us
  blocking collectives: 22.1 us -> 36.6 us
  other arithmetic: 9.46 us -> 0 us
  Pallas kernels: 0 us -> 5.66 us
  local copies, waits for them, and re-layouts: 8.49 us -> 13.3 us
  matrix products: 3.75 us -> 0 us
    all_to_all x4 -> x2, waiting for transfers between devices: 47.3 us -> 14.5 us  [the longest x1 10.6 us: shards(): lax.all_to_all(sent.reshape(rows, 2, width // 2), ('rep', 'c'), split_axi...]
    all_to_all x4 -> x2, starting transfers between devices: 34.4 us -> 17.8 us  [the longest x1 13.6 us: shards(): lax.all_to_all(sent.reshape(rows, 2, width // 2), ('rep', 'c'), split_axi...]
    ppermute x0 -> x4, starting transfers between devices: none -> 16.1 us  [shards(): lax.ppermute(value, 'c', sibling)]
    all_to_all x1 -> x2, blocking collectives: 22.1 us -> 36.6 us  [the longest x1 26.9 us: shards(): lax.all_to_all(back.reshape(rows, DRAFT, width), ('rep', 'c'), split_axis...]
    unnamed x18 -> x29, local copies, waits for them, and re-layouts: 4.66 us -> 11.4 us
    pallas_call x0 -> x5, Pallas kernels: none -> 5.66 us  [call(): pl.pallas_call(kernel, out_shape=[jax.ShapeDtypeStruct(shape, bf16) for s...]
    all_to_all x3 -> x0, other arithmetic: 4.37 us -> none  [move(): lax.all_to_all(blocks, 'rep', split_axis=0, concat_axis=0, tiled=True)]
    dot_general x9 -> x0, matrix products: 3.75 us -> none  [the longest x2 1.54 us: shards(): delta = jnp.dot(spread, up, preferred_element_type=f32).astype(bf16)]
  transfers between devices with their start and end apart: 4 -> 6, of which waited for: 4 -> 3; matrix products, arithmetic and copies ran while one was open for 8% -> 2% of each run, Pallas kernels for 0% -> 0%
where the time goes in v3:
time: 107 us; the launch traced here: 105 us
  blocking collectives  36.6 us (34%)
  starting transfers between devices  33.9 us (32%)
  waiting for transfers between devices  15.6 us (15%)
  local copies, waits for them, and re-layouts  13.3 us (12%)
  Pallas kernels  5.66 us (5%)
    all_to_all x1, blocking collectives, shards(): lax.all_to_all(back.reshape(rows, DRAFT, width), ('rep', 'c'), split_axis...  26.9 us
    ppermute x4, starting transfers between devices, shards(): lax.ppermute(value, 'c', sibling)  16.1 us
    all_to_all x1, starting transfers between devices, shards(): lax.all_to_all(sent.reshape(rows, 2, width // 2), ('rep', 'c'), split_axi...  13.6 us
    unnamed x29, local copies, waits for them, and re-layouts  11.4 us
    all_to_all x1, waiting for transfers between devices, shards(): lax.all_to_all(sent.reshape(rows, 2, width // 2), ('rep', 'c'), split_axi...  10.6 us
    all_to_all x1, blocking collectives, exchange(): return lax.all_to_all(message, 'y', split_axis=0, concat_axis=0, tiled=True)  9.64 us
    pallas_call x5, Pallas kernels, call(): pl.pallas_call(kernel, out_shape=[jax.ShapeDtypeStruct(shape, bf16) for s...  5.66 us
    all_to_all x1, starting transfers between devices, exchange(): return lax.all_to_all(message, 'y', split_axis=0, concat_axis=0, tiled=True)  4.19 us
  transfers between devices with their start and end apart: 6, of which 3 were waited for; matrix products, arithmetic and copies ran while one was open for 2% of the time, Pallas kernels for 0%

profile of v3, /device:TPU:1, one launch (start us, length us, event | category | flops | bytes accessed | tf_op | source)
XLA Modules:
  0.0 105.2 jit_solution(3136015464712440488)
XLA Ops:
  0.0 8.8 %collective-permute-start = (bf16[384,3072]{1,0:T(8,128)(2,1)}, bf16[384,3072]{1,0:T(8,128)(2,1)S(1)}, u32[]{:S(2)}, u32[]{:S(2)}) collective-permute-start(bf16[384,3072]{1,0:T(8,128)(2,1)} %refs_0_.3), channel_id=1, source_target_pairs={{0,1},{1,0},{2,3},{3,2},{4,5},{5,4},{6,7},{7,6},{8,9},{9,8},{10,11... | collective-permute-start | bytes 7077896 | tf_op jit(solution)/shard_map/ppermute | solution.py:192
  8.8 0.0 copy-start.5
  8.8 0.7 copy-done.5
  9.5 0.0 copy-start.13
  9.5 0.9 copy-done.13
  10.4 0.3 shard_map.64
  10.7 0.1 copy.10
  10.9 0.8 copy.11
  11.7 13.6 %all-to-all-start = ((bf16[128,2,192]{2,1,0:T(2,128)(2,1)}), bf16[128,2,192]{2,1,0:T(2,128)(2,1)S(1)}, u32[]{:S(2)}, u32[]{:S(2)}) async-start(bf16[128,2,192]{2,1,0:T(2,128)(2,1)} %copy.11), calls=%async_computation | async-start | bytes 262144 | tf_op jit(solution)/shard_map/all_to_all | solution.py:183
  25.3 2.8 %collective-permute-start.1 = (bf16[256,384]{1,0:T(8,128)(2,1)}, bf16[256,384]{1,0:T(8,128)(2,1)S(1)}, u32[]{:S(2)}, u32[]{:S(2)}) collective-permute-start(bf16[256,384]{1,0:T(8,128)(2,1)} %bitcast.8), channel_id=1, source_target_pairs={{0,1},{1,0},{2,3},{3,2},{4,5},{5,4},{6,7},{7,6},{8,9},{9,8},{10,11... | collective-permute-start | bytes 589832 | tf_op jit(solution)/shard_map/ppermute | solution.py:192
  28.1 0.7 broadcast_in_dim.3.refs_4_
  28.8 1.9 %collective-permute-start.2 = (f32[1,384]{1,0:T(1,128)S(1)}, f32[1,384]{1,0:T(1,128)S(1)}, u32[]{:S(2)}, u32[]{:S(2)}) collective-permute-start(f32[1,384]{1,0:T(1,128)S(1)} %broadcast_in_dim.3.refs_4_), channel_id=1, source_target_pairs={{0,1},{1,0},{2,3},{3,2},{4,5},{5,4},{6,7},{7,6},{8,9},{9,8},{10,11... | collective-permute-start | bytes 4616 | tf_op jit(solution)/shard_map/ppermute | solution.py:192
  30.7 10.6 %all-to-all-done = bf16[128,2,192]{2,1,0:T(2,128)(2,1)S(1)} async-done(((bf16[128,2,192]{2,1,0:T(2,128)(2,1)}), bf16[128,2,192]{2,1,0:T(2,128)(2,1)S(1)}, u32[]{:S(2)}, u32[]{:S(2)}) %all-to-all-start) | async-done | bytes 98336 | tf_op jit(solution)/shard_map/all_to_all | solution.py:183
  41.4 0.1 copy.12
  41.5 0.0 copy-start.7
  41.5 0.1 copy.14.x_ref
  41.6 0.0 collective-permute-done.2.refs_5_
  41.6 0.0 collective-permute-done.1.refs_3_
  41.7 0.0 collective-permute-done.refs_1_
  41.7 0.0 copy-start.2
  41.7 1.4 %copy-done.2 = bf16[384,3072]{1,0:T(8,128)(2,1)} copy-done((bf16[384,3072]{1,0:T(8,128)(2,1)}, bf16[384,3072]{1,0:T(8,128)(2,1)S(1)}, u32[]{:S(2)}) %copy-start.2) | copy-done | bytes 2359320
  43.1 0.0 copy-start
  43.1 1.7 %copy-done = bf16[384,3072]{1,0:T(8,128)(2,1)S(1)} copy-done((bf16[384,3072]{1,0:T(8,128)(2,1)S(1)}, bf16[384,3072]{1,0:T(8,128)(2,1)}, u32[]{:S(2)}) %copy-start) | copy-done | bytes 2359320
  44.8 0.0 copy-start.3
  44.8 1.7 %copy-done.3 = bf16[384,3072]{1,0:T(8,128)(2,1)S(1)} copy-done((bf16[384,3072]{1,0:T(8,128)(2,1)S(1)}, bf16[384,3072]{1,0:T(8,128)(2,1)}, u32[]{:S(2)}) %copy-start.3) | copy-done | bytes 2359320
  46.4 0.0 copy-start.6
  46.4 0.8 copy-done.6
  47.2 0.0 copy-start.8
  47.2 0.9 copy-done.8
  48.1 0.0 copy-start.10
  48.1 0.0 copy-start.1
  48.1 0.0 copy-start.9
  48.1 2.1 %shard_map.65 = bf16[4,64,896]{2,1,0:T(8,128)(2,1)} custom-call(s32[64,64]{1,0:T(8,128)S(1)} %copy-done.6, bf16[128,384]{1,0:T(8,128)(2,1)S(1)} %copy.14.x_ref, bf16[384,3072]{1,0:T(8,128)(2,1)S(1)} %copy-done, bf16[384,3072]{1,0:T(8,128)(2,1)S(1)} %copy-done.3, bf16[256,384]{1,0:T(8,128)(2,1)S(1)} %bitcast.9, ...), custom_call_target="tpu_custom_call" | custom-call | tf_op jit(solution)/shard_map/pallas_call | solution.py:163
  50.3 4.2 %all-to-all-start.1 = ((bf16[4,64,896]{2,1,0:T(8,128)(2,1)}), bf16[4,64,896]{2,1,0:T(8,128)(2,1)S(1)}, u32[]{:S(2)}, u32[]{:S(2)}) async-start(bf16[4,64,896]{2,1,0:T(8,128)(2,1)} %shard_map.65), calls=%async_computation.1 | async-start | bytes 917504 | tf_op jit(solution)/shard_map/all_to_all | solution.py:197
  54.5 0.0 copy-done.10
  54.5 2.6 %collective-permute-start.3 = (bf16[256,384]{1,0:T(8,128)(2,1)S(1)}, bf16[256,384]{1,0:T(8,128)(2,1)S(1)}, u32[]{:S(2)}, u32[]{:S(2)}) collective-permute-start(bf16[256,384]{1,0:T(8,128)(2,1)S(1)} %bitcast.11), channel_id=1, source_target_pairs={{0,1},{1,0},{2,3},{3,2},{4,5},{5,4},{6,7},{7,6},{8,9},{9,8},{10,11... | collective-permute-start | bytes 589832 | tf_op jit(solution)/shard_map/ppermute | solution.py:192
  57.0 1.0 collective-permute-done.3.other_up
  58.1 0.0 copy-start.11
  58.1 0.7 copy-done.11
  58.8 3.9 %all-to-all-done.1.got_ref = bf16[4,64,896]{2,1,0:T(8,128)(2,1)S(1)} async-done(((bf16[4,64,896]{2,1,0:T(8,128)(2,1)}), bf16[4,64,896]{2,1,0:T(8,128)(2,1)S(1)}, u32[]{:S(2)}, u32[]{:S(2)}) %all-to-all-start.1) | async-done | bytes 458784 | tf_op jit(solution)/shard_map/all_to_all | solution.py:197
  62.6 0.0 copy-done.7
  62.6 0.0 copy-done.1
  62.6 0.0 copy-done.9
  62.7 0.0 copy-start.4
  62.7 1.7 %copy-done.4 = bf16[384,3072]{1,0:T(8,128)(2,1)S(1)} copy-done((bf16[384,3072]{1,0:T(8,128)(2,1)S(1)}, bf16[384,3072]{1,0:T(8,128)(2,1)}, u32[]{:S(2)}) %copy-start.4) | copy-done | bytes 2359320
  64.3 0.0 copy-start.12
  64.3 0.9 copy-done.12
  65.2 1.6 %shard_map.66 = (bf16[4,64,896]{2,1,0:T(8,128)(2,1)S(1)}, bf16[64,768]{1,0:T(8,128)(2,1)S(1)}) custom-call(s32[64,64]{1,0:T(8,128)S(1)} %copy-done.7, bf16[128,384]{1,0:T(8,128)(2,1)S(1)} %copy.14.x_ref, bf16[4,64,896]{2,1,0:T(8,128)(2,1)S(1)} %all-to-all-done.1.got_ref, bf16[256,384]{1,0:T(8,128)(2,1)S(1)} %bitcast.12, bf16[256,384]{1,0:T(8,128)(2,1)S(1)} %copy-done.12, ...), custom_call_target="tpu_custom_call" | custom-call | tf_op jit(solution)/shard_map/pallas_call | solution.py:163
  66.9 9.6 %all_to_all.20.got_ref = bf16[4,64,896]{2,1,0:T(8,128)(2,1)S(1)} all-to-all(bf16[4,64,896]{2,1,0:T(8,128)(2,1)S(1)} %get-tuple-element.8), channel_id=1, replica_groups=mesh['rep'=64,'y'=4,'c'=2] {'y'}, dimensions={0} | all-to-all | bytes 917504 | tf_op jit(solution)/shard_map/all_to_all | solution.py:197
  76.5 0.6 shard_map.67
  77.1 0.1 reshape.22
  77.2 26.9 %all_to_all.21 = bf16[128,2,384]{2,1,0:T(2,128)(2,1)S(1)} all-to-all(bf16[128,2,384]{2,1,0:T(2,128)(2,1)S(1)} %reshape.22), channel_id=1, replica_groups=mesh['rep'=64,'y'=4,'c'=2] {'rep','c'}, dimensions={0} | all-to-all | bytes 393216 | tf_op jit(solution)/shard_map/all_to_all | solution.py:222
  104.1 1.1 %shard_map.68 = bf16[2,128,384]{2,1,0:T(8,128)(2,1)} custom-call(s32[64,64]{1,0:T(8,128)S(1)} %copy-done.7, bf16[128,768]{1,0:T(8,128)(2,1)S(1)} %bitcast.14), custom_call_target="tpu_custom_call" | custom-call | tf_op jit(solution)/shard_map/pallas_call | solution.py:163
  (1 shorter events, 0.0 us)
Async XLA Ops:
  0.0 41.7 %collective-permute-start = (bf16[384,3072]{1,0:T(8,128)(2,1)}, bf16[384,3072]{1,0:T(8,128)(2,1)S(1)}, u32[]{:S(2)}, u32[]{:S(2)}) collective-permute-start(bf16[384,3072]{1,0:T(8,128)(2,1)} %refs_0_.3), channel_id=1, source_target_pairs={{0,1},{1,0},{2,3},{3,2},{4,5},{5,4},{6,7},{7,6},{8,9},{9,8},{10,11... | collective-permute-start | bytes 7077896 | tf_op jit(solution)/shard_map/ppermute | solution.py:192
  8.8 0.8 copy-start.5
  9.5 0.9 copy-start.13
  11.7 29.7 %all-to-all-start = ((bf16[128,2,192]{2,1,0:T(2,128)(2,1)}), bf16[128,2,192]{2,1,0:T(2,128)(2,1)S(1)}, u32[]{:S(2)}, u32[]{:S(2)}) async-start(bf16[128,2,192]{2,1,0:T(2,128)(2,1)} %copy.11), calls=%async_computation | async-start | bytes 262144 | tf_op jit(solution)/shard_map/all_to_all | solution.py:183
  25.3 16.4 %collective-permute-start.1 = (bf16[256,384]{1,0:T(8,128)(2,1)}, bf16[256,384]{1,0:T(8,128)(2,1)S(1)}, u32[]{:S(2)}, u32[]{:S(2)}) collective-permute-start(bf16[256,384]{1,0:T(8,128)(2,1)} %bitcast.8), channel_id=1, source_target_pairs={{0,1},{1,0},{2,3},{3,2},{4,5},{5,4},{6,7},{7,6},{8,9},{9,8},{10,11... | collective-permute-start | bytes 589832 | tf_op jit(solution)/shard_map/ppermute | solution.py:192
  28.8 12.8 %collective-permute-start.2 = (f32[1,384]{1,0:T(1,128)S(1)}, f32[1,384]{1,0:T(1,128)S(1)}, u32[]{:S(2)}, u32[]{:S(2)}) collective-permute-start(f32[1,384]{1,0:T(1,128)S(1)} %broadcast_in_dim.3.refs_4_), channel_id=1, source_target_pairs={{0,1},{1,0},{2,3},{3,2},{4,5},{5,4},{6,7},{7,6},{8,9},{9,8},{10,11... | collective-permute-start | bytes 4616 | tf_op jit(solution)/shard_map/ppermute | solution.py:192
  41.5 21.2 %copy-start.7 = (s32[64,64]{1,0:T(8,128)S(1)}, s32[64,64]{1,0:T(8,128)}, u32[]{:S(2)}) copy-start(s32[64,64]{1,0:T(8,128)} %requests_ref.9) | copy-start | bytes 49156
  41.7 1.4 %copy-start.2 = (bf16[384,3072]{1,0:T(8,128)(2,1)}, bf16[384,3072]{1,0:T(8,128)(2,1)S(1)}, u32[]{:S(2)}) copy-start(bf16[384,3072]{1,0:T(8,128)(2,1)S(1)} %collective-permute-done.refs_1_) | copy-start | bytes 7077892
  43.1 1.7 %copy-start = (bf16[384,3072]{1,0:T(8,128)(2,1)S(1)}, bf16[384,3072]{1,0:T(8,128)(2,1)}, u32[]{:S(2)}) copy-start(bf16[384,3072]{1,0:T(8,128)(2,1)} %refs_0_.3) | copy-start | bytes 7077892
  44.8 1.7 %copy-start.3 = (bf16[384,3072]{1,0:T(8,128)(2,1)S(1)}, bf16[384,3072]{1,0:T(8,128)(2,1)}, u32[]{:S(2)}) copy-start(bf16[384,3072]{1,0:T(8,128)(2,1)} %copy-done.2) | copy-start | bytes 7077892
  46.4 0.8 copy-start.6
  47.2 0.9 copy-start.8
  48.1 6.3 %copy-start.10 = (bf16[4,64,384]{2,1,0:T(8,128)(2,1)S(1)}, bf16[4,64,384]{2,1,0:T(8,128)(2,1)}, u32[]{:S(2)}) copy-start(bf16[4,64,384]{2,1,0:T(8,128)(2,1)} %param.10) | copy-start | bytes 589828
  48.1 14.5 %copy-start.1 = (bf16[384,3072]{1,0:T(8,128)(2,1)S(1)}, bf16[384,3072]{1,0:T(8,128)(2,1)}, u32[]{:S(2)}) copy-start(bf16[384,3072]{1,0:T(8,128)(2,1)} %refs_0_.3) | copy-start | bytes 7077892
  48.1 14.5 %copy-start.9 = (bf16[4,384,64]{1,2,0:T(8,128)(2,1)S(1)}, bf16[4,384,64]{1,2,0:T(8,128)(2,1)}, u32[]{:S(2)}) copy-start(bf16[4,384,64]{1,2,0:T(8,128)(2,1)} %param.9) | copy-start | bytes 589828
  50.3 12.4 %all-to-all-start.1 = ((bf16[4,64,896]{2,1,0:T(8,128)(2,1)}), bf16[4,64,896]{2,1,0:T(8,128)(2,1)S(1)}, u32[]{:S(2)}, u32[]{:S(2)}) async-start(bf16[4,64,896]{2,1,0:T(8,128)(2,1)} %shard_map.65), calls=%async_computation.1 | async-start | bytes 917504 | tf_op jit(solution)/shard_map/all_to_all | solution.py:197
  54.5 3.6 %collective-permute-start.3 = (bf16[256,384]{1,0:T(8,128)(2,1)S(1)}, bf16[256,384]{1,0:T(8,128)(2,1)S(1)}, u32[]{:S(2)}, u32[]{:S(2)}) collective-permute-start(bf16[256,384]{1,0:T(8,128)(2,1)S(1)} %bitcast.11), channel_id=1, source_target_pairs={{0,1},{1,0},{2,3},{3,2},{4,5},{5,4},{6,7},{7,6},{8,9},{9,8},{10,11... | collective-permute-start | bytes 589832 | tf_op jit(solution)/shard_map/ppermute | solution.py:192
  58.1 0.7 copy-start.11
  62.7 1.7 %copy-start.4 = (bf16[384,3072]{1,0:T(8,128)(2,1)S(1)}, bf16[384,3072]{1,0:T(8,128)(2,1)}, u32[]{:S(2)}) copy-start(bf16[384,3072]{1,0:T(8,128)(2,1)} %copy-done.2) | copy-start | bytes 7077892
  64.3 0.9 copy-start.12

commit v4 on v3

v4 whole, which is shorter than its diff:
```python
import functools

import jax
import jax.numpy as jnp
from jax import lax
from jax.experimental import pallas as pl
from jax.experimental.pallas import tpu as pltpu
from jax.sharding import Mesh, PartitionSpec as P

DRAFT = 2
LANES = 128
EPSILON = 1e-06
TURN = 34
TURN_Y = 2
SLOT = 4

bf16, f32, i32 = jnp.bfloat16, jnp.float32, jnp.int32


def iota(shape, dim):
    return lax.broadcasted_iota(i32, shape, dim)


def mm(left, right):
    return jnp.dot(left, right, preferred_element_type=f32)


def mm_t(left, right):
    return lax.dot_general(left, right, (((1,), (1,)), ((), ())), preferred_element_type=f32)


def t_mm(left, right):
    return lax.dot_general(left, right, (((0,), (0,)), ((), ())), preferred_element_type=f32)


def moved_rows(my_requests, kept, blocks):
    rows = 2 * blocks
    repeat = (iota((blocks, rows), 1) // 2 == iota((blocks, rows), 0)).astype(bf16)
    owner = jnp.broadcast_to((my_requests // kept).astype(f32).astype(bf16), (8, blocks))
    place = (mm(owner, repeat)[:1].astype(i32) + (blocks - TURN)) % blocks
    return place * 2 + iota((1, rows), 1) % 2


def permute_in(kept, requests_hbm, x_hbm, sent_ref, requests_ref, x_ref, sems):
    x_copy = pltpu.make_async_copy(x_hbm, x_ref, sems.at[0])
    requests_copy = pltpu.make_async_copy(requests_hbm, requests_ref, sems.at[1])
    x_copy.start()
    requests_copy.start()
    requests_copy.wait()
    me = lax.axis_index("rep")
    blocks = requests_ref.shape[1]
    rows = 2 * blocks
    target = SLOT * moved_rows(requests_ref[pl.ds(me, 1), :], kept, blocks)
    picks = [
        (target + part == iota((SLOT * rows, rows), 0)).astype(bf16)
        for part in range(x_ref.shape[1] // LANES)
    ]
    x_copy.wait()
    sent_ref[...] = sum(
        mm(pick, x_ref[:, part * LANES : (part + 1) * LANES]) for part, pick in enumerate(picks)
    ).astype(bf16)


def permute_out(kept, requests_ref, home_ref, out_ref):
    me = lax.axis_index("rep")
    blocks = requests_ref.shape[1]
    width = out_ref.shape[2]
    target = moved_rows(requests_ref[pl.ds(me, 1), :], kept, blocks)
    pick = (target == iota((2 * blocks, 2 * blocks), 0)).astype(bf16)
    for step in range(DRAFT):
        out_ref[step] = t_mm(pick, home_ref[:, step * width : (step + 1) * width]).astype(bf16)


def find_held(kept, requests_ref, held_ref):
    requests = requests_ref[...]
    groups = requests.shape[0]
    held = jnp.sum(
        jnp.where(requests // kept == lax.axis_index("rep"), requests % kept, 0),
        axis=1,
        keepdims=True,
    )
    held = jnp.broadcast_to(held.astype(f32), (groups, LANES)).astype(bf16)
    turn = (iota((groups, groups), 0) + TURN) % groups == iota((groups, groups), 1)
    held_ref[...] = mm(turn.astype(bf16), held).astype(i32)


def products(wide, kept, held_ref, weight, down, scale, message_ref, arrived=None):
    count, chip_width = wide.shape
    rank_cols = down.shape[0]
    rank = rank_cols // kept
    chips = message_ref.shape[0]
    scaled = (wide * scale[...]).astype(bf16)
    squares = jnp.sum(wide * wide, axis=1, keepdims=True)
    top = squares.astype(bf16).astype(f32)
    lane = iota((count, LANES), 1)
    fold = iota((rank_cols, LANES), 0) % rank == iota((rank_cols, LANES), 1)
    owned = iota((count, rank_cols), 1) // rank == held_ref[:, :1]
    if arrived is not None:
        arrived(0)
    ranks = mm_t(scaled, down[...]).astype(bf16)
    ranks = jnp.where(owned, ranks, 0).astype(bf16)
    extra = mm(ranks, fold.astype(bf16))
    extra = jnp.where(lane == rank, top, extra)
    extra = jnp.where(lane == rank + 1, squares - top, extra).astype(bf16)
    for place in range(chips):
        chip = (place + TURN_Y) % chips
        if arrived is not None:
            arrived(1 + chip)
        message_ref[place, :, :chip_width] = mm(
            scaled, weight[:, chip * chip_width : (chip + 1) * chip_width]
        ).astype(bf16)
        message_ref[place, :, chip_width:] = extra


def update(wide, kept, held_ref, got_ref, up):
    count, chip_width = wide.shape
    rank_cols = up.shape[0]
    rank = rank_cols // kept
    chips = got_ref.shape[0]
    total = got_ref[0].astype(f32)
    for chip in range(1, chips):
        total += got_ref[chip].astype(f32)
    extra = total[:, chip_width:]
    lane = iota((count, LANES), 1)
    is_square = (lane == rank) | (lane == rank + 1)
    mean = jnp.sum(jnp.where(is_square, extra, 0.0), axis=1, keepdims=True) / (chip_width * chips)
    factor = lax.rsqrt(mean + EPSILON)
    ranks = jnp.where(lane < rank, extra * factor, 0.0).astype(bf16)
    unfold = iota((LANES, rank_cols), 1) % rank == iota((LANES, rank_cols), 0)
    spread = mm(ranks, unfold.astype(bf16))
    owned = iota((count, rank_cols), 1) // rank == held_ref[:, :1]
    spread = jnp.where(owned, spread, 0.0).astype(bf16)
    delta = mm(spread, up[...]).astype(bf16).astype(f32)
    return (wide + total[:, :chip_width] * factor + delta).astype(bf16)


def moved_in(x_ref):
    slots, lanes = x_ref.shape
    groups = slots // (2 * SLOT)
    parts = [(core, part) for core in range(2) for part in range(SLOT - 1)]
    row, slot = iota((groups, slots), 0), iota((groups, slots), 1)
    picks = [(slot == (2 * row + core) * SLOT + part).astype(bf16) for core, part in parts]
    rows = mm(jnp.concatenate(picks), x_ref[...])
    return jnp.concatenate(
        [rows[index * groups : (index + 1) * groups] for index in range(len(parts))], axis=1
    )


def first_products(kept, *refs):
    matrices, (scale, other_scale, x_ref, held_ref) = refs[:6], refs[6:10]
    message_ref, wide_ref, weight_out, down_out, up_out, scale_out, sems = refs[10:]
    width = scale.shape[1]
    chip_width = 2 * width
    chips = message_ref.shape[0]
    core = lax.axis_index("c")
    pieces = [[] for _ in range(chips + 2)]

    def add(piece, source, target):
        index = sum(map(len, pieces))
        copy = pltpu.make_async_copy(source, target, sems.at[index])
        copy.start()
        pieces[piece].append(copy)

    places = [
        pl.ds(pl.multiple_of(jnp.where(core == index, 0, width), LANES), width)
        for index in range(2)
    ]
    for index in range(2):
        add(0, matrices[1 + 3 * index], down_out.at[:, places[index]])
    for place in range(chips):
        chip = (place + TURN_Y) % chips
        cols = pl.ds(chip * chip_width, chip_width)
        for index in range(2):
            add(1 + chip, matrices[3 * index].at[:, cols], weight_out.at[places[index], cols])
    for index in range(2):
        add(chips + 1, matrices[2 + 3 * index], up_out.at[:, places[index]])

    def arrived(piece):
        for copy in pieces[piece]:
            copy.wait()

    low = jnp.where(core == 0, scale[...], other_scale[...])
    high = jnp.where(core == 0, other_scale[...], scale[...])
    scale_out[...] = jnp.concatenate([low, high], axis=1)
    wide = moved_in(x_ref)
    wide_ref[...] = wide.astype(bf16)
    products(wide, kept, held_ref, weight_out, down_out, scale_out, message_ref, arrived)
    arrived(chips + 1)


def next_products(kept, wide_ref, got_ref, held_ref, weight, down, up, scale, message_ref, state_ref):
    state = update(wide_ref[...].astype(f32), kept, held_ref, got_ref, up)
    state_ref[...] = state
    products(state.astype(f32), kept, held_ref, weight, down, scale, message_ref)


def last_update(kept, state_ref, got_ref, held_ref, up, back_ref):
    rows, cols = back_ref.shape
    width = cols // DRAFT
    old = state_ref[...]
    new = update(old.astype(f32), kept, held_ref, got_ref, up)
    row, place = iota((rows // 2, rows), 0), iota((rows // 2, rows), 1)
    picks = [(place == 2 * row + core).astype(bf16) for core in range(2)]
    for step, state in enumerate((old, new)):
        back_ref[:, step * width : (step + 1) * width] = sum(
            t_mm(pick, state[:, core * width : (core + 1) * width])
            for core, pick in enumerate(picks)
        ).astype(bf16)


def call(kernel, outs, operands, far=0, loose=0, **kwargs):
    spaces = [pltpu.HBM] * far + [pl.ANY] * loose
    spaces += [pltpu.VMEM] * (len(operands) - len(spaces))
    return pl.pallas_call(
        kernel,
        out_shape=outs,
        in_specs=[pl.BlockSpec(memory_space=space) for space in spaces],
        out_specs=[pl.BlockSpec(memory_space=pltpu.VMEM)] * len(outs),
        compiler_params=pltpu.CompilerParams(vmem_limit_bytes=24 * 2**20),
        **kwargs,
    )(*map(pltpu.with_memory_space_constraint, operands, spaces))


def shards(first_hidden_rows, norm_scale, projection_weight, down_weights, up_weights, requests):
    groups = lax.axis_size("rep")
    chips = lax.axis_size("y")
    cores = lax.axis_size("c")
    rows, width = first_hidden_rows.shape
    chip_width = width * cores
    kept, _, rank = down_weights.shape
    rank_cols = kept * rank

    def resident(shape, dtype=bf16):
        return pltpu.VMEM(shape, dtype)

    (sent,) = call(
        functools.partial(permute_in, kept),
        [resident((SLOT * rows, LANES))],
        [requests, first_hidden_rows],
        far=2,
        scratch_shapes=[
            pltpu.VMEM(requests.shape, i32),
            pltpu.VMEM((rows, width), bf16),
            pltpu.SemaphoreType.DMA((2,)),
        ],
    )
    movers = [[(place + TURN * cores) % rows for place in range(rows)]]
    adders = [[(place + TURN_Y) % chips for place in range(chips)]]

    def move(value):
        return lax.all_to_all(
            value, ("rep", "c"), split_axis=0, concat_axis=0, axis_index_groups=movers, tiled=True
        )

    def exchange(message):
        return lax.all_to_all(
            message, "y", split_axis=0, concat_axis=0, axis_index_groups=adders, tiled=True
        )

    got = move(sent.reshape(rows, SLOT, LANES)).reshape(SLOT * rows, LANES)

    sibling = [(core, cores - 1 - core) for core in range(cores)]
    down = jnp.transpose(down_weights, (0, 2, 1)).reshape(rank_cols, width)
    up = up_weights.reshape(rank_cols, width)
    matrices = [projection_weight, down, up]
    others = [lax.ppermute(value, "c", sibling) for value in matrices]
    scale = norm_scale[None]
    (held,) = call(
        functools.partial(find_held, kept),
        [resident((groups, LANES), i32)],
        [requests],
    )

    message_shape = resident((chips, groups, chip_width + LANES))
    state_shape = resident((groups, chip_width))
    message, wide, weight, down, up, scale = call(
        functools.partial(first_products, kept),
        [
            message_shape,
            state_shape,
            resident((chip_width, projection_weight.shape[1])),
            resident((rank_cols, chip_width)),
            resident((rank_cols, chip_width)),
            resident((1, chip_width), f32),
        ],
        matrices + others + [scale, lax.ppermute(scale, "c", sibling), got, held],
        far=len(matrices),
        loose=len(others),
        scratch_shapes=[pltpu.SemaphoreType.DMA((2 * chips + 4,))],
    )
    message, state = call(
        functools.partial(next_products, kept),
        [message_shape, state_shape],
        [wide, exchange(message), held, weight, down, up, scale],
    )
    (back,) = call(
        functools.partial(last_update, kept),
        [resident((rows, DRAFT * width))],
        [state, exchange(message), held, up],
    )
    home = move(back.reshape(rows, DRAFT, width)).reshape(rows, DRAFT * width)
    (result,) = call(
        functools.partial(permute_out, kept),
        [jax.ShapeDtypeStruct((DRAFT, rows, width), bf16)],
        [requests, home],
    )
    return result


def solution(mesh):
    chip_mesh = Mesh(mesh.devices.reshape(mesh.shape["rep"], -1, 2), ("rep", "y", "c"))
    tp = ("y", "c")
    return jax.shard_map(
        shards,
        mesh=chip_mesh,
        in_specs=(
            P("rep", tp),
            P(tp),
            P(tp, None),
            P("rep", tp, None),
            P("rep", None, tp),
            P(),
        ),
        out_specs=P(None, "rep", tp),
        check_vma=False,
    )
```

time: 107 us -> 91.8 us (0.86); the launches traced: 105 us -> 91.2 us
  waiting for transfers between devices: 15.6 us -> 0.01 us
  local copies, waits for them, and re-layouts: 13.3 us -> 1.52 us
  blocking collectives: 36.6 us -> 48.1 us
  Pallas kernels: 5.66 us -> 8.18 us
    all_to_all x2 -> x1, waiting for transfers between devices: 14.5 us -> 0.01 us  [move(): lax.all_to_all(value, ('rep', 'c'), split_axis=0, concat_axis=0, axis_ind...]
    all_to_all x2 -> x3, blocking collectives: 36.6 us -> 48.1 us  [the longest x1 26.4 us: move(): lax.all_to_all(value, ('rep', 'c'), split_axis=0, concat_axis=0, axis_ind...]
    unnamed x29 -> x5, local copies, waits for them, and re-layouts: 11.4 us -> 0.78 us
    pallas_call x5 -> x6, Pallas kernels: 5.66 us -> 8.18 us  [call(): pl.pallas_call(kernel, out_shape=outs, in_specs=[pl.BlockSpec(memory_spac...]
    all_to_all x2 -> x1, starting transfers between devices: 17.8 us -> 18 us  [move(): lax.all_to_all(value, ('rep', 'c'), split_axis=0, concat_axis=0, axis_ind...]
  transfers between devices with their start and end apart: 6 -> 5, of which waited for: 3 -> 0; matrix products, arithmetic and copies ran while one was open for 2% -> 1% of each run, Pallas kernels for 0% -> 2%
where the time goes in v4:
time: 91.8 us; the launch traced here: 91.2 us
  blocking collectives  48.1 us (52%)
  starting transfers between devices  33.3 us (36%)
  Pallas kernels  8.18 us (9%)
  local copies, waits for them, and re-layouts  1.52 us (2%)
    all_to_all x1, blocking collectives, move(): lax.all_to_all(value, ('rep', 'c'), split_axis=0, concat_axis=0, axis_ind...  26.4 us
    all_to_all x2, blocking collectives, exchange(): lax.all_to_all(message, 'y', split_axis=0, concat_axis=0, axis_index_grou...  21.6 us
    all_to_all x1, starting transfers between devices, move(): lax.all_to_all(value, ('rep', 'c'), split_axis=0, concat_axis=0, axis_ind...  18 us
    ppermute x3, starting transfers between devices, shards(): others = [lax.ppermute(value, 'c', sibling) for value in matrices]  13.1 us
    pallas_call x6, Pallas kernels, call(): pl.pallas_call(kernel, out_shape=outs, in_specs=[pl.BlockSpec(memory_spac...  8.18 us
    ppermute x1, starting transfers between devices, shards(): lax.ppermute(scale, 'c', sibling)  2.26 us
  transfers between devices with their start and end apart: 5, of which 0 were waited for; matrix products, arithmetic and copies ran while one was open for 1% of the time, Pallas kernels for 2%

profile of v4, /device:TPU:1, one launch (start us, length us, event | category | flops | bytes accessed | tf_op | source)
XLA Modules:
  0.0 91.2 jit_solution(7953935836145964966)
XLA Ops:
  0.0 8.8 %collective-permute-start = (bf16[384,3072]{1,0:T(8,128)(2,1)}, bf16[384,3072]{1,0:T(8,128)(2,1)S(1)}, u32[]{:S(2)}, u32[]{:S(2)}) collective-permute-start(bf16[384,3072]{1,0:T(8,128)(2,1)} %refs_0_.1), channel_id=1, source_target_pairs={{0,1},{1,0},{2,3},{3,2},{4,5},{5,4},{6,7},{7,6},{8,9},{9,8},{10,11... | collective-permute-start | bytes 7077896 | tf_op jit(solution)/shard_map/ppermute | solution.py:266
  8.8 2.0 %shard_map.64 = bf16[512,128]{1,0:T(8,128)(2,1)} custom-call(s32[64,64]{1,0:T(8,128)} %requests_ref.3, bf16[128,384]{1,0:T(8,128)(2,1)} %x_hbm.1), custom_call_target="tpu_custom_call" | custom-call | tf_op jit(solution)/shard_map/pallas_call | solution.py:214
  10.8 18.0 %all-to-all-start = ((bf16[128,4,128]{2,1,0:T(4,128)(2,1)}), bf16[128,4,128]{2,1,0:T(4,128)(2,1)S(1)}, u32[]{:S(2)}, u32[]{:S(2)}) async-start(bf16[128,4,128]{2,1,0:T(4,128)(2,1)} %bitcast.4), calls=%async_computation | async-start | bytes 262144 | tf_op jit(solution)/shard_map/all_to_all | solution.py:251
  28.7 2.3 %collective-permute-start.1 = (bf16[256,384]{1,0:T(8,128)(2,1)}, bf16[256,384]{1,0:T(8,128)(2,1)S(1)}, u32[]{:S(2)}, u32[]{:S(2)}) collective-permute-start(bf16[256,384]{1,0:T(8,128)(2,1)} %bitcast.11), channel_id=1, source_target_pairs={{0,1},{1,0},{2,3},{3,2},{4,5},{5,4},{6,7},{7,6},{8,9},{9,8},{10,11... | collective-permute-start | bytes 589832 | tf_op jit(solution)/shard_map/ppermute | solution.py:266
  31.0 2.1 %collective-permute-start.2 = (bf16[256,384]{1,0:T(8,128)(2,1)}, bf16[256,384]{1,0:T(8,128)(2,1)S(1)}, u32[]{:S(2)}, u32[]{:S(2)}) collective-permute-start(bf16[256,384]{1,0:T(8,128)(2,1)} %bitcast.13), channel_id=1, source_target_pairs={{0,1},{1,0},{2,3},{3,2},{4,5},{5,4},{6,7},{7,6},{8,9},{9,8},{10,11... | collective-permute-start | bytes 589832 | tf_op jit(solution)/shard_map/ppermute | solution.py:266
  33.1 0.7 broadcast_in_dim.3.refs_6_
  33.8 2.3 %collective-permute-start.3 = (f32[1,384]{1,0:T(1,128)S(1)}, f32[1,384]{1,0:T(1,128)S(1)}, u32[]{:S(2)}, u32[]{:S(2)}) collective-permute-start(f32[1,384]{1,0:T(1,128)S(1)} %broadcast_in_dim.3.refs_6_), channel_id=1, source_target_pairs={{0,1},{1,0},{2,3},{3,2},{4,5},{5,4},{6,7},{7,6},{8,9},{9,8},{10,11... | collective-permute-start | bytes 4616 | tf_op jit(solution)/shard_map/ppermute | solution.py:286
  36.0 0.0 copy-start
  36.0 0.7 copy-done
  36.8 0.2 shard_map.65.refs_9_.held_ref
  37.0 0.0 collective-permute-done.3.refs_7_
  37.0 0.0 collective-permute-done.1.refs_4_
  37.0 0.0 collective-permute-done.2.refs_5_
  37.0 0.0 all-to-all-done
  37.1 0.0 collective-permute-done.refs_3_
  37.1 3.0 %shard_map.66 = (bf16[4,64,896]{2,1,0:T(8,128)(2,1)S(1)}, bf16[64,768]{1,0:T(8,128)(2,1)S(1)}, bf16[768,3072]{1,0:T(8,128)(2,1)S(1)}, bf16[256,768]{1,0:T(8,128)...) custom-call(bf16[384,3072]{1,0:T(8,128)(2,1)} %refs_0_.1, bf16[256,384]{1,0:T(8,128)(2,1)} %bitcast.12, ...), custom_call_target="tpu_custom_call" | custom-call | tf_op jit(solution)/shard_map/pallas_call | solution.py:214
  40.1 11.4 %all_to_all.20.got_ref = bf16[4,64,896]{2,1,0:T(8,128)(2,1)S(1)} all-to-all(bf16[4,64,896]{2,1,0:T(8,128)(2,1)S(1)} %get-tuple-element.14), channel_id=1, replica_groups={{4,6,0,2},{5,7,1,3},{12,14,8,10},{13,15,9,11},{20,22,16,18},{21,23,17,1..., dimensions={0} | all-to-all | bytes 917504 | tf_op jit(solution)/shard_map/all_to_all | solution.py:256
  51.5 1.3 %shard_map.67 = (bf16[4,64,896]{2,1,0:T(8,128)(2,1)S(1)}, bf16[64,768]{1,0:T(8,128)(2,1)S(1)}) custom-call(bf16[64,768]{1,0:T(8,128)(2,1)S(1)} %get-tuple-element.13.wide_ref, bf16[4,64,896]{2,1,0:T(8,128)(2,1)S(1)} %all_to_all.20.got_ref, s32[64,128]{1,0:T(8,128)S(1)} %shard_map.65.refs_9_.held_ref, bf16[768,3072]{1,0:T(8,128)(2,1)S(1)} %get-tuple-element.15.weight, ...), custom_call_target="tpu_custom_call" | custom-call | tf_op jit(solution)/shard_map/pallas_call | solution.py:214
  52.9 0.0 copy-start.1
  52.9 10.2 %all_to_all.21.got_ref = bf16[4,64,896]{2,1,0:T(8,128)(2,1)S(1)} all-to-all(bf16[4,64,896]{2,1,0:T(8,128)(2,1)S(1)} %get-tuple-element.20), channel_id=1, replica_groups={{4,6,0,2},{5,7,1,3},{12,14,8,10},{13,15,9,11},{20,22,16,18},{21,23,17,1..., dimensions={0} | all-to-all | bytes 917504 | tf_op jit(solution)/shard_map/all_to_all | solution.py:256
  63.1 0.6 shard_map.68
  63.6 0.1 reshape.22
  63.7 26.4 %all_to_all.22 = bf16[128,2,384]{2,1,0:T(2,128)(2,1)S(1)} all-to-all(bf16[128,2,384]{2,1,0:T(2,128)(2,1)S(1)} %reshape.22), channel_id=1, replica_groups={{272,273,280,281,288,289,296,297,304,305,312,313,320,321,328,329,336,33..., dimensions={0} | all-to-all | bytes 393216 | tf_op jit(solution)/shard_map/all_to_all | solution.py:251
  90.2 0.0 copy-done.1
  90.2 1.1 %shard_map.69 = bf16[2,128,384]{2,1,0:T(8,128)(2,1)} custom-call(s32[64,64]{1,0:T(8,128)S(1)} %copy-done.1, bf16[128,768]{1,0:T(8,128)(2,1)S(1)} %bitcast.8), custom_call_target="tpu_custom_call" | custom-call | tf_op jit(solution)/shard_map/pallas_call | solution.py:214
  (1 shorter events, 0.0 us)
Async XLA Ops:
  0.0 37.1 %collective-permute-start = (bf16[384,3072]{1,0:T(8,128)(2,1)}, bf16[384,3072]{1,0:T(8,128)(2,1)S(1)}, u32[]{:S(2)}, u32[]{:S(2)}) collective-permute-start(bf16[384,3072]{1,0:T(8,128)(2,1)} %refs_0_.1), channel_id=1, source_target_pairs={{0,1},{1,0},{2,3},{3,2},{4,5},{5,4},{6,7},{7,6},{8,9},{9,8},{10,11... | collective-permute-start | bytes 7077896 | tf_op jit(solution)/shard_map/ppermute | solution.py:266
  10.8 26.3 %all-to-all-start = ((bf16[128,4,128]{2,1,0:T(4,128)(2,1)}), bf16[128,4,128]{2,1,0:T(4,128)(2,1)S(1)}, u32[]{:S(2)}, u32[]{:S(2)}) async-start(bf16[128,4,128]{2,1,0:T(4,128)(2,1)} %bitcast.4), calls=%async_computation | async-start | bytes 262144 | tf_op jit(solution)/shard_map/all_to_all | solution.py:251
  28.7 8.3 %collective-permute-start.1 = (bf16[256,384]{1,0:T(8,128)(2,1)}, bf16[256,384]{1,0:T(8,128)(2,1)S(1)}, u32[]{:S(2)}, u32[]{:S(2)}) collective-permute-start(bf16[256,384]{1,0:T(8,128)(2,1)} %bitcast.11), channel_id=1, source_target_pairs={{0,1},{1,0},{2,3},{3,2},{4,5},{5,4},{6,7},{7,6},{8,9},{9,8},{10,11... | collective-permute-start | bytes 589832 | tf_op jit(solution)/shard_map/ppermute | solution.py:266
  31.0 6.0 %collective-permute-start.2 = (bf16[256,384]{1,0:T(8,128)(2,1)}, bf16[256,384]{1,0:T(8,128)(2,1)S(1)}, u32[]{:S(2)}, u32[]{:S(2)}) collective-permute-start(bf16[256,384]{1,0:T(8,128)(2,1)} %bitcast.13), channel_id=1, source_target_pairs={{0,1},{1,0},{2,3},{3,2},{4,5},{5,4},{6,7},{7,6},{8,9},{9,8},{10,11... | collective-permute-start | bytes 589832 | tf_op jit(solution)/shard_map/ppermute | solution.py:266
  33.8 3.3 %collective-permute-start.3 = (f32[1,384]{1,0:T(1,128)S(1)}, f32[1,384]{1,0:T(1,128)S(1)}, u32[]{:S(2)}, u32[]{:S(2)}) collective-permute-start(f32[1,384]{1,0:T(1,128)S(1)} %broadcast_in_dim.3.refs_6_), channel_id=1, source_target_pairs={{0,1},{1,0},{2,3},{3,2},{4,5},{5,4},{6,7},{7,6},{8,9},{9,8},{10,11... | collective-permute-start | bytes 4616 | tf_op jit(solution)/shard_map/ppermute | solution.py:286
  36.0 0.8 copy-start
  52.9 37.3 %copy-start.1 = (s32[64,64]{1,0:T(8,128)S(1)}, s32[64,64]{1,0:T(8,128)}, u32[]{:S(2)}) copy-start(s32[64,64]{1,0:T(8,128)} %requests_ref.3) | copy-start | bytes 49156

commit v5 on v4

--- a/solution.py
+++ b/solution.py
@@ -12,6 +12,7 @@
 EPSILON = 1e-06
 TURN = 34
 TURN_Y = 2
+HINT = 2 * 10**11
 SLOT = 4
 
 bf16, f32, i32 = jnp.bfloat16, jnp.float32, jnp.int32
@@ -33,45 +34,74 @@
     return lax.dot_general(left, right, (((0,), (0,)), ((), ())), preferred_element_type=f32)
 
 
-def moved_rows(my_requests, kept, blocks):
-    rows = 2 * blocks
-    repeat = (iota((blocks, rows), 1) // 2 == iota((blocks, rows), 0)).astype(bf16)
-    owner = jnp.broadcast_to((my_requests // kept).astype(f32).astype(bf16), (8, blocks))
-    place = (mm(owner, repeat)[:1].astype(i32) + (blocks - TURN)) % blocks
-    return place * 2 + iota((1, rows), 1) % 2
-
-
-def permute_in(kept, requests_hbm, x_hbm, sent_ref, requests_ref, x_ref, sems):
-    x_copy = pltpu.make_async_copy(x_hbm, x_ref, sems.at[0])
-    requests_copy = pltpu.make_async_copy(requests_hbm, requests_ref, sems.at[1])
-    x_copy.start()
-    requests_copy.start()
-    requests_copy.wait()
+def holder_places(my_requests, kept):
+    blocks = my_requests.shape[1]
+    return (my_requests // kept + (blocks - TURN)) % blocks
+
+
+def split(values):
+    high = values.astype(bf16).astype(f32)
+    middle = (values - high).astype(bf16).astype(f32)
+    return high, middle, values - high - middle
+
+
+def permute_in(kept, requests_hbm, x_hbm, scale_hbm, sent_ref, requests_ref, x_ref, scale_ref, sems):
+    copies = [
+        pltpu.make_async_copy(source, target, sems.at[index])
+        for index, (source, target) in enumerate(
+            ((requests_hbm, requests_ref), (x_hbm, x_ref), (scale_hbm, scale_ref))
+        )
+    ]
+    for copy in copies:
+        copy.start()
     me = lax.axis_index("rep")
     blocks = requests_ref.shape[1]
-    rows = 2 * blocks
-    target = SLOT * moved_rows(requests_ref[pl.ds(me, 1), :], kept, blocks)
-    picks = [
-        (target + part == iota((SLOT * rows, rows), 0)).astype(bf16)
-        for part in range(x_ref.shape[1] // LANES)
+    rows, width = x_ref.shape
+    slots = sent_ref.shape[0]
+    parts = width // LANES
+    row_picks = [
+        (iota((blocks, rows), 1) == 2 * iota((blocks, rows), 0) + half).astype(bf16)
+        for half in range(2)
     ]
-    x_copy.wait()
-    sent_ref[...] = sum(
-        mm(pick, x_ref[:, part * LANES : (part + 1) * LANES]) for part, pick in enumerate(picks)
-    ).astype(bf16)
+    piece, block = iota((slots, 2 * parts * blocks), 1) // blocks, iota((slots, 2 * parts * blocks), 1) % blocks
+    slot = (2 * block + piece // parts) * SLOT + piece % parts
+    lay_out = (iota((slots, 2 * parts * blocks), 0) == slot).astype(bf16)
+    copies[1].wait()
+    halves = [mm(pick, x_ref[...]).astype(bf16) for pick in row_picks]
+    copies[2].wait()
+    wanted = (me + (blocks - TURN)) % blocks % (3 * parts)
+    gain = jnp.zeros((1, LANES), f32)
+    for part in range(parts):
+        for index, value in enumerate(split(scale_ref[part : part + 1, :])):
+            gain = jnp.where(wanted == 3 * part + index, value, gain)
+    copies[0].wait()
+    places = holder_places(requests_ref[pl.ds(me, 1), :], kept)
+    pick = (places == iota((blocks, blocks), 0)).astype(bf16)
+    picked = [mm(pick, half).astype(bf16) for half in halves]
+    stacked = jnp.concatenate(
+        [half[:, part * LANES : (part + 1) * LANES] for half in picked for part in range(parts)]
+    )
+    padding = iota((slots, LANES), 0) % SLOT == parts
+    sent_ref[...] = jnp.where(padding, gain, mm(lay_out, stacked)).astype(bf16)
 
 
 def permute_out(kept, requests_ref, home_ref, out_ref):
     me = lax.axis_index("rep")
     blocks = requests_ref.shape[1]
-    width = out_ref.shape[2]
-    target = moved_rows(requests_ref[pl.ds(me, 1), :], kept, blocks)
-    pick = (target == iota((2 * blocks, 2 * blocks), 0)).astype(bf16)
+    rows, width = out_ref.shape[1:]
+    repeat = (iota((blocks, rows), 1) // 2 == iota((blocks, rows), 0)).astype(bf16)
+    places = holder_places(requests_ref[pl.ds(me, 1), :], kept)
+    places = jnp.broadcast_to(places.astype(f32), (8, blocks)).astype(bf16)
+    target = mm(places, repeat)[:1].astype(i32) * 2 + iota((1, rows), 1) % 2
+    pick = (target == iota((rows, rows), 0)).astype(bf16)
     for step in range(DRAFT):
         out_ref[step] = t_mm(pick, home_ref[:, step * width : (step + 1) * width]).astype(bf16)
 
 
-def find_held(kept, requests_ref, held_ref):
+def find_held(kept, requests_hbm, held_ref, requests_ref, sem):
+    copy = pltpu.make_async_copy(requests_hbm, requests_ref, sem)
+    copy.start()
+    copy.wait()
     requests = requests_ref[...]
     groups = requests.shape[0]
     held = jnp.sum(
@@ -140,17 +170,23 @@
     parts = [(core, part) for core in range(2) for part in range(SLOT - 1)]
     row, slot = iota((groups, slots), 0), iota((groups, slots), 1)
     picks = [(slot == (2 * row + core) * SLOT + part).astype(bf16) for core, part in parts]
+    row, slot = iota((16, slots), 0), iota((16, slots), 1)
+    place, core = slot // (2 * SLOT), slot // SLOT % 2
+    padding = (slot % SLOT == SLOT - 1) & (place < 3 * (SLOT - 1))
+    picks.append((padding & (row == core * (SLOT - 1) + place // 3)).astype(bf16))
     rows = mm(jnp.concatenate(picks), x_ref[...])
-    return jnp.concatenate(
+    gains = rows[len(parts) * groups :]
+    wide = jnp.concatenate(
         [rows[index * groups : (index + 1) * groups] for index in range(len(parts))], axis=1
     )
+    return wide, jnp.concatenate([gains[index : index + 1] for index in range(len(parts))], axis=1)
 
 
 def first_products(kept, *refs):
-    matrices, (scale, other_scale, x_ref, held_ref) = refs[:6], refs[6:10]
-    message_ref, wide_ref, weight_out, down_out, up_out, scale_out, sems = refs[10:]
-    width = scale.shape[1]
-    chip_width = 2 * width
+    (x_ref, held_ref), matrices = refs[:2], (refs[5:8], refs[2:5])
+    message_ref, wide_ref, weight_out, down_out, up_out, scale_out, sems = refs[8:]
+    chip_width = wide_ref.shape[1]
+    width = chip_width // 2
     chips = message_ref.shape[0]
     core = lax.axis_index("c")
     pieces = [[] for _ in range(chips + 2)]
@@ -166,23 +202,21 @@
         for index in range(2)
     ]
     for index in range(2):
-        add(0, matrices[1 + 3 * index], down_out.at[:, places[index]])
+        add(0, matrices[index][0], down_out.at[:, places[index]])
     for place in range(chips):
         chip = (place + TURN_Y) % chips
         cols = pl.ds(chip * chip_width, chip_width)
         for index in range(2):
-            add(1 + chip, matrices[3 * index].at[:, cols], weight_out.at[places[index], cols])
+            add(1 + chip, matrices[index][2].at[:, cols], weight_out.at[places[index], cols])
     for index in range(2):
-        add(chips + 1, matrices[2 + 3 * index], up_out.at[:, places[index]])
+        add(chips + 1, matrices[index][1], up_out.at[:, places[index]])
 
     def arrived(piece):
         for copy in pieces[piece]:
             copy.wait()
 
-    low = jnp.where(core == 0, scale[...], other_scale[...])
-    high = jnp.where(core == 0, other_scale[...], scale[...])
-    scale_out[...] = jnp.concatenate([low, high], axis=1)
-    wide = moved_in(x_ref)
+    wide, scale = moved_in(x_ref)
+    scale_out[...] = scale
     wide_ref[...] = wide.astype(bf16)
     products(wide, kept, held_ref, weight_out, down_out, scale_out, message_ref, arrived)
     arrived(chips + 1)
@@ -208,9 +242,8 @@
         ).astype(bf16)
 
 
-def call(kernel, outs, operands, far=0, loose=0, **kwargs):
-    spaces = [pltpu.HBM] * far + [pl.ANY] * loose
-    spaces += [pltpu.VMEM] * (len(operands) - len(spaces))
+def call(kernel, outs, operands, far=0, **kwargs):
+    spaces = [pltpu.VMEM] * (len(operands) - far) + [pltpu.HBM] * far
     return pl.pallas_call(
         kernel,
         out_shape=outs,
@@ -236,12 +269,13 @@
     (sent,) = call(
         functools.partial(permute_in, kept),
         [resident((SLOT * rows, LANES))],
-        [requests, first_hidden_rows],
-        far=2,
+        [requests, first_hidden_rows, norm_scale.reshape(-1, LANES)],
+        far=3,
         scratch_shapes=[
             pltpu.VMEM(requests.shape, i32),
             pltpu.VMEM((rows, width), bf16),
-            pltpu.SemaphoreType.DMA((2,)),
+            pltpu.VMEM((width // LANES, LANES), f32),
+            pltpu.SemaphoreType.DMA((3,)),
         ],
     )
     movers = [[(place + TURN * cores) % rows for place in range(rows)]]
@@ -262,13 +296,15 @@
     sibling = [(core, cores - 1 - core) for core in range(cores)]
     down = jnp.transpose(down_weights, (0, 2, 1)).reshape(rank_cols, width)
     up = up_weights.reshape(rank_cols, width)
-    matrices = [projection_weight, down, up]
+    matrices = [down, up, projection_weight]
     others = [lax.ppermute(value, "c", sibling) for value in matrices]
-    scale = norm_scale[None]
     (held,) = call(
         functools.partial(find_held, kept),
         [resident((groups, LANES), i32)],
         [requests],
+        far=1,
+        scratch_shapes=[pltpu.VMEM(requests.shape, i32), pltpu.SemaphoreType.DMA(())],
+        cost_estimate=pl.CostEstimate(flops=HINT, bytes_accessed=0, transcendentals=0),
     )
 
     message_shape = resident((chips, groups, chip_width + LANES))
@@ -283,9 +319,8 @@
             resident((rank_cols, chip_width)),
             resident((1, chip_width), f32),
         ],
-        matrices + others + [scale, lax.ppermute(scale, "c", sibling), got, held],
+        [got, held] + others + matrices,
         far=len(matrices),
-        loose=len(others),
         scratch_shapes=[pltpu.SemaphoreType.DMA((2 * chips + 4,))],
     )
     message, state = call(

time: 91.8 us -> 94.7 us (1.032)
  waiting for transfers between devices: 0.01 us -> 3.46 us
  Pallas kernels: 8.18 us -> 11.1 us
  starting transfers between devices: 33.3 us -> 31.8 us
  local copies, waits for them, and re-layouts: 1.52 us -> 0.08 us
    all_to_all x1, starting transfers between devices: 18 us -> 25.2 us  [move(): lax.all_to_all(value, ('rep', 'c'), split_axis=0, concat_axis=0, axis_ind...]
    ppermute x3, starting transfers between devices: 13.1 us -> 6.61 us  [shards(): others = [lax.ppermute(value, 'c', sibling) for value in matrices]]
    ppermute x3, waiting for transfers between devices: 0.01 us -> 3.46 us  [shards(): others = [lax.ppermute(value, 'c', sibling) for value in matrices]]
    pallas_call x6, Pallas kernels: 8.18 us -> 11.1 us  [call(): pl.pallas_call(kernel, out_shape=outs, in_specs=[pl.BlockSpec(memory_spac...]
    ppermute x1 -> x0, starting transfers between devices: 2.26 us -> none  [shards(): lax.ppermute(scale, 'c', sibling)]
    all_to_all x2, blocking collectives: 21.6 us -> 20.6 us  [exchange(): lax.all_to_all(message, 'y', split_axis=0, concat_axis=0, axis_index_grou...]
  transfers between devices with their start and end apart: 5 -> 4, of which waited for: 0 -> 1; matrix products, arithmetic and copies ran while one was open for 1% -> 0% of each run, Pallas kernels for 2% -> 1%
where the time goes in v5:
time: 94.7 us; the launch traced here: 94.1 us
  blocking collectives  47.6 us (50%)
  starting transfers between devices  31.8 us (34%)
  Pallas kernels  11.1 us (12%)
  waiting for transfers between devices  3.46 us (4%)
    all_to_all x1, blocking collectives, move(): lax.all_to_all(value, ('rep', 'c'), split_axis=0, concat_axis=0, axis_ind...  27 us
    all_to_all x1, starting transfers between devices, move(): lax.all_to_all(value, ('rep', 'c'), split_axis=0, concat_axis=0, axis_ind...  25.2 us
    all_to_all x2, blocking collectives, exchange(): lax.all_to_all(message, 'y', split_axis=0, concat_axis=0, axis_index_grou...  20.6 us
    pallas_call x6, Pallas kernels, call(): pl.pallas_call(kernel, out_shape=outs, in_specs=[pl.BlockSpec(memory_spac...  11.1 us
    ppermute x3, starting transfers between devices, shards(): others = [lax.ppermute(value, 'c', sibling) for value in matrices]  6.61 us
    ppermute x3, waiting for transfers between devices, shards(): others = [lax.ppermute(value, 'c', sibling) for value in matrices]  3.46 us
  transfers between devices with their start and end apart: 4, of which 1 were waited for; matrix products, arithmetic and copies ran while one was open for 0% of the time, Pallas kernels for 1%

profile of v5, /device:TPU:1, one launch (start us, length us, event | category | flops | bytes accessed | tf_op | source)
XLA Modules:
  0.0 94.1 jit_solution(17898008130872913628)
XLA Ops:
  0.0 2.2 %shard_map.64 = bf16[512,128]{1,0:T(8,128)(2,1)} custom-call(s32[64,64]{1,0:T(8,128)} %requests_ref.1, bf16[128,384]{1,0:T(8,128)(2,1)} %x_hbm.1, f32[3,128]{1,0:T(4,128)} %bitcast.15), custom_call_target="tpu_custom_call" | custom-call | tf_op jit(solution)/shard_map/pallas_call | solution.py:247
  2.2 25.2 %all-to-all-start = ((bf16[128,4,128]{2,1,0:T(4,128)(2,1)}), bf16[128,4,128]{2,1,0:T(4,128)(2,1)}, u32[]{:S(2)}, u32[]{:S(2)}) async-start(bf16[128,4,128]{2,1,0:T(4,128)(2,1)} %bitcast.1), calls=%async_computation | async-start | bytes 262144 | tf_op jit(solution)/shard_map/all_to_all | solution.py:285
  27.4 2.3 %collective-permute-start = (bf16[256,384]{1,0:T(8,128)(2,1)}, bf16[256,384]{1,0:T(8,128)(2,1)}, u32[]{:S(2)}, u32[]{:S(2)}) collective-permute-start(bf16[256,384]{1,0:T(8,128)(2,1)} %bitcast.11), channel_id=1, source_target_pairs={{0,1},{1,0},{2,3},{3,2},{4,5},{5,4},{6,7},{7,6},{8,9},{9,8},{10,11... | collective-permute-start | bytes 589832 | tf_op jit(solution)/shard_map/ppermute | solution.py:300
  29.7 2.1 %collective-permute-start.1 = (bf16[256,384]{1,0:T(8,128)(2,1)}, bf16[256,384]{1,0:T(8,128)(2,1)}, u32[]{:S(2)}, u32[]{:S(2)}) collective-permute-start(bf16[256,384]{1,0:T(8,128)(2,1)} %bitcast.13), channel_id=1, source_target_pairs={{0,1},{1,0},{2,3},{3,2},{4,5},{5,4},{6,7},{7,6},{8,9},{9,8},{10,11... | collective-permute-start | bytes 589832 | tf_op jit(solution)/shard_map/ppermute | solution.py:300
  31.7 2.3 %collective-permute-start.2 = (bf16[384,3072]{1,0:T(8,128)(2,1)}, bf16[384,3072]{1,0:T(8,128)(2,1)}, u32[]{:S(2)}, u32[]{:S(2)}) collective-permute-start(bf16[384,3072]{1,0:T(8,128)(2,1)} %refs_7_.1), channel_id=1, source_target_pairs={{0,1},{1,0},{2,3},{3,2},{4,5},{5,4},{6,7},{7,6},{8,9},{9,8},{10,11... | collective-permute-start | bytes 7077896 | tf_op jit(solution)/shard_map/ppermute | solution.py:300
  34.0 1.0 %shard_map.65.refs_1_.held_ref = s32[64,128]{1,0:T(8,128)S(1)} custom-call(s32[64,64]{1,0:T(8,128)} %requests_ref.1), custom_call_target="tpu_custom_call" | custom-call | flops 199999995904 | tf_op jit(solution)/shard_map/pallas_call | solution.py:247
  35.0 0.0 collective-permute-done.refs_2_
  35.0 0.0 collective-permute-done.1.refs_3_
  35.1 0.0 all-to-all-done
  35.1 3.5 %collective-permute-done.2.refs_4_ = bf16[384,3072]{1,0:T(8,128)(2,1)} collective-permute-done((bf16[384,3072]{1,0:T(8,128)(2,1)}, bf16[384,3072]{1,0:T(8,128)(2,1)}, u32[]{:S(2)}, u32[]{:S(2)}) %collective-permute-start.2) | collective-permute-done | bytes 2359328 | tf_op jit(solution)/shard_map/ppermute | solution.py:300
  38.5 4.9 %shard_map.66 = (bf16[4,64,896]{2,1,0:T(8,128)(2,1)S(1)}, bf16[64,768]{1,0:T(8,128)(2,1)S(1)}, bf16[768,3072]{1,0:T(8,128)(2,1)S(1)}, bf16[256,768]{1,0:T(8,128)...) custom-call(bf16[512,128]{1,0:T(8,128)(2,1)} %bitcast.2.refs_0_, ...), custom_call_target="tpu_custom_call" | custom-call | tf_op jit(solution)/shard_map/pallas_call | solution.py:247
  43.5 11.2 %all_to_all.20.got_ref = bf16[4,64,896]{2,1,0:T(8,128)(2,1)S(1)} all-to-all(bf16[4,64,896]{2,1,0:T(8,128)(2,1)S(1)} %get-tuple-element.14), channel_id=1, replica_groups={{4,6,0,2},{5,7,1,3},{12,14,8,10},{13,15,9,11},{20,22,16,18},{21,23,17,1..., dimensions={0} | all-to-all | bytes 917504 | tf_op jit(solution)/shard_map/all_to_all | solution.py:290
  54.7 1.3 %shard_map.67 = (bf16[4,64,896]{2,1,0:T(8,128)(2,1)S(1)}, bf16[64,768]{1,0:T(8,128)(2,1)S(1)}) custom-call(bf16[64,768]{1,0:T(8,128)(2,1)S(1)} %get-tuple-element.13.wide_ref, bf16[4,64,896]{2,1,0:T(8,128)(2,1)S(1)} %all_to_all.20.got_ref, s32[64,128]{1,0:T(8,128)S(1)} %shard_map.65.refs_1_.held_ref, bf16[768,3072]{1,0:T(8,128)(2,1)S(1)} %get-tuple-element.15.weight, ...), custom_call_target="tpu_custom_call" | custom-call | tf_op jit(solution)/shard_map/pallas_call | solution.py:247
  56.0 0.0 copy-start
  56.0 9.4 %all_to_all.21.got_ref = bf16[4,64,896]{2,1,0:T(8,128)(2,1)S(1)} all-to-all(bf16[4,64,896]{2,1,0:T(8,128)(2,1)S(1)} %get-tuple-element.20), channel_id=1, replica_groups={{4,6,0,2},{5,7,1,3},{12,14,8,10},{13,15,9,11},{20,22,16,18},{21,23,17,1..., dimensions={0} | all-to-all | bytes 917504 | tf_op jit(solution)/shard_map/all_to_all | solution.py:290
  65.4 0.6 shard_map.68
  66.0 0.1 reshape.26
  66.0 27.0 %all_to_all.22 = bf16[128,2,384]{2,1,0:T(2,128)(2,1)S(1)} all-to-all(bf16[128,2,384]{2,1,0:T(2,128)(2,1)S(1)} %reshape.26), channel_id=1, replica_groups={{272,273,280,281,288,289,296,297,304,305,312,313,320,321,328,329,336,33..., dimensions={0} | all-to-all | bytes 393216 | tf_op jit(solution)/shard_map/all_to_all | solution.py:285
  93.0 0.0 copy-done
  93.1 1.1 %shard_map.69 = bf16[2,128,384]{2,1,0:T(8,128)(2,1)} custom-call(s32[64,64]{1,0:T(8,128)S(1)} %copy-done, bf16[128,768]{1,0:T(8,128)(2,1)S(1)} %bitcast.9), custom_call_target="tpu_custom_call" | custom-call | tf_op jit(solution)/shard_map/pallas_call | solution.py:247
  (1 shorter events, 0.0 us)
Async XLA Ops:
  2.2 32.8 %all-to-all-start = ((bf16[128,4,128]{2,1,0:T(4,128)(2,1)}), bf16[128,4,128]{2,1,0:T(4,128)(2,1)}, u32[]{:S(2)}, u32[]{:S(2)}) async-start(bf16[128,4,128]{2,1,0:T(4,128)(2,1)} %bitcast.1), calls=%async_computation | async-start | bytes 262144 | tf_op jit(solution)/shard_map/all_to_all | solution.py:285
  27.4 7.6 %collective-permute-start = (bf16[256,384]{1,0:T(8,128)(2,1)}, bf16[256,384]{1,0:T(8,128)(2,1)}, u32[]{:S(2)}, u32[]{:S(2)}) collective-permute-start(bf16[256,384]{1,0:T(8,128)(2,1)} %bitcast.11), channel_id=1, source_target_pairs={{0,1},{1,0},{2,3},{3,2},{4,5},{5,4},{6,7},{7,6},{8,9},{9,8},{10,11... | collective-permute-start | bytes 589832 | tf_op jit(solution)/shard_map/ppermute | solution.py:300
  29.7 5.4 %collective-permute-start.1 = (bf16[256,384]{1,0:T(8,128)(2,1)}, bf16[256,384]{1,0:T(8,128)(2,1)}, u32[]{:S(2)}, u32[]{:S(2)}) collective-permute-start(bf16[256,384]{1,0:T(8,128)(2,1)} %bitcast.13), channel_id=1, source_target_pairs={{0,1},{1,0},{2,3},{3,2},{4,5},{5,4},{6,7},{7,6},{8,9},{9,8},{10,11... | collective-permute-start | bytes 589832 | tf_op jit(solution)/shard_map/ppermute | solution.py:300
  31.7 6.8 %collective-permute-start.2 = (bf16[384,3072]{1,0:T(8,128)(2,1)}, bf16[384,3072]{1,0:T(8,128)(2,1)}, u32[]{:S(2)}, u32[]{:S(2)}) collective-permute-start(bf16[384,3072]{1,0:T(8,128)(2,1)} %refs_7_.1), channel_id=1, source_target_pairs={{0,1},{1,0},{2,3},{3,2},{4,5},{5,4},{6,7},{7,6},{8,9},{9,8},{10,11... | collective-permute-start | bytes 7077896 | tf_op jit(solution)/shard_map/ppermute | solution.py:300
  56.0 37.0 %copy-start = (s32[64,64]{1,0:T(8,128)S(1)}, s32[64,64]{1,0:T(8,128)}, u32[]{:S(2)}) copy-start(s32[64,64]{1,0:T(8,128)} %requests_ref.1) | copy-start | bytes 49156

commit v6 on v5

v6 whole, which is shorter than its diff:
```python
import functools

import jax
import jax.numpy as jnp
from jax import lax
from jax.experimental import pallas as pl
from jax.experimental.pallas import tpu as pltpu
from jax.sharding import Mesh, PartitionSpec as P

DRAFT = 2
LANES = 128
EPSILON = 1e-06
TURN = 34
TURN_Y = 2
HINT = 2 * 10**11
SLOT = 4

bf16, f32, i32 = jnp.bfloat16, jnp.float32, jnp.int32


def iota(shape, dim):
    return lax.broadcasted_iota(i32, shape, dim)


def over(values, size):
    return values >> (size.bit_length() - 1)


def within(values, size):
    return values & (size - 1)


def mm(left, right):
    return jnp.dot(left, right, preferred_element_type=f32)


def mm_t(left, right):
    return lax.dot_general(left, right, (((1,), (1,)), ((), ())), preferred_element_type=f32)


def t_mm(left, right):
    return lax.dot_general(left, right, (((0,), (0,)), ((), ())), preferred_element_type=f32)


def holder_places(my_requests, kept):
    blocks = my_requests.shape[1]
    return within(over(my_requests, kept) + (blocks - TURN), blocks)


def split(values):
    high = values.astype(bf16).astype(f32)
    middle = (values - high).astype(bf16).astype(f32)
    return high, middle, values - high - middle


def permute_in(kept, requests_hbm, x_hbm, scale_hbm, down_hbm, up_hbm, *refs):
    sent_ref, adapters_hbm, requests_ref, x_ref, scale_ref, sems = refs
    rank_cols = down_hbm.shape[0]
    copies = [
        pltpu.make_async_copy(source, target, sems.at[index])
        for index, (source, target) in enumerate(
            (
                (x_hbm, x_ref),
                (requests_hbm, requests_ref),
                (scale_hbm, scale_ref),
                (down_hbm, adapters_hbm.at[:rank_cols]),
                (up_hbm, adapters_hbm.at[rank_cols:]),
            )
        )
    ]
    for copy in copies:
        copy.start()
    me = lax.axis_index("rep")
    blocks = requests_ref.shape[1]
    rows, width = x_ref.shape
    slots = sent_ref.shape[0]
    parts = width // LANES
    row_picks = [
        (iota((blocks, rows), 1) == 2 * iota((blocks, rows), 0) + half).astype(bf16)
        for half in range(2)
    ]
    index = iota((1, 2 * parts * blocks), 1)
    piece, block = over(index, blocks), within(index, blocks)
    slot = 2 * SLOT * block + jnp.where(piece < parts, piece, SLOT + piece - parts)
    lay_out = (iota((slots, 2 * parts * blocks), 0) == slot).astype(bf16)
    padding = within(iota((slots, 1), 0), SLOT) == parts
    copies[0].wait()
    halves = [mm(pick, x_ref[...]).astype(bf16) for pick in row_picks]
    copies[1].wait()
    places = holder_places(requests_ref[pl.ds(me, 1), :], kept)
    pick = (places == iota((blocks, blocks), 0)).astype(bf16)
    picked = [mm(pick, half).astype(bf16) for half in halves]
    stacked = jnp.concatenate(
        [half[:, part * LANES : (part + 1) * LANES] for half in picked for part in range(parts)]
    )
    copies[2].wait()
    wanted = lax.rem(within(me + (blocks - TURN), blocks), 3 * parts)
    gain = jnp.zeros((1, LANES), f32)
    for part in range(parts):
        for number, value in enumerate(split(scale_ref[part : part + 1, :])):
            gain = jnp.where(wanted == 3 * part + number, value, gain)
    sent_ref[...] = jnp.where(padding, gain, mm(lay_out, stacked)).astype(bf16)
    for copy in copies[3:]:
        copy.wait()


def permute_out(kept, requests_ref, home_ref, out_ref):
    me = lax.axis_index("rep")
    blocks = requests_ref.shape[1]
    rows, width = out_ref.shape[1:]
    repeat = (over(iota((blocks, rows), 1), 2) == iota((blocks, rows), 0)).astype(bf16)
    places = holder_places(requests_ref[pl.ds(me, 1), :], kept)
    places = jnp.broadcast_to(places.astype(f32), (8, blocks)).astype(bf16)
    target = mm(places, repeat)[:1].astype(i32) * 2 + within(iota((1, rows), 1), 2)
    pick = (target == iota((rows, rows), 0)).astype(bf16)
    for step in range(DRAFT):
        out_ref[step] = t_mm(pick, home_ref[:, step * width : (step + 1) * width]).astype(bf16)


def unpack_picks(pick_ref):
    slots = pick_ref.shape[1]
    groups = over(slots, 2 * SLOT)
    parts = SLOT - 1
    row, slot = iota((groups, slots), 0), iota((groups, slots), 1)
    for core in range(2):
        for part in range(parts):
            start = (core * parts + part) * groups
            hit = slot == (2 * row + core) * SLOT + part
            pick_ref[start : start + groups, :] = hit.astype(bf16)
    row, slot = iota((16, slots), 0), iota((1, slots), 1)
    place, core = over(slot, 2 * SLOT), within(over(slot, SLOT), 2)
    part = (place >= 3).astype(i32) + (place >= 6).astype(i32)
    padding = (within(slot, SLOT) == parts) & (place < 3 * parts)
    target = jnp.where(padding, core * parts + part, 16)
    pick_ref[2 * parts * groups :, :] = (row == target).astype(bf16)


def find_held(requests, kept):
    groups = requests.shape[0]
    mine = over(requests, kept) == lax.axis_index("rep")
    held = jnp.sum(jnp.where(mine, within(requests, kept), 0), axis=1, keepdims=True)
    held = jnp.broadcast_to(held.astype(f32), (groups, LANES)).astype(bf16)
    turn = within(iota((groups, groups), 0) + TURN, groups) == iota((groups, groups), 1)
    return mm(turn.astype(bf16), held).astype(i32)


def halves(values, first):
    width = values.shape[1] // 2
    low, high = values[:, :width], values[:, width:]
    return jnp.where(first, low, high), jnp.where(first, high, low)


def products(wide, kept, held, scale, weights, message_ref, arrived=lambda piece: None):
    weight, adapters, other_weight, other_adapters = weights
    count, chip_width = wide.shape
    rank_cols = adapters.shape[0] // 2
    rank = rank_cols // kept
    chips = message_ref.shape[0]
    mine, other = halves((wide * scale).astype(bf16), lax.axis_index("c") == 0)
    squares = jnp.sum(wide * wide, axis=1, keepdims=True)
    top = squares.astype(bf16).astype(f32)
    lane = iota((count, LANES), 1)
    fold = within(iota((rank_cols, LANES), 0), rank) == iota((rank_cols, LANES), 1)
    owned = over(iota((count, rank_cols), 1), rank) == held[:, :1]
    other_ranks = mm_t(other, other_adapters[:rank_cols])
    sums = []
    for place in range(chips):
        chip = within(place + TURN_Y, chips)
        cols = pl.ds(chip * chip_width, chip_width)
        sums.append(mm(other, other_weight[:, cols]))
    for place in range(chips):
        chip = within(place + TURN_Y, chips)
        cols = pl.ds(chip * chip_width, chip_width)
        arrived(chip)
        message_ref[place, :, :chip_width] = (sums[place] + mm(mine, weight[:, cols])).astype(bf16)
    arrived(chips)
    ranks = (other_ranks + mm_t(mine, adapters[:rank_cols])).astype(bf16)
    ranks = jnp.where(owned, ranks, 0).astype(bf16)
    extra = mm(ranks, fold.astype(bf16))
    extra = jnp.where(lane == rank, top, extra)
    extra = jnp.where(lane == rank + 1, squares - top, extra).astype(bf16)
    for place in range(chips):
        message_ref[place, :, chip_width:] = extra


def update(wide, kept, held, got_ref, adapters, other_adapters):
    count, chip_width = wide.shape
    rank_cols = adapters.shape[0] // 2
    rank = rank_cols // kept
    chips = got_ref.shape[0]
    total = got_ref[0].astype(f32)
    for chip in range(1, chips):
        total += got_ref[chip].astype(f32)
    extra = total[:, chip_width:]
    lane = iota((count, LANES), 1)
    is_square = (lane == rank) | (lane == rank + 1)
    mean = jnp.sum(jnp.where(is_square, extra, 0.0), axis=1, keepdims=True) / (chip_width * chips)
    factor = lax.rsqrt(mean + EPSILON)
    ranks = jnp.where(lane < rank, extra * factor, 0.0).astype(bf16)
    unfold = within(iota((LANES, rank_cols), 1), rank) == iota((LANES, rank_cols), 0)
    spread = mm(ranks, unfold.astype(bf16))
    owned = over(iota((count, rank_cols), 1), rank) == held[:, :1]
    spread = jnp.where(owned, spread, 0.0).astype(bf16)
    first = lax.axis_index("c") == 0
    mine, other = mm(spread, adapters[rank_cols:]), mm(spread, other_adapters[rank_cols:])
    delta = [jnp.where(first, mine, other), jnp.where(first, other, mine)]
    delta = jnp.concatenate(delta, axis=1).astype(bf16).astype(f32)
    return (wide + total[:, :chip_width] * factor + delta).astype(bf16)


def first_products(kept, x_ref, pick_ref, other_weight, other_adapters, *refs):
    weight_hbm, adapters_hbm, requests_hbm = refs[:3]
    message_ref, wide_ref, scale_ref, held_ref, weight, adapters, requests_ref, sems = refs[3:]
    groups, chip_width = wide_ref.shape
    chips = message_ref.shape[0]
    copies = []
    for place in range(chips):
        cols = pl.ds(within(place + TURN_Y, chips) * chip_width, chip_width)
        copies.append((weight_hbm.at[:, cols], weight.at[:, cols]))
    copies += [(adapters_hbm, adapters), (requests_hbm, requests_ref)]
    copies = [
        pltpu.make_async_copy(source, target, sems.at[index])
        for index, (source, target) in enumerate(copies)
    ]
    for copy in copies[-1:] + copies[:-1]:
        copy.start()

    def arrived(piece):
        copies[piece if piece == chips else within(piece + chips - TURN_Y, chips)].wait()

    rows = mm(pick_ref[...], x_ref[...])
    parts = 2 * (SLOT - 1)
    wide = jnp.concatenate(
        [rows[index * groups : (index + 1) * groups] for index in range(parts)], axis=1
    )
    start = parts * groups
    scale = jnp.concatenate(
        [rows[start + index : start + index + 1] for index in range(parts)], axis=1
    )
    wide_ref[...] = wide.astype(bf16)
    scale_ref[...] = scale
    copies[-1].wait()
    held = find_held(requests_ref[...], kept)
    held_ref[...] = held
    weights = weight, adapters, other_weight, other_adapters
    products(wide, kept, held, scale, weights, message_ref, arrived)


def next_products(kept, wide_ref, got_ref, held_ref, scale_ref, *refs):
    weights, (message_ref, state_ref) = refs[:4], refs[4:]
    held = held_ref[...]
    state = update(wide_ref[...].astype(f32), kept, held, got_ref, weights[1], weights[3])
    state_ref[...] = state
    products(state.astype(f32), kept, held, scale_ref[...], weights, message_ref)


def last_update(kept, state_ref, got_ref, held_ref, adapters, other_adapters, back_ref):
    rows, cols = back_ref.shape
    width = cols // DRAFT
    old = state_ref[...]
    new = update(old.astype(f32), kept, held_ref[...], got_ref, adapters, other_adapters)
    row, place = iota((rows // 2, rows), 0), iota((rows // 2, rows), 1)
    picks = [(place == 2 * row + core).astype(bf16) for core in range(2)]
    for step, state in enumerate((old, new)):
        back_ref[:, step * width : (step + 1) * width] = sum(
            t_mm(pick, state[:, core * width : (core + 1) * width])
            for core, pick in enumerate(picks)
        ).astype(bf16)


def call(kernel, outs, operands, far=0, **kwargs):
    spaces = [pltpu.VMEM] * (len(operands) - far) + [pltpu.HBM] * far
    return pl.pallas_call(
        kernel,
        out_shape=outs,
        in_specs=[pl.BlockSpec(memory_space=space) for space in spaces],
        out_specs=[
            pl.BlockSpec(memory_space=getattr(out, "memory_space", pltpu.VMEM)) for out in outs
        ],
        compiler_params=pltpu.CompilerParams(vmem_limit_bytes=24 * 2**20),
        **kwargs,
    )(*map(pltpu.with_memory_space_constraint, operands, spaces))


def shards(first_hidden_rows, norm_scale, projection_weight, down_weights, up_weights, requests):
    groups = lax.axis_size("rep")
    chips = lax.axis_size("y")
    cores = lax.axis_size("c")
    rows, width = first_hidden_rows.shape
    chip_width = width * cores
    kept, _, rank = down_weights.shape
    rank_cols = kept * rank

    def resident(shape, dtype=bf16):
        return pltpu.VMEM(shape, dtype)

    down = jnp.transpose(down_weights, (0, 2, 1)).reshape(rank_cols, width)
    up = up_weights.reshape(rank_cols, width)
    sent, adapters = call(
        functools.partial(permute_in, kept),
        [resident((SLOT * rows, LANES)), pltpu.HBM((2 * rank_cols, width), bf16)],
        [requests, first_hidden_rows, norm_scale.reshape(-1, LANES), down, up],
        far=5,
        scratch_shapes=[
            pltpu.VMEM(requests.shape, i32),
            pltpu.VMEM((rows, width), bf16),
            pltpu.VMEM((width // LANES, LANES), f32),
            pltpu.SemaphoreType.DMA((5,)),
        ],
    )
    movers = [[(place + TURN * cores) % rows for place in range(rows)]]
    adders = [[(place + TURN_Y) % chips for place in range(chips)]]

    def move(value):
        return lax.all_to_all(
            value, ("rep", "c"), split_axis=0, concat_axis=0, axis_index_groups=movers, tiled=True
        )

    def exchange(message):
        return lax.all_to_all(
            message, "y", split_axis=0, concat_axis=0, axis_index_groups=adders, tiled=True
        )

    got = move(sent.reshape(rows, SLOT, LANES)).reshape(SLOT * rows, LANES)

    sibling = [(core, cores - 1 - core) for core in range(cores)]
    other_weight, other_adapters = (
        lax.ppermute(value, "c", sibling) for value in (projection_weight, adapters)
    )
    (picks,) = call(
        unpack_picks,
        [resident((2 * (SLOT - 1) * groups + 16, SLOT * rows))],
        [],
        cost_estimate=pl.CostEstimate(flops=HINT, bytes_accessed=0, transcendentals=0),
    )

    message_shape = resident((chips, groups, chip_width + LANES))
    state_shape = resident((groups, chip_width))
    message, wide, scale, held, weight, adapters = call(
        functools.partial(first_products, kept),
        [
            message_shape,
            state_shape,
            resident((1, chip_width), f32),
            resident((groups, LANES), i32),
            resident(projection_weight.shape),
            resident(adapters.shape),
        ],
        [got, picks, other_weight, other_adapters, projection_weight, adapters, requests],
        far=3,
        scratch_shapes=[
            pltpu.VMEM(requests.shape, i32),
            pltpu.SemaphoreType.DMA((chips + 2,)),
        ],
    )
    weights = [weight, adapters, other_weight, other_adapters]
    message, state = call(
        functools.partial(next_products, kept),
        [message_shape, state_shape],
        [wide, exchange(message), held, scale] + weights,
    )
    (back,) = call(
        functools.partial(last_update, kept),
        [resident((rows, DRAFT * width))],
        [state, exchange(message), held, adapters, other_adapters],
    )
    home = move(back.reshape(rows, DRAFT, width)).reshape(rows, DRAFT * width)
    (result,) = call(
        functools.partial(permute_out, kept),
        [jax.ShapeDtypeStruct((DRAFT, rows, width), bf16)],
        [requests, home],
    )
    return result


def solution(mesh):
    chip_mesh = Mesh(mesh.devices.reshape(mesh.shape["rep"], -1, 2), ("rep", "y", "c"))
    tp = ("y", "c")
    return jax.shard_map(
        shards,
        mesh=chip_mesh,
        in_specs=(
            P("rep", tp),
            P(tp),
            P(tp, None),
            P("rep", tp, None),
            P("rep", None, tp),
            P(),
        ),
        out_specs=P(None, "rep", tp),
        check_vma=False,
    )
```

time: 94.7 us -> 108 us (1.14)
  Pallas kernels: 11.1 us -> 25.1 us
  starting transfers between devices: 31.8 us -> 29.5 us
  waiting for transfers between devices: 3.46 us -> 4.6 us
    pallas_call x6, Pallas kernels: 11.1 us -> 25.1 us  [call(): pl.pallas_call(kernel, out_shape=outs, in_specs=[pl.BlockSpec(memory_spac...]
    ppermute x3 -> x2, starting transfers between devices: 6.61 us -> 4.33 us  [shards(): lax.ppermute(value, 'c', sibling)]
    all_to_all x1, waiting for transfers between devices: 0.01 us -> 1.57 us  [move(): lax.all_to_all(value, ('rep', 'c'), split_axis=0, concat_axis=0, axis_ind...]
    all_to_all x2, blocking collectives: 20.6 us -> 21.7 us  [exchange(): lax.all_to_all(message, 'y', split_axis=0, concat_axis=0, axis_index_grou...]
    ppermute x3 -> x2, waiting for transfers between devices: 3.46 us -> 3.03 us  [shards(): lax.ppermute(value, 'c', sibling)]
  transfers between devices with their start and end apart: 4 -> 3, of which waited for: 1 -> 2; matrix products, arithmetic and copies ran while one was open for 0% -> 0% of each run, Pallas kernels for 1% -> 0%
where the time goes in v6:
time: 108 us; the launch traced here: 107 us
  blocking collectives  48.1 us (45%)
  starting transfers between devices  29.5 us (27%)
  Pallas kernels  25.1 us (23%)
  waiting for transfers between devices  4.6 us (4%)
    all_to_all x1, blocking collectives, move(): lax.all_to_all(value, ('rep', 'c'), split_axis=0, concat_axis=0, axis_ind...  26.4 us
    all_to_all x1, starting transfers between devices, move(): lax.all_to_all(value, ('rep', 'c'), split_axis=0, concat_axis=0, axis_ind...  25.2 us
    pallas_call x6, Pallas kernels, call(): pl.pallas_call(kernel, out_shape=outs, in_specs=[pl.BlockSpec(memory_spac...  25.1 us
    all_to_all x2, blocking collectives, exchange(): lax.all_to_all(message, 'y', split_axis=0, concat_axis=0, axis_index_grou...  21.7 us
    ppermute x2, starting transfers between devices, shards(): lax.ppermute(value, 'c', sibling)  4.33 us
    ppermute x2, waiting for transfers between devices, shards(): lax.ppermute(value, 'c', sibling)  3.03 us
  transfers between devices with their start and end apart: 3, of which 2 were waited for; matrix products, arithmetic and copies ran while one was open for 0% of the time, Pallas kernels for 0%

profile of v6, /device:TPU:1, one launch (start us, length us, event | category | flops | bytes accessed | tf_op | source)
XLA Modules:
  0.0 107.4 jit_solution(18107426678321529313)
XLA Ops:
  0.0 13.7 %shard_map.64 = (bf16[512,128]{1,0:T(8,128)(2,1)}, bf16[512,384]{1,0:T(8,128)(2,1)}) custom-call(s32[64,64]{1,0:T(8,128)} %requests_ref.1, bf16[128,384]{1,0:T(8,128)(2,1)} %x_hbm.1, f32[3,128]{1,0:T(4,128)} %bitcast.13, bf16[256,384]{1,0:T(8,128)(2,1)} %bitcast.11, bf16[256,384]{1,0:T(8,128)(2,1)} %bitcast.12), custom_call_target="tpu_custom_call" | custom-call | tf_op jit(solution)/shard_map/pallas_call | solution.py:273
  13.7 25.2 %all-to-all-start = ((bf16[128,4,128]{2,1,0:T(4,128)(2,1)}), bf16[128,4,128]{2,1,0:T(4,128)(2,1)}, u32[]{:S(2)}, u32[]{:S(2)}) async-start(bf16[128,4,128]{2,1,0:T(4,128)(2,1)} %bitcast.4), calls=%async_computation | async-start | bytes 262144 | tf_op jit(solution)/shard_map/all_to_all | solution.py:315
  38.9 2.3 %collective-permute-start.1 = (bf16[512,384]{1,0:T(8,128)(2,1)}, bf16[512,384]{1,0:T(8,128)(2,1)}, u32[]{:S(2)}, u32[]{:S(2)}) collective-permute-start(bf16[512,384]{1,0:T(8,128)(2,1)} %get-tuple-element.16.refs_1_), channel_id=1, source_target_pairs={{0,1},{1,0},{2,3},{3,2},{4,5},{5,4},{6,7},{7,6},{8,9},{9,8},{10,11... | collective-permute-start | bytes 1179656 | tf_op jit(solution)/shard_map/ppermute | solution.py:328
  41.2 2.1 %collective-permute-start = (bf16[384,3072]{1,0:T(8,128)(2,1)}, bf16[384,3072]{1,0:T(8,128)(2,1)}, u32[]{:S(2)}, u32[]{:S(2)}) collective-permute-start(bf16[384,3072]{1,0:T(8,128)(2,1)} %refs_0_.1), channel_id=1, source_target_pairs={{0,1},{1,0},{2,3},{3,2},{4,5},{5,4},{6,7},{7,6},{8,9},{9,8},{10,11... | collective-permute-start | bytes 7077896 | tf_op jit(solution)/shard_map/ppermute | solution.py:328
  43.3 0.1 shard_map.65.pick_ref
  43.3 0.0 collective-permute-done.1.other_adapters.refs_3_
  43.4 1.6 %all-to-all-done = bf16[128,4,128]{2,1,0:T(4,128)(2,1)} async-done(((bf16[128,4,128]{2,1,0:T(4,128)(2,1)}), bf16[128,4,128]{2,1,0:T(4,128)(2,1)}, u32[]{:S(2)}, u32[]{:S(2)}) %all-to-all-start) | async-done | bytes 131104 | tf_op jit(solution)/shard_map/all_to_all | solution.py:315
  44.9 3.0 %collective-permute-done.other_weight.refs_2_ = bf16[384,3072]{1,0:T(8,128)(2,1)} collective-permute-done((bf16[384,3072]{1,0:T(8,128)(2,1)}, bf16[384,3072]{1,0:T(8,128)(2,1)}, u32[]{:S(2)}, u32[]{:S(2)}) %collective-permute-start) | collective-permute-done | bytes 2359328 | tf_op jit(solution)/shard_map/ppermute | solution.py:328
  48.0 5.3 %shard_map.66 = (bf16[4,64,896]{2,1,0:T(8,128)(2,1)S(1)}, bf16[64,768]{1,0:T(8,128)(2,1)S(1)}, f32[1,768]{1,0:T(1,128)S(1)}, s32[64,128]{1,0:T(8,128)S(1)}, bf16...) custom-call(bf16[512,128]{1,0:T(8,128)(2,1)} %bitcast.5.x_ref, bf16[400,512]{1,0:T(8,128)(2,1)S(1)} %shard_map.65.pick_ref, ...), custom_call_target="tpu_custom_call" | custom-call | tf_op jit(solution)/shard_map/pallas_call | solution.py:273
  53.3 11.4 %all_to_all.20.got_ref = bf16[4,64,896]{2,1,0:T(8,128)(2,1)S(1)} all-to-all(bf16[4,64,896]{2,1,0:T(8,128)(2,1)S(1)} %get-tuple-element.18), channel_id=1, replica_groups={{4,6,0,2},{5,7,1,3},{12,14,8,10},{13,15,9,11},{20,22,16,18},{21,23,17,1..., dimensions={0} | all-to-all | bytes 917504 | tf_op jit(solution)/shard_map/all_to_all | solution.py:320
  64.7 3.3 %shard_map.67 = (bf16[4,64,896]{2,1,0:T(8,128)(2,1)S(1)}, bf16[64,768]{1,0:T(8,128)(2,1)S(1)}) custom-call(bf16[64,768]{1,0:T(8,128)(2,1)S(1)} %get-tuple-element.17.wide_ref, bf16[4,64,896]{2,1,0:T(8,128)(2,1)S(1)} %all_to_all.20.got_ref, s32[64,128]{1,0:T(8,128)S(1)} %get-tuple-element.19.held_ref, f32[1,768]{1,0:T(1,128)S(1)} %get-tuple-element.20.scale_ref, ...), custom_call_target="tpu_custom_call" | custom-call | tf_op jit(solution)/shard_map/pallas_call | solution.py:273
  68.1 0.0 copy-start
  68.1 10.2 %all_to_all.21.got_ref = bf16[4,64,896]{2,1,0:T(8,128)(2,1)S(1)} all-to-all(bf16[4,64,896]{2,1,0:T(8,128)(2,1)S(1)} %get-tuple-element.24), channel_id=1, replica_groups={{4,6,0,2},{5,7,1,3},{12,14,8,10},{13,15,9,11},{20,22,16,18},{21,23,17,1..., dimensions={0} | all-to-all | bytes 917504 | tf_op jit(solution)/shard_map/all_to_all | solution.py:320
  78.3 1.6 %shard_map.68 = bf16[128,768]{1,0:T(8,128)(2,1)S(1)} custom-call(bf16[64,768]{1,0:T(8,128)(2,1)S(1)} %get-tuple-element.23.state_ref, bf16[4,64,896]{2,1,0:T(8,128)(2,1)S(1)} %all_to_all.21.got_ref, s32[64,128]{1,0:T(8,128)S(1)} %get-tuple-element.19.held_ref, bf16[512,384]{1,0:T(8,128)(2,1)S(1)} %get-tuple-element.22.refs_1_.adapters, ...), custom_call_target="tpu_custom_call" | custom-call | tf_op jit(solution)/shard_map/pallas_call | solution.py:273
  79.9 0.1 reshape.26
  79.9 26.4 %all_to_all.22 = bf16[128,2,384]{2,1,0:T(2,128)(2,1)S(1)} all-to-all(bf16[128,2,384]{2,1,0:T(2,128)(2,1)S(1)} %reshape.26), channel_id=1, replica_groups={{272,273,280,281,288,289,296,297,304,305,312,313,320,321,328,329,336,33..., dimensions={0} | all-to-all | bytes 393216 | tf_op jit(solution)/shard_map/all_to_all | solution.py:315
  106.4 0.0 copy-done
  106.4 1.1 shard_map.69
  (1 shorter events, 0.0 us)
Async XLA Ops:
  13.7 31.2 %all-to-all-start = ((bf16[128,4,128]{2,1,0:T(4,128)(2,1)}), bf16[128,4,128]{2,1,0:T(4,128)(2,1)}, u32[]{:S(2)}, u32[]{:S(2)}) async-start(bf16[128,4,128]{2,1,0:T(4,128)(2,1)} %bitcast.4), calls=%async_computation | async-start | bytes 262144 | tf_op jit(solution)/shard_map/all_to_all | solution.py:315
  38.9 4.4 %collective-permute-start.1 = (bf16[512,384]{1,0:T(8,128)(2,1)}, bf16[512,384]{1,0:T(8,128)(2,1)}, u32[]{:S(2)}, u32[]{:S(2)}) collective-permute-start(bf16[512,384]{1,0:T(8,128)(2,1)} %get-tuple-element.16.refs_1_), channel_id=1, source_target_pairs={{0,1},{1,0},{2,3},{3,2},{4,5},{5,4},{6,7},{7,6},{8,9},{9,8},{10,11... | collective-permute-start | bytes 1179656 | tf_op jit(solution)/shard_map/ppermute | solution.py:328
  41.2 6.8 %collective-permute-start = (bf16[384,3072]{1,0:T(8,128)(2,1)}, bf16[384,3072]{1,0:T(8,128)(2,1)}, u32[]{:S(2)}, u32[]{:S(2)}) collective-permute-start(bf16[384,3072]{1,0:T(8,128)(2,1)} %refs_0_.1), channel_id=1, source_target_pairs={{0,1},{1,0},{2,3},{3,2},{4,5},{5,4},{6,7},{7,6},{8,9},{9,8},{10,11... | collective-permute-start | bytes 7077896 | tf_op jit(solution)/shard_map/ppermute | solution.py:328
  68.1 38.3 %copy-start = (s32[64,64]{1,0:T(8,128)S(1)}, s32[64,64]{1,0:T(8,128)}, u32[]{:S(2)}) copy-start(s32[64,64]{1,0:T(8,128)} %requests_ref.1) | copy-start | bytes 49156

commit v7 on v6

--- a/solution.py
+++ b/solution.py
@@ -53,19 +53,11 @@
     return high, middle, values - high - middle
 
 
-def permute_in(kept, requests_hbm, x_hbm, scale_hbm, down_hbm, up_hbm, *refs):
-    sent_ref, adapters_hbm, requests_ref, x_ref, scale_ref, sems = refs
-    rank_cols = down_hbm.shape[0]
+def permute_in(kept, requests_hbm, x_hbm, scale_hbm, sent_ref, requests_ref, x_ref, scale_ref, sems):
     copies = [
         pltpu.make_async_copy(source, target, sems.at[index])
         for index, (source, target) in enumerate(
-            (
-                (x_hbm, x_ref),
-                (requests_hbm, requests_ref),
-                (scale_hbm, scale_ref),
-                (down_hbm, adapters_hbm.at[:rank_cols]),
-                (up_hbm, adapters_hbm.at[rank_cols:]),
-            )
+            ((x_hbm, x_ref), (requests_hbm, requests_ref), (scale_hbm, scale_ref))
         )
     ]
     for copy in copies:
@@ -100,8 +92,6 @@
         for number, value in enumerate(split(scale_ref[part : part + 1, :])):
             gain = jnp.where(wanted == 3 * part + number, value, gain)
     sent_ref[...] = jnp.where(padding, gain, mm(lay_out, stacked)).astype(bf16)
-    for copy in copies[3:]:
-        copy.wait()
 
 
 def permute_out(kept, requests_ref, home_ref, out_ref):
@@ -135,6 +125,18 @@
     pick_ref[2 * parts * groups :, :] = (row == target).astype(bf16)
 
 
+def pack(after_ref, down_hbm, up_hbm, out_ref, sems):
+    rank_cols = down_hbm.shape[0]
+    copies = [
+        pltpu.make_async_copy(down_hbm, out_ref.at[:rank_cols], sems.at[0]),
+        pltpu.make_async_copy(up_hbm, out_ref.at[rank_cols:], sems.at[1]),
+    ]
+    for copy in copies:
+        copy.start()
+    for copy in copies:
+        copy.wait()
+
+
 def find_held(requests, kept):
     groups = requests.shape[0]
     mine = over(requests, kept) == lax.axis_index("rep")
@@ -144,46 +146,33 @@
     return mm(turn.astype(bf16), held).astype(i32)
 
 
-def halves(values, first):
-    width = values.shape[1] // 2
-    low, high = values[:, :width], values[:, width:]
-    return jnp.where(first, low, high), jnp.where(first, high, low)
-
-
-def products(wide, kept, held, scale, weights, message_ref, arrived=lambda piece: None):
-    weight, adapters, other_weight, other_adapters = weights
+def products(wide, kept, held, scale, weight, adapters, message_ref, arrived=lambda piece: None):
     count, chip_width = wide.shape
     rank_cols = adapters.shape[0] // 2
     rank = rank_cols // kept
     chips = message_ref.shape[0]
-    mine, other = halves((wide * scale).astype(bf16), lax.axis_index("c") == 0)
+    scaled = (wide * scale).astype(bf16)
     squares = jnp.sum(wide * wide, axis=1, keepdims=True)
     top = squares.astype(bf16).astype(f32)
     lane = iota((count, LANES), 1)
     fold = within(iota((rank_cols, LANES), 0), rank) == iota((rank_cols, LANES), 1)
     owned = over(iota((count, rank_cols), 1), rank) == held[:, :1]
-    other_ranks = mm_t(other, other_adapters[:rank_cols])
-    sums = []
-    for place in range(chips):
-        chip = within(place + TURN_Y, chips)
-        cols = pl.ds(chip * chip_width, chip_width)
-        sums.append(mm(other, other_weight[:, cols]))
-    for place in range(chips):
-        chip = within(place + TURN_Y, chips)
-        cols = pl.ds(chip * chip_width, chip_width)
-        arrived(chip)
-        message_ref[place, :, :chip_width] = (sums[place] + mm(mine, weight[:, cols])).astype(bf16)
-    arrived(chips)
-    ranks = (other_ranks + mm_t(mine, adapters[:rank_cols])).astype(bf16)
+    arrived(0)
+    ranks = mm_t(scaled, adapters[:rank_cols]).astype(bf16)
     ranks = jnp.where(owned, ranks, 0).astype(bf16)
     extra = mm(ranks, fold.astype(bf16))
     extra = jnp.where(lane == rank, top, extra)
     extra = jnp.where(lane == rank + 1, squares - top, extra).astype(bf16)
     for place in range(chips):
+        arrived(1 + place)
+        chip = within(place + TURN_Y, chips)
+        message_ref[place, :, :chip_width] = mm(
+            scaled, weight[:, chip * chip_width : (chip + 1) * chip_width]
+        ).astype(bf16)
         message_ref[place, :, chip_width:] = extra
 
 
-def update(wide, kept, held, got_ref, adapters, other_adapters):
+def update(wide, kept, held, got_ref, adapters):
     count, chip_width = wide.shape
     rank_cols = adapters.shape[0] // 2
     rank = rank_cols // kept
@@ -201,32 +190,44 @@
     spread = mm(ranks, unfold.astype(bf16))
     owned = over(iota((count, rank_cols), 1), rank) == held[:, :1]
     spread = jnp.where(owned, spread, 0.0).astype(bf16)
-    first = lax.axis_index("c") == 0
-    mine, other = mm(spread, adapters[rank_cols:]), mm(spread, other_adapters[rank_cols:])
-    delta = [jnp.where(first, mine, other), jnp.where(first, other, mine)]
-    delta = jnp.concatenate(delta, axis=1).astype(bf16).astype(f32)
+    delta = mm(spread, adapters[rank_cols:]).astype(bf16).astype(f32)
     return (wide + total[:, :chip_width] * factor + delta).astype(bf16)
 
 
-def first_products(kept, x_ref, pick_ref, other_weight, other_adapters, *refs):
-    weight_hbm, adapters_hbm, requests_hbm = refs[:3]
-    message_ref, wide_ref, scale_ref, held_ref, weight, adapters, requests_ref, sems = refs[3:]
+def first_products(kept, x_ref, pick_ref, *refs):
+    weights, (down, others, up, requests_hbm) = refs[:2], refs[2:6]
+    message_ref, wide_ref, scale_ref, held_ref, weight_out, adapters_out, requests_ref, sems = refs[6:]
     groups, chip_width = wide_ref.shape
+    width = chip_width // 2
+    rank_cols = adapters_out.shape[0] // 2
     chips = message_ref.shape[0]
-    copies = []
+    core = lax.axis_index("c")
+    places = [
+        pl.ds(pl.multiple_of(jnp.where(core == index, 0, width), LANES), width)
+        for index in range(2)
+    ]
+    pieces = [[] for _ in range(chips + 3)]
+
+    def add(piece, source, target):
+        copy = pltpu.make_async_copy(source, target, sems.at[sum(map(len, pieces))])
+        copy.start()
+        pieces[piece].append(copy)
+
+    def arrived(piece):
+        for copy in pieces[piece]:
+            copy.wait()
+
+    add(chips + 2, requests_hbm, requests_ref)
+    for index in range(2):
+        source = (down, others.at[:rank_cols])[index]
+        add(0, source, adapters_out.at[:rank_cols, places[index]])
     for place in range(chips):
         cols = pl.ds(within(place + TURN_Y, chips) * chip_width, chip_width)
-        copies.append((weight_hbm.at[:, cols], weight.at[:, cols]))
-    copies += [(adapters_hbm, adapters), (requests_hbm, requests_ref)]
-    copies = [
-        pltpu.make_async_copy(source, target, sems.at[index])
-        for index, (source, target) in enumerate(copies)
-    ]
-    for copy in copies[-1:] + copies[:-1]:
-        copy.start()
-
-    def arrived(piece):
-        copies[piece if piece == chips else within(piece + chips - TURN_Y, chips)].wait()
+        for index in range(2):
+            add(1 + place, weights[index].at[:, cols], weight_out.at[places[index], cols])
+    for index in range(2):
+        source = (up, others.at[rank_cols:])[index]
+        add(chips + 1, source, adapters_out.at[rank_cols:, places[index]])
 
     rows = mm(pick_ref[...], x_ref[...])
     parts = 2 * (SLOT - 1)
@@ -239,26 +240,25 @@
     )
     wide_ref[...] = wide.astype(bf16)
     scale_ref[...] = scale
-    copies[-1].wait()
+    arrived(chips + 2)
     held = find_held(requests_ref[...], kept)
     held_ref[...] = held
-    weights = weight, adapters, other_weight, other_adapters
-    products(wide, kept, held, scale, weights, message_ref, arrived)
-
-
-def next_products(kept, wide_ref, got_ref, held_ref, scale_ref, *refs):
-    weights, (message_ref, state_ref) = refs[:4], refs[4:]
+    products(wide, kept, held, scale, weight_out, adapters_out, message_ref, arrived)
+    arrived(chips + 1)
+
+
+def next_products(kept, wide_ref, got_ref, held_ref, scale_ref, weight, adapters, message_ref, state_ref):
     held = held_ref[...]
-    state = update(wide_ref[...].astype(f32), kept, held, got_ref, weights[1], weights[3])
+    state = update(wide_ref[...].astype(f32), kept, held, got_ref, adapters)
     state_ref[...] = state
-    products(state.astype(f32), kept, held, scale_ref[...], weights, message_ref)
-
-
-def last_update(kept, state_ref, got_ref, held_ref, adapters, other_adapters, back_ref):
+    products(state.astype(f32), kept, held, scale_ref[...], weight, adapters, message_ref)
+
+
+def last_update(kept, state_ref, got_ref, held_ref, adapters, back_ref):
     rows, cols = back_ref.shape
     width = cols // DRAFT
     old = state_ref[...]
-    new = update(old.astype(f32), kept, held_ref[...], got_ref, adapters, other_adapters)
+    new = update(old.astype(f32), kept, held_ref[...], got_ref, adapters)
     row, place = iota((rows // 2, rows), 0), iota((rows // 2, rows), 1)
     picks = [(place == 2 * row + core).astype(bf16) for core in range(2)]
     for step, state in enumerate((old, new)):
@@ -268,8 +268,10 @@
         ).astype(bf16)
 
 
-def call(kernel, outs, operands, far=0, **kwargs):
+def call(kernel, outs, operands, far=0, loose=(), **kwargs):
     spaces = [pltpu.VMEM] * (len(operands) - far) + [pltpu.HBM] * far
+    for index in loose:
+        spaces[index] = pl.ANY
     return pl.pallas_call(
         kernel,
         out_shape=outs,
@@ -294,18 +296,16 @@
     def resident(shape, dtype=bf16):
         return pltpu.VMEM(shape, dtype)
 
-    down = jnp.transpose(down_weights, (0, 2, 1)).reshape(rank_cols, width)
-    up = up_weights.reshape(rank_cols, width)
-    sent, adapters = call(
+    (sent,) = call(
         functools.partial(permute_in, kept),
-        [resident((SLOT * rows, LANES)), pltpu.HBM((2 * rank_cols, width), bf16)],
-        [requests, first_hidden_rows, norm_scale.reshape(-1, LANES), down, up],
-        far=5,
+        [resident((SLOT * rows, LANES))],
+        [requests, first_hidden_rows, norm_scale.reshape(-1, LANES)],
+        far=3,
         scratch_shapes=[
             pltpu.VMEM(requests.shape, i32),
             pltpu.VMEM((rows, width), bf16),
             pltpu.VMEM((width // LANES, LANES), f32),
-            pltpu.SemaphoreType.DMA((5,)),
+            pltpu.SemaphoreType.DMA((3,)),
         ],
     )
     movers = [[(place + TURN * cores) % rows for place in range(rows)]]
@@ -323,15 +323,24 @@
 
     got = move(sent.reshape(rows, SLOT, LANES)).reshape(SLOT * rows, LANES)
 
-    sibling = [(core, cores - 1 - core) for core in range(cores)]
-    other_weight, other_adapters = (
-        lax.ppermute(value, "c", sibling) for value in (projection_weight, adapters)
-    )
     (picks,) = call(
         unpack_picks,
         [resident((2 * (SLOT - 1) * groups + 16, SLOT * rows))],
         [],
         cost_estimate=pl.CostEstimate(flops=HINT, bytes_accessed=0, transcendentals=0),
+    )
+    down = jnp.transpose(down_weights, (0, 2, 1)).reshape(rank_cols, width)
+    up = up_weights.reshape(rank_cols, width)
+    (adapters,) = call(
+        pack,
+        [resident((2 * rank_cols, width))],
+        [picks, down, up],
+        far=2,
+        scratch_shapes=[pltpu.SemaphoreType.DMA((2,))],
+    )
+    sibling = [(core, cores - 1 - core) for core in range(cores)]
+    other_weight, other_adapters = (
+        lax.ppermute(value, "c", sibling) for value in (projection_weight, adapters)
     )
 
     message_shape = resident((chips, groups, chip_width + LANES))
@@ -343,26 +352,26 @@
             state_shape,
             resident((1, chip_width), f32),
             resident((groups, LANES), i32),
-            resident(projection_weight.shape),
-            resident(adapters.shape),
+            resident((chip_width, projection_weight.shape[1])),
+            resident((2 * rank_cols, chip_width)),
         ],
-        [got, picks, other_weight, other_adapters, projection_weight, adapters, requests],
-        far=3,
+        [got, picks, projection_weight, other_weight, down, other_adapters, up, requests],
+        far=6,
+        loose=(3, 5),
         scratch_shapes=[
             pltpu.VMEM(requests.shape, i32),
-            pltpu.SemaphoreType.DMA((chips + 2,)),
+            pltpu.SemaphoreType.DMA((2 * chips + 5,)),
         ],
     )
-    weights = [weight, adapters, other_weight, other_adapters]
     message, state = call(
         functools.partial(next_products, kept),
         [message_shape, state_shape],
-        [wide, exchange(message), held, scale] + weights,
+        [wide, exchange(message), held, scale, weight, adapters],
     )
     (back,) = call(
         functools.partial(last_update, kept),
         [resident((rows, DRAFT * width))],
-        [state, exchange(message), held, adapters, other_adapters],
+        [state, exchange(message), held, adapters],
     )
     home = move(back.reshape(rows, DRAFT, width)).reshape(rows, DRAFT * width)
     (result,) = call(

time: 108 us -> 89.6 us (0.83)
  Pallas kernels: 25.1 us -> 10.3 us
  waiting for transfers between devices: 4.6 us -> 1.56 us
    pallas_call x6 -> x7, Pallas kernels: 25.1 us -> 10.3 us  [call(): pl.pallas_call(kernel, out_shape=outs, in_specs=[pl.BlockSpec(memory_spac...]
    all_to_all x1, waiting for transfers between devices: 1.57 us -> 0.01 us  [move(): lax.all_to_all(value, ('rep', 'c'), split_axis=0, concat_axis=0, axis_ind...]
    ppermute x2, waiting for transfers between devices: 3.03 us -> 1.55 us  [shards(): lax.ppermute(value, 'c', sibling)]
  transfers between devices with their start and end apart: 3 -> 3, of which waited for: 2 -> 1; matrix products, arithmetic and copies ran while one was open for 0% -> 0% of each run, Pallas kernels for 0% -> 1%
where the time goes in v7:
time: 89.6 us; the launch traced here: 89.2 us
  blocking collectives  47.6 us (53%)
  starting transfers between devices  29.5 us (33%)
  Pallas kernels  10.3 us (11%)
  waiting for transfers between devices  1.56 us (2%)
    all_to_all x1, blocking collectives, move(): lax.all_to_all(value, ('rep', 'c'), split_axis=0, concat_axis=0, axis_ind...  27 us
    all_to_all x1, starting transfers between devices, move(): lax.all_to_all(value, ('rep', 'c'), split_axis=0, concat_axis=0, axis_ind...  25.2 us
    all_to_all x2, blocking collectives, exchange(): lax.all_to_all(message, 'y', split_axis=0, concat_axis=0, axis_index_grou...  20.6 us
    pallas_call x7, Pallas kernels, call(): pl.pallas_call(kernel, out_shape=outs, in_specs=[pl.BlockSpec(memory_spac...  10.3 us
    ppermute x2, starting transfers between devices, shards(): lax.ppermute(value, 'c', sibling)  4.33 us
  transfers between devices with their start and end apart: 3, of which 1 were waited for; matrix products, arithmetic and copies ran while one was open for 0% of the time, Pallas kernels for 1%

profile of v7, /device:TPU:1, one launch (start us, length us, event | category | flops | bytes accessed | tf_op | source)
XLA Modules:
  0.0 89.2 jit_solution(12999062819934787227)
XLA Ops:
  0.0 2.2 %shard_map.64 = bf16[512,128]{1,0:T(8,128)(2,1)} custom-call(s32[64,64]{1,0:T(8,128)} %requests_ref.1, bf16[128,384]{1,0:T(8,128)(2,1)} %x_hbm.1, f32[3,128]{1,0:T(4,128)} %bitcast.15), custom_call_target="tpu_custom_call" | custom-call | tf_op jit(solution)/shard_map/pallas_call | solution.py:275
  2.2 25.2 %all-to-all-start = ((bf16[128,4,128]{2,1,0:T(4,128)(2,1)}), bf16[128,4,128]{2,1,0:T(4,128)(2,1)}, u32[]{:S(2)}, u32[]{:S(2)}) async-start(bf16[128,4,128]{2,1,0:T(4,128)(2,1)} %bitcast.1), calls=%async_computation | async-start | bytes 262144 | tf_op jit(solution)/shard_map/all_to_all | solution.py:315
  27.3 2.3 %collective-permute-start = (bf16[384,3072]{1,0:T(8,128)(2,1)}, bf16[384,3072]{1,0:T(8,128)(2,1)}, u32[]{:S(2)}, u32[]{:S(2)}) collective-permute-start(bf16[384,3072]{1,0:T(8,128)(2,1)} %refs_0_.1), channel_id=1, source_target_pairs={{0,1},{1,0},{2,3},{3,2},{4,5},{5,4},{6,7},{7,6},{8,9},{9,8},{10,11... | collective-permute-start | bytes 7077896 | tf_op jit(solution)/shard_map/ppermute | solution.py:343
  29.6 0.1 shard_map.65.after_ref.pick_ref
  29.7 1.0 %shard_map.66 = bf16[512,384]{1,0:T(8,128)(2,1)S(1)} custom-call(bf16[400,512]{1,0:T(8,128)(2,1)S(1)} %shard_map.65.after_ref.pick_ref, bf16[256,384]{1,0:T(8,128)(2,1)} %bitcast.10, bf16[256,384]{1,0:T(8,128)(2,1)} %bitcast.12), custom_call_target="tpu_custom_call" | custom-call | tf_op jit(solution)/shard_map/pallas_call | solution.py:275
  30.8 2.1 %collective-permute-start.1 = (bf16[512,384]{1,0:T(8,128)(2,1)S(1)}, bf16[512,384]{1,0:T(8,128)(2,1)S(1)}, u32[]{:S(2)}, u32[]{:S(2)}) collective-permute-start(bf16[512,384]{1,0:T(8,128)(2,1)S(1)} %shard_map.66), channel_id=1, source_target_pairs={{0,1},{1,0},{2,3},{3,2},{4,5},{5,4},{6,7},{7,6},{8,9},{9,8},{10,11... | collective-permute-start | bytes 1179656 | tf_op jit(solution)/shard_map/ppermute | solution.py:343
  32.8 1.6 %collective-permute-done.1.refs_3_ = bf16[512,384]{1,0:T(8,128)(2,1)S(1)} collective-permute-done((bf16[512,384]{1,0:T(8,128)(2,1)S(1)}, bf16[512,384]{1,0:T(8,128)(2,1)S(1)}, u32[]{:S(2)}, u32[]{:S(2)}) %collective-permute-start.1) | collective-permute-done | bytes 393248 | tf_op jit(solution)/shard_map/ppermute | solution.py:343
  34.4 0.0 all-to-all-done
  34.4 0.0 collective-permute-done.refs_1_
  34.4 4.0 %shard_map.67 = (bf16[4,64,896]{2,1,0:T(8,128)(2,1)S(1)}, bf16[64,768]{1,0:T(8,128)(2,1)S(1)}, f32[1,768]{1,0:T(1,128)S(1)}, s32[64,128]{1,0:T(8,128)S(1)}, bf16...) custom-call(bf16[512,128]{1,0:T(8,128)(2,1)} %bitcast.2.x_ref, ...), custom_call_target="tpu_custom_call" | custom-call | tf_op jit(solution)/shard_map/pallas_call | solution.py:275
  38.5 11.3 %all_to_all.20.got_ref = bf16[4,64,896]{2,1,0:T(8,128)(2,1)S(1)} all-to-all(bf16[4,64,896]{2,1,0:T(8,128)(2,1)S(1)} %get-tuple-element.14), channel_id=1, replica_groups={{4,6,0,2},{5,7,1,3},{12,14,8,10},{13,15,9,11},{20,22,16,18},{21,23,17,1..., dimensions={0} | all-to-all | bytes 917504 | tf_op jit(solution)/shard_map/all_to_all | solution.py:320
  49.8 1.3 %shard_map.68 = (bf16[4,64,896]{2,1,0:T(8,128)(2,1)S(1)}, bf16[64,768]{1,0:T(8,128)(2,1)S(1)}) custom-call(bf16[64,768]{1,0:T(8,128)(2,1)S(1)} %get-tuple-element.13.wide_ref, bf16[4,64,896]{2,1,0:T(8,128)(2,1)S(1)} %all_to_all.20.got_ref, s32[64,128]{1,0:T(8,128)S(1)} %get-tuple-element.15.held_ref, f32[1,768]{1,0:T(1,128)S(1)} %get-tuple-element.16.scale_ref, ...), custom_call_target="tpu_custom_call" | custom-call | tf_op jit(solution)/shard_map/pallas_call | solution.py:275
  51.1 0.0 copy-start
  51.2 9.2 %all_to_all.21.got_ref = bf16[4,64,896]{2,1,0:T(8,128)(2,1)S(1)} all-to-all(bf16[4,64,896]{2,1,0:T(8,128)(2,1)S(1)} %get-tuple-element.20), channel_id=1, replica_groups={{4,6,0,2},{5,7,1,3},{12,14,8,10},{13,15,9,11},{20,22,16,18},{21,23,17,1..., dimensions={0} | all-to-all | bytes 917504 | tf_op jit(solution)/shard_map/all_to_all | solution.py:320
  60.4 0.6 shard_map.69
  61.0 0.1 reshape.26
  61.1 27.0 %all_to_all.22 = bf16[128,2,384]{2,1,0:T(2,128)(2,1)S(1)} all-to-all(bf16[128,2,384]{2,1,0:T(2,128)(2,1)S(1)} %reshape.26), channel_id=1, replica_groups={{272,273,280,281,288,289,296,297,304,305,312,313,320,321,328,329,336,33..., dimensions={0} | all-to-all | bytes 393216 | tf_op jit(solution)/shard_map/all_to_all | solution.py:315
  88.1 0.0 copy-done
  88.1 1.1 %shard_map.70 = bf16[2,128,384]{2,1,0:T(8,128)(2,1)} custom-call(s32[64,64]{1,0:T(8,128)S(1)} %copy-done, bf16[128,768]{1,0:T(8,128)(2,1)S(1)} %bitcast.9), custom_call_target="tpu_custom_call" | custom-call | tf_op jit(solution)/shard_map/pallas_call | solution.py:275
  (1 shorter events, 0.0 us)
Async XLA Ops:
  2.2 32.2 %all-to-all-start = ((bf16[128,4,128]{2,1,0:T(4,128)(2,1)}), bf16[128,4,128]{2,1,0:T(4,128)(2,1)}, u32[]{:S(2)}, u32[]{:S(2)}) async-start(bf16[128,4,128]{2,1,0:T(4,128)(2,1)} %bitcast.1), calls=%async_computation | async-start | bytes 262144 | tf_op jit(solution)/shard_map/all_to_all | solution.py:315
  27.3 7.0 %collective-permute-start = (bf16[384,3072]{1,0:T(8,128)(2,1)}, bf16[384,3072]{1,0:T(8,128)(2,1)}, u32[]{:S(2)}, u32[]{:S(2)}) collective-permute-start(bf16[384,3072]{1,0:T(8,128)(2,1)} %refs_0_.1), channel_id=1, source_target_pairs={{0,1},{1,0},{2,3},{3,2},{4,5},{5,4},{6,7},{7,6},{8,9},{9,8},{10,11... | collective-permute-start | bytes 7077896 | tf_op jit(solution)/shard_map/ppermute | solution.py:343
  30.8 3.6 %collective-permute-start.1 = (bf16[512,384]{1,0:T(8,128)(2,1)S(1)}, bf16[512,384]{1,0:T(8,128)(2,1)S(1)}, u32[]{:S(2)}, u32[]{:S(2)}) collective-permute-start(bf16[512,384]{1,0:T(8,128)(2,1)S(1)} %shard_map.66), channel_id=1, source_target_pairs={{0,1},{1,0},{2,3},{3,2},{4,5},{5,4},{6,7},{7,6},{8,9},{9,8},{10,11... | collective-permute-start | bytes 1179656 | tf_op jit(solution)/shard_map/ppermute | solution.py:343
  51.1 37.0 %copy-start = (s32[64,64]{1,0:T(8,128)S(1)}, s32[64,64]{1,0:T(8,128)}, u32[]{:S(2)}) copy-start(s32[64,64]{1,0:T(8,128)} %requests_ref.1) | copy-start | bytes 49156

commit v8 on v7

--- a/solution.py
+++ b/solution.py
@@ -107,25 +107,23 @@
         out_ref[step] = t_mm(pick, home_ref[:, step * width : (step + 1) * width]).astype(bf16)
 
 
-def unpack_picks(pick_ref):
-    slots = pick_ref.shape[1]
-    groups = over(slots, 2 * SLOT)
-    parts = SLOT - 1
+def unpack_picks(groups):
+    slots, parts = 2 * SLOT * groups, SLOT - 1
     row, slot = iota((groups, slots), 0), iota((groups, slots), 1)
-    for core in range(2):
-        for part in range(parts):
-            start = (core * parts + part) * groups
-            hit = slot == (2 * row + core) * SLOT + part
-            pick_ref[start : start + groups, :] = hit.astype(bf16)
+    picks = [
+        (slot == (2 * row + core) * SLOT + part).astype(bf16)
+        for core in range(2)
+        for part in range(parts)
+    ]
     row, slot = iota((16, slots), 0), iota((1, slots), 1)
     place, core = over(slot, 2 * SLOT), within(over(slot, SLOT), 2)
     part = (place >= 3).astype(i32) + (place >= 6).astype(i32)
     padding = (within(slot, SLOT) == parts) & (place < 3 * parts)
-    target = jnp.where(padding, core * parts + part, 16)
-    pick_ref[2 * parts * groups :, :] = (row == target).astype(bf16)
-
-
-def pack(after_ref, down_hbm, up_hbm, out_ref, sems):
+    picks.append((row == jnp.where(padding, core * parts + part, 16)).astype(bf16))
+    return jnp.concatenate(picks)
+
+
+def pack(down_hbm, up_hbm, out_ref, sems):
     rank_cols = down_hbm.shape[0]
     copies = [
         pltpu.make_async_copy(down_hbm, out_ref.at[:rank_cols], sems.at[0]),
@@ -146,7 +144,7 @@
     return mm(turn.astype(bf16), held).astype(i32)
 
 
-def products(wide, kept, held, scale, weight, adapters, message_ref, arrived=lambda piece: None):
+def products(wide, kept, held, scale, weights, adapters, message_ref, arrived=lambda chip: None):
     count, chip_width = wide.shape
     rank_cols = adapters.shape[0] // 2
     rank = rank_cols // kept
@@ -157,17 +155,22 @@
     lane = iota((count, LANES), 1)
     fold = within(iota((rank_cols, LANES), 0), rank) == iota((rank_cols, LANES), 1)
     owned = over(iota((count, rank_cols), 1), rank) == held[:, :1]
-    arrived(0)
     ranks = mm_t(scaled, adapters[:rank_cols]).astype(bf16)
     ranks = jnp.where(owned, ranks, 0).astype(bf16)
     extra = mm(ranks, fold.astype(bf16))
     extra = jnp.where(lane == rank, top, extra)
     extra = jnp.where(lane == rank + 1, squares - top, extra).astype(bf16)
-    for place in range(chips):
-        arrived(1 + place)
-        chip = within(place + TURN_Y, chips)
+    staged, loaded = weights
+    for chip in range(chips):
+        place = within(chip + chips - TURN_Y, chips)
+        start = chip * chip_width
+        weight = staged
+        if start >= staged.shape[1]:
+            start -= staged.shape[1]
+            weight = loaded
+            arrived(start // chip_width)
         message_ref[place, :, :chip_width] = mm(
-            scaled, weight[:, chip * chip_width : (chip + 1) * chip_width]
+            scaled, weight[:, start : start + chip_width]
         ).astype(bf16)
         message_ref[place, :, chip_width:] = extra
 
@@ -194,42 +197,59 @@
     return (wide + total[:, :chip_width] * factor + delta).astype(bf16)
 
 
-def first_products(kept, x_ref, pick_ref, *refs):
-    weights, (down, others, up, requests_hbm) = refs[:2], refs[2:6]
-    message_ref, wide_ref, scale_ref, held_ref, weight_out, adapters_out, requests_ref, sems = refs[6:]
+def stage(kept, weight, other_weight, down, others, up, requests_hbm, *refs):
+    weight_out, adapters_out, held_ref, requests_ref, sems = refs
+    width = adapters_out.shape[1] // 2
+    rank_cols = adapters_out.shape[0] // 2
+    core = lax.axis_index("c")
+    copies = [(requests_hbm, requests_ref)]
+    for index in range(2):
+        place = pl.ds(pl.multiple_of(jnp.where(core == index, 0, width), LANES), width)
+        copies += [
+            ((down, others.at[:rank_cols])[index], adapters_out.at[:rank_cols, place]),
+            ((up, others.at[rank_cols:])[index], adapters_out.at[rank_cols:, place]),
+        ]
+        for chip in range(weight_out.shape[1] // (2 * width)):
+            cols = pl.ds(chip * 2 * width, 2 * width)
+            source = (weight, other_weight)[index]
+            copies.append((source.at[:, cols], weight_out.at[place, cols]))
+    copies = [
+        pltpu.make_async_copy(source, target, sems.at[index])
+        for index, (source, target) in enumerate(copies)
+    ]
+    for copy in copies:
+        copy.start()
+    copies[0].wait()
+    held_ref[...] = find_held(requests_ref[...], kept)
+    for copy in copies[1:]:
+        copy.wait()
+
+
+def first_products(kept, held_ref, staged, adapters, x_hbm, weight, other_weight, *refs):
+    message_ref, wide_ref, scale_ref, loaded, x_ref, sems = refs
     groups, chip_width = wide_ref.shape
     width = chip_width // 2
-    rank_cols = adapters_out.shape[0] // 2
-    chips = message_ref.shape[0]
     core = lax.axis_index("c")
-    places = [
-        pl.ds(pl.multiple_of(jnp.where(core == index, 0, width), LANES), width)
-        for index in range(2)
-    ]
-    pieces = [[] for _ in range(chips + 3)]
-
-    def add(piece, source, target):
-        copy = pltpu.make_async_copy(source, target, sems.at[sum(map(len, pieces))])
-        copy.start()
-        pieces[piece].append(copy)
-
-    def arrived(piece):
-        for copy in pieces[piece]:
+    copies = [pltpu.make_async_copy(x_hbm, x_ref, sems.at[0])]
+    copies[0].start()
+    for chip in range(loaded.shape[1] // chip_width):
+        cols = pl.ds(chip * chip_width, chip_width)
+        source_cols = pl.ds(staged.shape[1] + chip * chip_width, chip_width)
+        for index, source in enumerate((weight, other_weight)):
+            place = pl.ds(pl.multiple_of(jnp.where(core == index, 0, width), LANES), width)
+            copy = pltpu.make_async_copy(
+                source.at[:, source_cols], loaded.at[place, cols], sems.at[len(copies)]
+            )
+            copy.start()
+            copies.append(copy)
+
+    def arrived(chip):
+        for copy in copies[1 + 2 * chip : 3 + 2 * chip]:
             copy.wait()
 
-    add(chips + 2, requests_hbm, requests_ref)
-    for index in range(2):
-        source = (down, others.at[:rank_cols])[index]
-        add(0, source, adapters_out.at[:rank_cols, places[index]])
-    for place in range(chips):
-        cols = pl.ds(within(place + TURN_Y, chips) * chip_width, chip_width)
-        for index in range(2):
-            add(1 + place, weights[index].at[:, cols], weight_out.at[places[index], cols])
-    for index in range(2):
-        source = (up, others.at[rank_cols:])[index]
-        add(chips + 1, source, adapters_out.at[rank_cols:, places[index]])
-
-    rows = mm(pick_ref[...], x_ref[...])
+    picks = unpack_picks(groups)
+    copies[0].wait()
+    rows = mm(picks, x_ref[...])
     parts = 2 * (SLOT - 1)
     wide = jnp.concatenate(
         [rows[index * groups : (index + 1) * groups] for index in range(parts)], axis=1
@@ -240,18 +260,15 @@
     )
     wide_ref[...] = wide.astype(bf16)
     scale_ref[...] = scale
-    arrived(chips + 2)
-    held = find_held(requests_ref[...], kept)
-    held_ref[...] = held
-    products(wide, kept, held, scale, weight_out, adapters_out, message_ref, arrived)
-    arrived(chips + 1)
-
-
-def next_products(kept, wide_ref, got_ref, held_ref, scale_ref, weight, adapters, message_ref, state_ref):
+    products(wide, kept, held_ref[...], scale, (staged, loaded), adapters, message_ref, arrived)
+
+
+def next_products(kept, wide_ref, got_ref, held_ref, scale_ref, staged, loaded, adapters, *refs):
+    message_ref, state_ref = refs
     held = held_ref[...]
     state = update(wide_ref[...].astype(f32), kept, held, got_ref, adapters)
     state_ref[...] = state
-    products(state.astype(f32), kept, held, scale_ref[...], weight, adapters, message_ref)
+    products(state.astype(f32), kept, held, scale_ref[...], (staged, loaded), adapters, message_ref)
 
 
 def last_update(kept, state_ref, got_ref, held_ref, adapters, back_ref):
@@ -323,20 +340,15 @@
 
     got = move(sent.reshape(rows, SLOT, LANES)).reshape(SLOT * rows, LANES)
 
-    (picks,) = call(
-        unpack_picks,
-        [resident((2 * (SLOT - 1) * groups + 16, SLOT * rows))],
-        [],
-        cost_estimate=pl.CostEstimate(flops=HINT, bytes_accessed=0, transcendentals=0),
-    )
     down = jnp.transpose(down_weights, (0, 2, 1)).reshape(rank_cols, width)
     up = up_weights.reshape(rank_cols, width)
     (adapters,) = call(
         pack,
         [resident((2 * rank_cols, width))],
-        [picks, down, up],
+        [down, up],
         far=2,
         scratch_shapes=[pltpu.SemaphoreType.DMA((2,))],
+        cost_estimate=pl.CostEstimate(flops=HINT, bytes_accessed=0, transcendentals=0),
     )
     sibling = [(core, cores - 1 - core) for core in range(cores)]
     other_weight, other_adapters = (
@@ -345,28 +357,27 @@
 
     message_shape = resident((chips, groups, chip_width + LANES))
     state_shape = resident((groups, chip_width))
-    message, wide, scale, held, weight, adapters = call(
+    half = resident((chip_width, projection_weight.shape[1] // 2))
+    staged, adapters, held = call(
+        functools.partial(stage, kept),
+        [half, resident((2 * rank_cols, chip_width)), resident((groups, LANES), i32)],
+        [projection_weight, other_weight, down, other_adapters, up, requests],
+        far=6,
+        loose=(1, 3),
+        scratch_shapes=[pltpu.VMEM(requests.shape, i32), pltpu.SemaphoreType.DMA((chips + 5,))],
+    )
+    message, wide, scale, loaded = call(
         functools.partial(first_products, kept),
-        [
-            message_shape,
-            state_shape,
-            resident((1, chip_width), f32),
-            resident((groups, LANES), i32),
-            resident((chip_width, projection_weight.shape[1])),
-            resident((2 * rank_cols, chip_width)),
-        ],
-        [got, picks, projection_weight, other_weight, down, other_adapters, up, requests],
-        far=6,
+        [message_shape, state_shape, resident((1, chip_width), f32), half],
+        [held, staged, adapters, got, projection_weight, other_weight],
+        far=3,
         loose=(3, 5),
-        scratch_shapes=[
-            pltpu.VMEM(requests.shape, i32),
-            pltpu.SemaphoreType.DMA((2 * chips + 5,)),
-        ],
+        scratch_shapes=[pltpu.VMEM(got.shape, bf16), pltpu.SemaphoreType.DMA((chips + 1,))],
     )
     message, state = call(
         functools.partial(next_products, kept),
         [message_shape, state_shape],
-        [wide, exchange(message), held, scale, weight, adapters],
+        [wide, exchange(message), held, scale, staged, loaded, adapters],
     )
     (back,) = call(
         functools.partial(last_update, kept),

time: 89.6 us -> 90.2 us (level)
  transfers between devices with their start and end apart: 3 -> 3, of which waited for: 1 -> 1; matrix products, arithmetic and copies ran while one was open for 0% -> 0% of each run, Pallas kernels for 1% -> 3%
where the time goes in v8:
time: 90.2 us; the launch traced here: 89.8 us
  blocking collectives  47.6 us (53%)
  starting transfers between devices  29.5 us (33%)
  Pallas kernels  10.9 us (12%)
  waiting for transfers between devices  1.6 us (2%)
    all_to_all x1, blocking collectives, move(): lax.all_to_all(value, ('rep', 'c'), split_axis=0, concat_axis=0, axis_ind...  27 us
    all_to_all x1, starting transfers between devices, move(): lax.all_to_all(value, ('rep', 'c'), split_axis=0, concat_axis=0, axis_ind...  25.2 us
    all_to_all x2, blocking collectives, exchange(): lax.all_to_all(message, 'y', split_axis=0, concat_axis=0, axis_index_grou...  20.6 us
    pallas_call x7, Pallas kernels, call(): pl.pallas_call(kernel, out_shape=outs, in_specs=[pl.BlockSpec(memory_spac...  10.9 us
    ppermute x2, starting transfers between devices, shards(): lax.ppermute(value, 'c', sibling)  4.33 us
  transfers between devices with their start and end apart: 3, of which 1 were waited for; matrix products, arithmetic and copies ran while one was open for 0% of the time, Pallas kernels for 3%

profile of v8, /device:TPU:1, one launch (start us, length us, event | category | flops | bytes accessed | tf_op | source)
XLA Modules:
  0.0 89.8 jit_solution(9302486805175312557)
XLA Ops:
  0.0 2.2 %shard_map.66 = bf16[512,128]{1,0:T(8,128)(2,1)} custom-call(s32[64,64]{1,0:T(8,128)} %requests_ref.1, bf16[128,384]{1,0:T(8,128)(2,1)} %x_hbm.1, f32[3,128]{1,0:T(4,128)} %bitcast.15), custom_call_target="tpu_custom_call" | custom-call | tf_op jit(solution)/shard_map/pallas_call | solution.py:292
  2.2 25.2 %all-to-all-start = ((bf16[128,4,128]{2,1,0:T(4,128)(2,1)}), bf16[128,4,128]{2,1,0:T(4,128)(2,1)}, u32[]{:S(2)}, u32[]{:S(2)}) async-start(bf16[128,4,128]{2,1,0:T(4,128)(2,1)} %bitcast.5), calls=%async_computation | async-start | bytes 262144 | tf_op jit(solution)/shard_map/all_to_all | solution.py:332
  27.3 2.3 %collective-permute-start = (bf16[384,3072]{1,0:T(8,128)(2,1)}, bf16[384,3072]{1,0:T(8,128)(2,1)}, u32[]{:S(2)}, u32[]{:S(2)}) collective-permute-start(bf16[384,3072]{1,0:T(8,128)(2,1)} %weight.3), channel_id=1, source_target_pairs={{0,1},{1,0},{2,3},{3,2},{4,5},{5,4},{6,7},{7,6},{8,9},{9,8},{10,11... | collective-permute-start | bytes 7077896 | tf_op jit(solution)/shard_map/ppermute | solution.py:355
  29.6 1.0 %shard_map.64 = bf16[512,384]{1,0:T(8,128)(2,1)S(1)} custom-call(bf16[256,384]{1,0:T(8,128)(2,1)} %bitcast.11, bf16[256,384]{1,0:T(8,128)(2,1)} %bitcast.13), custom_call_target="tpu_custom_call" | custom-call | flops 199999995904 | tf_op jit(solution)/shard_map/pallas_call | solution.py:292
  30.7 2.1 %collective-permute-start.1 = (bf16[512,384]{1,0:T(8,128)(2,1)S(1)}, bf16[512,384]{1,0:T(8,128)(2,1)S(1)}, u32[]{:S(2)}, u32[]{:S(2)}) collective-permute-start(bf16[512,384]{1,0:T(8,128)(2,1)S(1)} %shard_map.64), channel_id=1, source_target_pairs={{0,1},{1,0},{2,3},{3,2},{4,5},{5,4},{6,7},{7,6},{8,9},{9,8},{10,11... | collective-permute-start | bytes 1179656 | tf_op jit(solution)/shard_map/ppermute | solution.py:355
  32.7 1.6 %collective-permute-done.1.others = bf16[512,384]{1,0:T(8,128)(2,1)S(1)} collective-permute-done((bf16[512,384]{1,0:T(8,128)(2,1)S(1)}, bf16[512,384]{1,0:T(8,128)(2,1)S(1)}, u32[]{:S(2)}, u32[]{:S(2)}) %collective-permute-start.1) | collective-permute-done | bytes 393248 | tf_op jit(solution)/shard_map/ppermute | solution.py:355
  34.3 0.0 collective-permute-done.other_weight
  34.3 1.9 %shard_map.65 = (bf16[768,1536]{1,0:T(8,128)(2,1)S(1)}, bf16[512,768]{1,0:T(8,128)(2,1)S(1)}, s32[64,128]{1,0:T(8,128)S(1)}) custom-call(bf16[384,3072]{1,0:T(8,128)(2,1)} %weight.3, bf16[384,3072]{1,0:T(8,128)(2,1)} %collective-permute-done.other_weight, bf16[256,384]{1,0:T(8,128)(2,1)} %bitcast.12, bf16[512,384]{1,0:T(8,128)(2,1)S(1)} %collective-permute-done.1.others, ...), custom_call_target="tpu_custom_call" | custom-call | tf_op jit(solution)/shard_map/pallas_call | solution.py:292
  36.3 0.0 all-to-all-done
  36.3 2.8 %shard_map.67 = (bf16[4,64,896]{2,1,0:T(8,128)(2,1)S(1)}, bf16[64,768]{1,0:T(8,128)(2,1)S(1)}, f32[1,768]{1,0:T(1,128)S(1)}, bf16[768,1536]{1,0:T(8,128)(2,1)S(1)}) custom-call(s32[64,128]{1,0:T(8,128)S(1)} %get-tuple-element.14.held_ref, bf16[768,1536]{1,0:T(8,128)(2,1)S(1)} %get-tuple-element.15.staged, bf16[512,768]{1,0:T(8,128)(2,1)S(1)} %get-tuple-element.16.adapters, ...), custom_call_target="tpu_custom_call" | custom-call | tf_op jit(solution)/shard_map/pallas_call | solution.py:292
  39.1 11.2 %all_to_all.20.got_ref = bf16[4,64,896]{2,1,0:T(8,128)(2,1)S(1)} all-to-all(bf16[4,64,896]{2,1,0:T(8,128)(2,1)S(1)} %get-tuple-element.18), channel_id=1, replica_groups={{4,6,0,2},{5,7,1,3},{12,14,8,10},{13,15,9,11},{20,22,16,18},{21,23,17,1..., dimensions={0} | all-to-all | bytes 917504 | tf_op jit(solution)/shard_map/all_to_all | solution.py:337
  50.3 1.3 %shard_map.68 = (bf16[4,64,896]{2,1,0:T(8,128)(2,1)S(1)}, bf16[64,768]{1,0:T(8,128)(2,1)S(1)}) custom-call(bf16[64,768]{1,0:T(8,128)(2,1)S(1)} %get-tuple-element.17.wide_ref, bf16[4,64,896]{2,1,0:T(8,128)(2,1)S(1)} %all_to_all.20.got_ref, s32[64,128]{1,0:T(8,128)S(1)} %get-tuple-element.14.held_ref, f32[1,768]{1,0:T(1,128)S(1)} %get-tuple-element.19.scale_ref, ...), custom_call_target="tpu_custom_call" | custom-call | tf_op jit(solution)/shard_map/pallas_call | solution.py:292
  51.7 0.0 copy-start
  51.7 9.4 %all_to_all.21.got_ref = bf16[4,64,896]{2,1,0:T(8,128)(2,1)S(1)} all-to-all(bf16[4,64,896]{2,1,0:T(8,128)(2,1)S(1)} %get-tuple-element.22), channel_id=1, replica_groups={{4,6,0,2},{5,7,1,3},{12,14,8,10},{13,15,9,11},{20,22,16,18},{21,23,17,1..., dimensions={0} | all-to-all | bytes 917504 | tf_op jit(solution)/shard_map/all_to_all | solution.py:337
  61.1 0.6 shard_map.69
  61.6 0.1 reshape.26
  61.7 27.0 %all_to_all.22 = bf16[128,2,384]{2,1,0:T(2,128)(2,1)S(1)} all-to-all(bf16[128,2,384]{2,1,0:T(2,128)(2,1)S(1)} %reshape.26), channel_id=1, replica_groups={{272,273,280,281,288,289,296,297,304,305,312,313,320,321,328,329,336,33..., dimensions={0} | all-to-all | bytes 393216 | tf_op jit(solution)/shard_map/all_to_all | solution.py:332
  88.7 0.0 copy-done
  88.7 1.1 %shard_map.70 = bf16[2,128,384]{2,1,0:T(8,128)(2,1)} custom-call(s32[64,64]{1,0:T(8,128)S(1)} %copy-done, bf16[128,768]{1,0:T(8,128)(2,1)S(1)} %bitcast.9), custom_call_target="tpu_custom_call" | custom-call | tf_op jit(solution)/shard_map/pallas_call | solution.py:292
  (1 shorter events, 0.0 us)
Async XLA Ops:
  2.2 34.1 %all-to-all-start = ((bf16[128,4,128]{2,1,0:T(4,128)(2,1)}), bf16[128,4,128]{2,1,0:T(4,128)(2,1)}, u32[]{:S(2)}, u32[]{:S(2)}) async-start(bf16[128,4,128]{2,1,0:T(4,128)(2,1)} %bitcast.5), calls=%async_computation | async-start | bytes 262144 | tf_op jit(solution)/shard_map/all_to_all | solution.py:332
  27.3 7.0 %collective-permute-start = (bf16[384,3072]{1,0:T(8,128)(2,1)}, bf16[384,3072]{1,0:T(8,128)(2,1)}, u32[]{:S(2)}, u32[]{:S(2)}) collective-permute-start(bf16[384,3072]{1,0:T(8,128)(2,1)} %weight.3), channel_id=1, source_target_pairs={{0,1},{1,0},{2,3},{3,2},{4,5},{5,4},{6,7},{7,6},{8,9},{9,8},{10,11... | collective-permute-start | bytes 7077896 | tf_op jit(solution)/shard_map/ppermute | solution.py:355
  30.7 3.7 %collective-permute-start.1 = (bf16[512,384]{1,0:T(8,128)(2,1)S(1)}, bf16[512,384]{1,0:T(8,128)(2,1)S(1)}, u32[]{:S(2)}, u32[]{:S(2)}) collective-permute-start(bf16[512,384]{1,0:T(8,128)(2,1)S(1)} %shard_map.64), channel_id=1, source_target_pairs={{0,1},{1,0},{2,3},{3,2},{4,5},{5,4},{6,7},{7,6},{8,9},{9,8},{10,11... | collective-permute-start | bytes 1179656 | tf_op jit(solution)/shard_map/ppermute | solution.py:355
  51.7 37.1 %copy-start = (s32[64,64]{1,0:T(8,128)S(1)}, s32[64,64]{1,0:T(8,128)}, u32[]{:S(2)}) copy-start(s32[64,64]{1,0:T(8,128)} %requests_ref.1) | copy-start | bytes 49156

commit v9 on v6

--- a/solution.py
+++ b/solution.py
@@ -12,7 +12,7 @@
 EPSILON = 1e-06
 TURN = 34
 TURN_Y = 2
-HINT = 2 * 10**11
+HINT = 6 * 10**10
 SLOT = 4
 
 bf16, f32, i32 = jnp.bfloat16, jnp.float32, jnp.int32
@@ -54,7 +54,7 @@
 
 
 def permute_in(kept, requests_hbm, x_hbm, scale_hbm, down_hbm, up_hbm, *refs):
-    sent_ref, adapters_hbm, requests_ref, x_ref, scale_ref, sems = refs
+    sent_ref, adapters_ref, requests_ref, x_ref, scale_ref, sems = refs
     rank_cols = down_hbm.shape[0]
     copies = [
         pltpu.make_async_copy(source, target, sems.at[index])
@@ -63,8 +63,8 @@
                 (x_hbm, x_ref),
                 (requests_hbm, requests_ref),
                 (scale_hbm, scale_ref),
-                (down_hbm, adapters_hbm.at[:rank_cols]),
-                (up_hbm, adapters_hbm.at[rank_cols:]),
+                (down_hbm, adapters_ref.at[:rank_cols]),
+                (up_hbm, adapters_ref.at[rank_cols:]),
             )
         )
     ]
@@ -117,22 +117,24 @@
         out_ref[step] = t_mm(pick, home_ref[:, step * width : (step + 1) * width]).astype(bf16)
 
 
-def unpack_picks(pick_ref):
-    slots = pick_ref.shape[1]
-    groups = over(slots, 2 * SLOT)
-    parts = SLOT - 1
+def unpack_picks(groups):
+    slots, parts = 2 * SLOT * groups, SLOT - 1
     row, slot = iota((groups, slots), 0), iota((groups, slots), 1)
-    for core in range(2):
-        for part in range(parts):
-            start = (core * parts + part) * groups
-            hit = slot == (2 * row + core) * SLOT + part
-            pick_ref[start : start + groups, :] = hit.astype(bf16)
+    picks = [
+        (slot == (2 * row + core) * SLOT + part).astype(bf16)
+        for core in range(2)
+        for part in range(parts)
+    ]
     row, slot = iota((16, slots), 0), iota((1, slots), 1)
     place, core = over(slot, 2 * SLOT), within(over(slot, SLOT), 2)
     part = (place >= 3).astype(i32) + (place >= 6).astype(i32)
     padding = (within(slot, SLOT) == parts) & (place < 3 * parts)
-    target = jnp.where(padding, core * parts + part, 16)
-    pick_ref[2 * parts * groups :, :] = (row == target).astype(bf16)
+    picks.append((row == jnp.where(padding, core * parts + part, 16)).astype(bf16))
+    return jnp.concatenate(picks)
+
+
+def pass_on(value_ref, out_ref):
+    out_ref[...] = value_ref[...]
 
 
 def find_held(requests, kept):
@@ -144,46 +146,33 @@
     return mm(turn.astype(bf16), held).astype(i32)
 
 
-def halves(values, first):
-    width = values.shape[1] // 2
-    low, high = values[:, :width], values[:, width:]
-    return jnp.where(first, low, high), jnp.where(first, high, low)
-
-
-def products(wide, kept, held, scale, weights, message_ref, arrived=lambda piece: None):
-    weight, adapters, other_weight, other_adapters = weights
+def products(wide, kept, held, scale, weight, adapters, message_ref, arrived=lambda piece: None):
     count, chip_width = wide.shape
     rank_cols = adapters.shape[0] // 2
     rank = rank_cols // kept
     chips = message_ref.shape[0]
-    mine, other = halves((wide * scale).astype(bf16), lax.axis_index("c") == 0)
+    scaled = (wide * scale).astype(bf16)
     squares = jnp.sum(wide * wide, axis=1, keepdims=True)
     top = squares.astype(bf16).astype(f32)
     lane = iota((count, LANES), 1)
     fold = within(iota((rank_cols, LANES), 0), rank) == iota((rank_cols, LANES), 1)
     owned = over(iota((count, rank_cols), 1), rank) == held[:, :1]
-    other_ranks = mm_t(other, other_adapters[:rank_cols])
-    sums = []
-    for place in range(chips):
-        chip = within(place + TURN_Y, chips)
-        cols = pl.ds(chip * chip_width, chip_width)
-        sums.append(mm(other, other_weight[:, cols]))
-    for place in range(chips):
-        chip = within(place + TURN_Y, chips)
-        cols = pl.ds(chip * chip_width, chip_width)
-        arrived(chip)
-        message_ref[place, :, :chip_width] = (sums[place] + mm(mine, weight[:, cols])).astype(bf16)
     arrived(chips)
-    ranks = (other_ranks + mm_t(mine, adapters[:rank_cols])).astype(bf16)
+    ranks = mm_t(scaled, adapters[:rank_cols]).astype(bf16)
     ranks = jnp.where(owned, ranks, 0).astype(bf16)
     extra = mm(ranks, fold.astype(bf16))
     extra = jnp.where(lane == rank, top, extra)
     extra = jnp.where(lane == rank + 1, squares - top, extra).astype(bf16)
-    for place in range(chips):
+    for chip in range(chips):
+        place = within(chip + chips - TURN_Y, chips)
+        arrived(chip)
+        message_ref[place, :, :chip_width] = mm(
+            scaled, weight[:, chip * chip_width : (chip + 1) * chip_width]
+        ).astype(bf16)
         message_ref[place, :, chip_width:] = extra
 
 
-def update(wide, kept, held, got_ref, adapters, other_adapters):
+def update(wide, kept, held, got_ref, adapters):
     count, chip_width = wide.shape
     rank_cols = adapters.shape[0] // 2
     rank = rank_cols // kept
@@ -201,34 +190,35 @@
     spread = mm(ranks, unfold.astype(bf16))
     owned = over(iota((count, rank_cols), 1), rank) == held[:, :1]
     spread = jnp.where(owned, spread, 0.0).astype(bf16)
+    delta = mm(spread, adapters[rank_cols:]).astype(bf16).astype(f32)
+    return (wide + total[:, :chip_width] * factor + delta).astype(bf16)
+
+
+def first_products(kept, x_ref, other_weight, others, weight, down, up, requests_hbm, *refs):
+    message_ref, wide_ref, scale_ref, held_ref, weight_out, adapters_out = refs[:6]
+    requests_ref, sems = refs[6:]
+    groups, chip_width = wide_ref.shape
+    width = chip_width // 2
+    rank_cols = adapters_out.shape[0] // 2
+    chips = message_ref.shape[0]
     first = lax.axis_index("c") == 0
-    mine, other = mm(spread, adapters[rank_cols:]), mm(spread, other_adapters[rank_cols:])
-    delta = [jnp.where(first, mine, other), jnp.where(first, other, mine)]
-    delta = jnp.concatenate(delta, axis=1).astype(bf16).astype(f32)
-    return (wide + total[:, :chip_width] * factor + delta).astype(bf16)
-
-
-def first_products(kept, x_ref, pick_ref, other_weight, other_adapters, *refs):
-    weight_hbm, adapters_hbm, requests_hbm = refs[:3]
-    message_ref, wide_ref, scale_ref, held_ref, weight, adapters, requests_ref, sems = refs[3:]
-    groups, chip_width = wide_ref.shape
-    chips = message_ref.shape[0]
-    copies = []
-    for place in range(chips):
-        cols = pl.ds(within(place + TURN_Y, chips) * chip_width, chip_width)
-        copies.append((weight_hbm.at[:, cols], weight.at[:, cols]))
-    copies += [(adapters_hbm, adapters), (requests_hbm, requests_ref)]
+    mine = pl.ds(pl.multiple_of(jnp.where(first, 0, width), LANES), width)
+    other = pl.ds(pl.multiple_of(jnp.where(first, width, 0), LANES), width)
+    blocks = [pl.ds(chip * chip_width, chip_width) for chip in range(chips)]
+    copies = [(weight.at[:, cols], weight_out.at[mine, cols]) for cols in blocks]
+    copies += [
+        (down, adapters_out.at[:rank_cols, mine]),
+        (up, adapters_out.at[rank_cols:, mine]),
+        (requests_hbm, requests_ref),
+    ]
     copies = [
         pltpu.make_async_copy(source, target, sems.at[index])
         for index, (source, target) in enumerate(copies)
     ]
-    for copy in copies[-1:] + copies[:-1]:
+    for copy in [copies[-1], copies[chips]] + copies[:chips] + [copies[chips + 1]]:
         copy.start()
 
-    def arrived(piece):
-        copies[piece if piece == chips else within(piece + chips - TURN_Y, chips)].wait()
-
-    rows = mm(pick_ref[...], x_ref[...])
+    rows = mm(unpack_picks(groups), x_ref[...])
     parts = 2 * (SLOT - 1)
     wide = jnp.concatenate(
         [rows[index * groups : (index + 1) * groups] for index in range(parts)], axis=1
@@ -239,26 +229,33 @@
     )
     wide_ref[...] = wide.astype(bf16)
     scale_ref[...] = scale
+    adapters_out[:, other] = others[...]
+    for cols in blocks:
+        weight_out[other, cols] = other_weight[:, cols]
     copies[-1].wait()
     held = find_held(requests_ref[...], kept)
     held_ref[...] = held
-    weights = weight, adapters, other_weight, other_adapters
-    products(wide, kept, held, scale, weights, message_ref, arrived)
-
-
-def next_products(kept, wide_ref, got_ref, held_ref, scale_ref, *refs):
-    weights, (message_ref, state_ref) = refs[:4], refs[4:]
+
+    def arrived(piece):
+        copies[piece].wait()
+
+    products(wide, kept, held, scale, weight_out, adapters_out, message_ref, arrived)
+    copies[chips + 1].wait()
+
+
+def next_products(kept, wide_ref, got_ref, held_ref, scale_ref, weight, adapters, *refs):
+    message_ref, state_ref = refs
     held = held_ref[...]
-    state = update(wide_ref[...].astype(f32), kept, held, got_ref, weights[1], weights[3])
+    state = update(wide_ref[...].astype(f32), kept, held, got_ref, adapters)
     state_ref[...] = state
-    products(state.astype(f32), kept, held, scale_ref[...], weights, message_ref)
-
-
-def last_update(kept, state_ref, got_ref, held_ref, adapters, other_adapters, back_ref):
+    products(state.astype(f32), kept, held, scale_ref[...], weight, adapters, message_ref)
+
+
+def last_update(kept, state_ref, got_ref, held_ref, adapters, back_ref):
     rows, cols = back_ref.shape
     width = cols // DRAFT
     old = state_ref[...]
-    new = update(old.astype(f32), kept, held_ref[...], got_ref, adapters, other_adapters)
+    new = update(old.astype(f32), kept, held_ref[...], got_ref, adapters)
     row, place = iota((rows // 2, rows), 0), iota((rows // 2, rows), 1)
     picks = [(place == 2 * row + core).astype(bf16) for core in range(2)]
     for step, state in enumerate((old, new)):
@@ -298,7 +295,7 @@
     up = up_weights.reshape(rank_cols, width)
     sent, adapters = call(
         functools.partial(permute_in, kept),
-        [resident((SLOT * rows, LANES)), pltpu.HBM((2 * rank_cols, width), bf16)],
+        [resident((SLOT * rows, LANES)), resident((2 * rank_cols, width))],
         [requests, first_hidden_rows, norm_scale.reshape(-1, LANES), down, up],
         far=5,
         scratch_shapes=[
@@ -323,15 +320,15 @@
 
     got = move(sent.reshape(rows, SLOT, LANES)).reshape(SLOT * rows, LANES)
 
+    (adapters,) = call(
+        pass_on,
+        [resident(adapters.shape)],
+        [adapters],
+        cost_estimate=pl.CostEstimate(flops=HINT, bytes_accessed=0, transcendentals=0),
+    )
     sibling = [(core, cores - 1 - core) for core in range(cores)]
     other_weight, other_adapters = (
         lax.ppermute(value, "c", sibling) for value in (projection_weight, adapters)
-    )
-    (picks,) = call(
-        unpack_picks,
-        [resident((2 * (SLOT - 1) * groups + 16, SLOT * rows))],
-        [],
-        cost_estimate=pl.CostEstimate(flops=HINT, bytes_accessed=0, transcendentals=0),
     )
 
     message_shape = resident((chips, groups, chip_width + LANES))
@@ -343,26 +340,25 @@
             state_shape,
             resident((1, chip_width), f32),
             resident((groups, LANES), i32),
-            resident(projection_weight.shape),
-            resident(adapters.shape),
+            resident((chip_width, projection_weight.shape[1])),
+            resident((2 * rank_cols, chip_width)),
         ],
-        [got, picks, other_weight, other_adapters, projection_weight, adapters, requests],
-        far=3,
+        [got, other_weight, other_adapters, projection_weight, down, up, requests],
+        far=4,
         scratch_shapes=[
             pltpu.VMEM(requests.shape, i32),
-            pltpu.SemaphoreType.DMA((chips + 2,)),
+            pltpu.SemaphoreType.DMA((chips + 3,)),
         ],
     )
-    weights = [weight, adapters, other_weight, other_adapters]
     message, state = call(
         functools.partial(next_products, kept),
         [message_shape, state_shape],
-        [wide, exchange(message), held, scale] + weights,
+        [wide, exchange(message), held, scale, weight, adapters],
     )
     (back,) = call(
         functools.partial(last_update, kept),
         [resident((rows, DRAFT * width))],
-        [state, exchange(message), held, adapters, other_adapters],
+        [state, exchange(message), held, adapters],
     )
     home = move(back.reshape(rows, DRAFT, width)).reshape(rows, DRAFT * width)
     (result,) = call(

time: 108 us -> 88.3 us (0.82)
  Pallas kernels: 25.1 us -> 8.29 us
  waiting for transfers between devices: 4.6 us -> 2.61 us
    pallas_call x6, Pallas kernels: 25.1 us -> 8.29 us  [call(): pl.pallas_call(kernel, out_shape=outs, in_specs=[pl.BlockSpec(memory_spac...]
    all_to_all x1, waiting for transfers between devices: 1.57 us -> 0.01 us  [move(): lax.all_to_all(value, ('rep', 'c'), split_axis=0, concat_axis=0, axis_ind...]
    all_to_all x2, blocking collectives: 21.7 us -> 20.6 us  [exchange(): lax.all_to_all(message, 'y', split_axis=0, concat_axis=0, axis_index_grou...]
  transfers between devices with their start and end apart: 3 -> 3, of which waited for: 2 -> 1; matrix products, arithmetic and copies ran while one was open for 0% -> 0% of each run, Pallas kernels for 0% -> 0%
where the time goes in v9:
time: 88.3 us; the launch traced here: 87.9 us
  blocking collectives  47.8 us (54%)
  starting transfers between devices  29 us (33%)
  Pallas kernels  8.29 us (9%)
  waiting for transfers between devices  2.61 us (3%)
    all_to_all x1, blocking collectives, move(): lax.all_to_all(value, ('rep', 'c'), split_axis=0, concat_axis=0, axis_ind...  27.2 us
    all_to_all x1, starting transfers between devices, move(): lax.all_to_all(value, ('rep', 'c'), split_axis=0, concat_axis=0, axis_ind...  24.7 us
    all_to_all x2, blocking collectives, exchange(): lax.all_to_all(message, 'y', split_axis=0, concat_axis=0, axis_index_grou...  20.6 us
    pallas_call x6, Pallas kernels, call(): pl.pallas_call(kernel, out_shape=outs, in_specs=[pl.BlockSpec(memory_spac...  8.29 us
    ppermute x2, starting transfers between devices, shards(): lax.ppermute(value, 'c', sibling)  4.33 us
    ppermute x2, waiting for transfers between devices, shards(): lax.ppermute(value, 'c', sibling)  2.61 us
  transfers between devices with their start and end apart: 3, of which 1 were waited for; matrix products, arithmetic and copies ran while one was open for 0% of the time, Pallas kernels for 0%

profile of v9, /device:TPU:1, one launch (start us, length us, event | category | flops | bytes accessed | tf_op | source)
XLA Modules:
  0.0 87.9 jit_solution(10252681577951172049)
XLA Ops:
  0.0 2.2 %shard_map.64 = (bf16[512,128]{1,0:T(8,128)(2,1)}, bf16[512,384]{1,0:T(8,128)(2,1)S(1)}) custom-call(s32[64,64]{1,0:T(8,128)} %requests_ref.1, bf16[128,384]{1,0:T(8,128)(2,1)} %x_hbm.1, f32[3,128]{1,0:T(4,128)} %bitcast.16, bf16[256,384]{1,0:T(8,128)(2,1)} %bitcast.11, bf16[256,384]{1,0:T(8,128)(2,1)} %bitcast.13), custom_call_target="tpu_custom_call" | custom-call | tf_op jit(solution)/shard_map/pallas_call | solution.py:270
  2.2 24.7 %all-to-all-start = ((bf16[128,4,128]{2,1,0:T(4,128)(2,1)}), bf16[128,4,128]{2,1,0:T(4,128)(2,1)S(1)}, u32[]{:S(2)}, u32[]{:S(2)}) async-start(bf16[128,4,128]{2,1,0:T(4,128)(2,1)} %bitcast.4), calls=%async_computation | async-start | bytes 262144 | tf_op jit(solution)/shard_map/all_to_all | solution.py:312
  26.9 2.3 %collective-permute-start = (bf16[384,3072]{1,0:T(8,128)(2,1)}, bf16[384,3072]{1,0:T(8,128)(2,1)S(1)}, u32[]{:S(2)}, u32[]{:S(2)}) collective-permute-start(bf16[384,3072]{1,0:T(8,128)(2,1)} %weight.1), channel_id=1, source_target_pairs={{0,1},{1,0},{2,3},{3,2},{4,5},{5,4},{6,7},{7,6},{8,9},{9,8},{10,11... | collective-permute-start | bytes 7077896 | tf_op jit(solution)/shard_map/ppermute | solution.py:331
  29.2 2.1 %collective-permute-start.1 = (bf16[512,384]{1,0:T(8,128)(2,1)S(1)}, bf16[512,384]{1,0:T(8,128)(2,1)S(1)}, u32[]{:S(2)}, u32[]{:S(2)}) collective-permute-start(bf16[512,384]{1,0:T(8,128)(2,1)S(1)} %shard_map.65), channel_id=1, source_target_pairs={{0,1},{1,0},{2,3},{3,2},{4,5},{5,4},{6,7},{7,6},{8,9},{9,8},{10,11... | collective-permute-start | bytes 1179656 | tf_op jit(solution)/shard_map/ppermute | solution.py:331
  31.3 2.6 %collective-permute-done.1.others = bf16[512,384]{1,0:T(8,128)(2,1)S(1)} collective-permute-done((bf16[512,384]{1,0:T(8,128)(2,1)S(1)}, bf16[512,384]{1,0:T(8,128)(2,1)S(1)}, u32[]{:S(2)}, u32[]{:S(2)}) %collective-permute-start.1) | collective-permute-done | bytes 393248 | tf_op jit(solution)/shard_map/ppermute | solution.py:331
  33.9 0.0 all-to-all-done
  33.9 0.0 collective-permute-done.other_weight
  33.9 3.1 %shard_map.66 = (bf16[4,64,896]{2,1,0:T(8,128)(2,1)S(1)}, bf16[64,768]{1,0:T(8,128)(2,1)S(1)}, f32[1,768]{1,0:T(1,128)S(1)}, s32[64,128]{1,0:T(8,128)S(1)}, bf16...) custom-call(bf16[512,128]{1,0:T(8,128)(2,1)S(1)} %bitcast.10, ...), custom_call_target="tpu_custom_call" | custom-call | tf_op jit(solution)/shard_map/pallas_call | solution.py:270
  37.0 11.2 %all_to_all.20.got_ref = bf16[4,64,896]{2,1,0:T(8,128)(2,1)S(1)} all-to-all(bf16[4,64,896]{2,1,0:T(8,128)(2,1)S(1)} %get-tuple-element.18), channel_id=1, replica_groups={{4,6,0,2},{5,7,1,3},{12,14,8,10},{13,15,9,11},{20,22,16,18},{21,23,17,1..., dimensions={0} | all-to-all | bytes 917504 | tf_op jit(solution)/shard_map/all_to_all | solution.py:317
  48.2 1.3 %shard_map.67 = (bf16[4,64,896]{2,1,0:T(8,128)(2,1)S(1)}, bf16[64,768]{1,0:T(8,128)(2,1)S(1)}) custom-call(bf16[64,768]{1,0:T(8,128)(2,1)S(1)} %get-tuple-element.17.wide_ref, bf16[4,64,896]{2,1,0:T(8,128)(2,1)S(1)} %all_to_all.20.got_ref, s32[64,128]{1,0:T(8,128)S(1)} %get-tuple-element.19.held_ref, f32[1,768]{1,0:T(1,128)S(1)} %get-tuple-element.20.scale_ref, ...), custom_call_target="tpu_custom_call" | custom-call | tf_op jit(solution)/shard_map/pallas_call | solution.py:270
  49.6 0.0 copy-start
  49.6 9.4 %all_to_all.21.got_ref = bf16[4,64,896]{2,1,0:T(8,128)(2,1)S(1)} all-to-all(bf16[4,64,896]{2,1,0:T(8,128)(2,1)S(1)} %get-tuple-element.24), channel_id=1, replica_groups={{4,6,0,2},{5,7,1,3},{12,14,8,10},{13,15,9,11},{20,22,16,18},{21,23,17,1..., dimensions={0} | all-to-all | bytes 917504 | tf_op jit(solution)/shard_map/all_to_all | solution.py:317
  58.9 0.6 shard_map.68
  59.5 0.1 reshape.26
  59.6 27.2 %all_to_all.22 = bf16[128,2,384]{2,1,0:T(2,128)(2,1)S(1)} all-to-all(bf16[128,2,384]{2,1,0:T(2,128)(2,1)S(1)} %reshape.26), channel_id=1, replica_groups={{272,273,280,281,288,289,296,297,304,305,312,313,320,321,328,329,336,33..., dimensions={0} | all-to-all | bytes 393216 | tf_op jit(solution)/shard_map/all_to_all | solution.py:312
  86.8 0.0 copy-done
  86.8 1.1 %shard_map.69 = bf16[2,128,384]{2,1,0:T(8,128)(2,1)} custom-call(s32[64,64]{1,0:T(8,128)S(1)} %copy-done, bf16[128,768]{1,0:T(8,128)(2,1)S(1)} %bitcast.9), custom_call_target="tpu_custom_call" | custom-call | tf_op jit(solution)/shard_map/pallas_call | solution.py:270
  (2 shorter events, 0.1 us)
Async XLA Ops:
  2.2 31.7 %all-to-all-start = ((bf16[128,4,128]{2,1,0:T(4,128)(2,1)}), bf16[128,4,128]{2,1,0:T(4,128)(2,1)S(1)}, u32[]{:S(2)}, u32[]{:S(2)}) async-start(bf16[128,4,128]{2,1,0:T(4,128)(2,1)} %bitcast.4), calls=%async_computation | async-start | bytes 262144 | tf_op jit(solution)/shard_map/all_to_all | solution.py:312
  26.9 7.0 %collective-permute-start = (bf16[384,3072]{1,0:T(8,128)(2,1)}, bf16[384,3072]{1,0:T(8,128)(2,1)S(1)}, u32[]{:S(2)}, u32[]{:S(2)}) collective-permute-start(bf16[384,3072]{1,0:T(8,128)(2,1)} %weight.1), channel_id=1, source_target_pairs={{0,1},{1,0},{2,3},{3,2},{4,5},{5,4},{6,7},{7,6},{8,9},{9,8},{10,11... | collective-permute-start | bytes 7077896 | tf_op jit(solution)/shard_map/ppermute | solution.py:331
  29.2 4.7 %collective-permute-start.1 = (bf16[512,384]{1,0:T(8,128)(2,1)S(1)}, bf16[512,384]{1,0:T(8,128)(2,1)S(1)}, u32[]{:S(2)}, u32[]{:S(2)}) collective-permute-start(bf16[512,384]{1,0:T(8,128)(2,1)S(1)} %shard_map.65), channel_id=1, source_target_pairs={{0,1},{1,0},{2,3},{3,2},{4,5},{5,4},{6,7},{7,6},{8,9},{9,8},{10,11... | collective-permute-start | bytes 1179656 | tf_op jit(solution)/shard_map/ppermute | solution.py:331
  49.6 37.3 %copy-start = (s32[64,64]{1,0:T(8,128)S(1)}, s32[64,64]{1,0:T(8,128)}, u32[]{:S(2)}) copy-start(s32[64,64]{1,0:T(8,128)} %requests_ref.1) | copy-start | bytes 49156

commit v10 on v9

--- a/solution.py
+++ b/solution.py
@@ -10,9 +10,10 @@
 DRAFT = 2
 LANES = 128
 EPSILON = 1e-06
-TURN = 34
+TURN = 46
 TURN_Y = 2
 HINT = 6 * 10**10
+BANDS = 2
 SLOT = 4
 
 bf16, f32, i32 = jnp.bfloat16, jnp.float32, jnp.int32
@@ -75,30 +76,34 @@
     rows, width = x_ref.shape
     slots = sent_ref.shape[0]
     parts = width // LANES
-    row_picks = [
-        (iota((blocks, rows), 1) == 2 * iota((blocks, rows), 0) + half).astype(bf16)
-        for half in range(2)
-    ]
-    index = iota((1, 2 * parts * blocks), 1)
-    piece, block = over(index, blocks), within(index, blocks)
-    slot = 2 * SLOT * block + jnp.where(piece < parts, piece, SLOT + piece - parts)
-    lay_out = (iota((slots, 2 * parts * blocks), 0) == slot).astype(bf16)
+    row_picks = jnp.concatenate(
+        [
+            (iota((blocks, rows), 1) == 2 * iota((blocks, rows), 0) + half).astype(bf16)
+            for half in range(2)
+        ]
+    )
+    piece = over(iota((1, 2 * parts * blocks), 1), blocks)
+    slot = iota((slots, 2 * parts * blocks), 0) - jnp.where(piece < parts, piece, SLOT + piece - parts)
     padding = within(iota((slots, 1), 0), SLOT) == parts
-    copies[0].wait()
-    halves = [mm(pick, x_ref[...]).astype(bf16) for pick in row_picks]
-    copies[1].wait()
-    places = holder_places(requests_ref[pl.ds(me, 1), :], kept)
-    pick = (places == iota((blocks, blocks), 0)).astype(bf16)
-    picked = [mm(pick, half).astype(bf16) for half in halves]
-    stacked = jnp.concatenate(
-        [half[:, part * LANES : (part + 1) * LANES] for half in picked for part in range(parts)]
-    )
     copies[2].wait()
     wanted = lax.rem(within(me + (blocks - TURN), blocks), 3 * parts)
     gain = jnp.zeros((1, LANES), f32)
     for part in range(parts):
         for number, value in enumerate(split(scale_ref[part : part + 1, :])):
             gain = jnp.where(wanted == 3 * part + number, value, gain)
+    copies[1].wait()
+    places = 2 * SLOT * holder_places(requests_ref[pl.ds(me, 1), :], kept)
+    places = jnp.concatenate([jnp.concatenate([places, places], axis=1)] * parts, axis=1)
+    lay_out = (slot == places).astype(bf16)
+    copies[0].wait()
+    halves = mm(row_picks, x_ref[...]).astype(bf16)
+    stacked = jnp.concatenate(
+        [
+            halves[half * blocks : (half + 1) * blocks, part * LANES : (part + 1) * LANES]
+            for half in range(2)
+            for part in range(parts)
+        ]
+    )
     sent_ref[...] = jnp.where(padding, gain, mm(lay_out, stacked)).astype(bf16)
     for copy in copies[3:]:
         copy.wait()
@@ -146,30 +151,18 @@
     return mm(turn.astype(bf16), held).astype(i32)
 
 
-def products(wide, kept, held, scale, weight, adapters, message_ref, arrived=lambda piece: None):
-    count, chip_width = wide.shape
-    rank_cols = adapters.shape[0] // 2
+def small_sums(wide, ranks, kept, held):
+    count, rank_cols = ranks.shape
     rank = rank_cols // kept
-    chips = message_ref.shape[0]
-    scaled = (wide * scale).astype(bf16)
+    owned = over(iota((count, rank_cols), 1), rank) == held[:, :1]
+    ranks = jnp.where(owned, ranks.astype(bf16), 0).astype(bf16)
+    fold = within(iota((rank_cols, LANES), 0), rank) == iota((rank_cols, LANES), 1)
+    sums = mm(ranks, fold.astype(bf16))
     squares = jnp.sum(wide * wide, axis=1, keepdims=True)
     top = squares.astype(bf16).astype(f32)
     lane = iota((count, LANES), 1)
-    fold = within(iota((rank_cols, LANES), 0), rank) == iota((rank_cols, LANES), 1)
-    owned = over(iota((count, rank_cols), 1), rank) == held[:, :1]
-    arrived(chips)
-    ranks = mm_t(scaled, adapters[:rank_cols]).astype(bf16)
-    ranks = jnp.where(owned, ranks, 0).astype(bf16)
-    extra = mm(ranks, fold.astype(bf16))
-    extra = jnp.where(lane == rank, top, extra)
-    extra = jnp.where(lane == rank + 1, squares - top, extra).astype(bf16)
-    for chip in range(chips):
-        place = within(chip + chips - TURN_Y, chips)
-        arrived(chip)
-        message_ref[place, :, :chip_width] = mm(
-            scaled, weight[:, chip * chip_width : (chip + 1) * chip_width]
-        ).astype(bf16)
-        message_ref[place, :, chip_width:] = extra
+    sums = jnp.where(lane == rank, top, sums)
+    return jnp.where(lane == rank + 1, squares - top, sums).astype(bf16)
 
 
 def update(wide, kept, held, got_ref, adapters):
@@ -194,28 +187,26 @@
     return (wide + total[:, :chip_width] * factor + delta).astype(bf16)
 
 
-def first_products(kept, x_ref, other_weight, others, weight, down, up, requests_hbm, *refs):
-    message_ref, wide_ref, scale_ref, held_ref, weight_out, adapters_out = refs[:6]
-    requests_ref, sems = refs[6:]
+def first_products(kept, x_ref, requests_ref, other_weight, others, own, weight_hbm, *refs):
+    message_ref, wide_ref, scale_ref, held_ref, weight, adapters, sems = refs
     groups, chip_width = wide_ref.shape
     width = chip_width // 2
-    rank_cols = adapters_out.shape[0] // 2
+    rank_cols = adapters.shape[0] // 2
     chips = message_ref.shape[0]
     first = lax.axis_index("c") == 0
-    mine = pl.ds(pl.multiple_of(jnp.where(first, 0, width), LANES), width)
-    other = pl.ds(pl.multiple_of(jnp.where(first, width, 0), LANES), width)
-    blocks = [pl.ds(chip * chip_width, chip_width) for chip in range(chips)]
-    copies = [(weight.at[:, cols], weight_out.at[mine, cols]) for cols in blocks]
-    copies += [
-        (down, adapters_out.at[:rank_cols, mine]),
-        (up, adapters_out.at[rank_cols:, mine]),
-        (requests_hbm, requests_ref),
+    my_place = pl.ds(pl.multiple_of(jnp.where(first, 0, width), LANES), width)
+    other_place = pl.ds(pl.multiple_of(jnp.where(first, width, 0), LANES), width)
+    columns = [pl.ds(chip * chip_width, chip_width) for chip in range(chips)]
+    band = width // BANDS
+    copies = [
+        pltpu.make_async_copy(
+            weight_hbm.at[pl.ds(index * band, band), :],
+            weight.at[pl.ds(pl.multiple_of(jnp.where(first, 0, width) + index * band, 16), band), :],
+            sems.at[index],
+        )
+        for index in range(BANDS)
     ]
-    copies = [
-        pltpu.make_async_copy(source, target, sems.at[index])
-        for index, (source, target) in enumerate(copies)
-    ]
-    for copy in [copies[-1], copies[chips]] + copies[:chips] + [copies[chips + 1]]:
+    for copy in copies:
         copy.start()
 
     rows = mm(unpack_picks(groups), x_ref[...])
@@ -229,18 +220,25 @@
     )
     wide_ref[...] = wide.astype(bf16)
     scale_ref[...] = scale
-    adapters_out[:, other] = others[...]
-    for cols in blocks:
-        weight_out[other, cols] = other_weight[:, cols]
-    copies[-1].wait()
+    scaled = (wide * scale).astype(bf16)
+    low, high = scaled[:, :width], scaled[:, width:]
+    mine, other = jnp.where(first, low, high), jnp.where(first, high, low)
+    sums = [mm(other, other_weight[:, cols]) for cols in columns]
     held = find_held(requests_ref[...], kept)
     held_ref[...] = held
-
-    def arrived(piece):
-        copies[piece].wait()
-
-    products(wide, kept, held, scale, weight_out, adapters_out, message_ref, arrived)
-    copies[chips + 1].wait()
+    ranks = mm_t(mine, own[:rank_cols]) + mm_t(other, others[:rank_cols])
+    small = small_sums(wide, ranks, kept, held)
+    adapters[:, my_place] = own[...]
+    adapters[:, other_place] = others[...]
+    for cols in columns:
+        weight[other_place, cols] = other_weight[:, cols]
+    for copy in copies:
+        copy.wait()
+    for chip, cols in enumerate(columns):
+        place = within(chip + chips - TURN_Y, chips)
+        product = sums[chip] + mm(mine, weight[my_place, cols])
+        message_ref[place, :, :chip_width] = product.astype(bf16)
+        message_ref[place, :, chip_width:] = small
 
 
 def next_products(kept, wide_ref, got_ref, held_ref, scale_ref, weight, adapters, *refs):
@@ -248,7 +246,18 @@
     held = held_ref[...]
     state = update(wide_ref[...].astype(f32), kept, held, got_ref, adapters)
     state_ref[...] = state
-    products(state.astype(f32), kept, held, scale_ref[...], weight, adapters, message_ref)
+    chips = message_ref.shape[0]
+    chip_width = state.shape[1]
+    wide = state.astype(f32)
+    scaled = (wide * scale_ref[...]).astype(bf16)
+    ranks = mm_t(scaled, adapters[: adapters.shape[0] // 2])
+    small = small_sums(wide, ranks, kept, held)
+    for chip in range(chips):
+        place = within(chip + chips - TURN_Y, chips)
+        message_ref[place, :, :chip_width] = mm(
+            scaled, weight[:, chip * chip_width : (chip + 1) * chip_width]
+        ).astype(bf16)
+        message_ref[place, :, chip_width:] = small
 
 
 def last_update(kept, state_ref, got_ref, held_ref, adapters, back_ref):
@@ -293,13 +302,16 @@
 
     down = jnp.transpose(down_weights, (0, 2, 1)).reshape(rank_cols, width)
     up = up_weights.reshape(rank_cols, width)
-    sent, adapters = call(
+    sent, adapters, near_requests = call(
         functools.partial(permute_in, kept),
-        [resident((SLOT * rows, LANES)), resident((2 * rank_cols, width))],
+        [
+            resident((SLOT * rows, LANES)),
+            resident((2 * rank_cols, width)),
+            resident(requests.shape, i32),
+        ],
         [requests, first_hidden_rows, norm_scale.reshape(-1, LANES), down, up],
         far=5,
         scratch_shapes=[
-            pltpu.VMEM(requests.shape, i32),
             pltpu.VMEM((rows, width), bf16),
             pltpu.VMEM((width // LANES, LANES), f32),
             pltpu.SemaphoreType.DMA((5,)),
@@ -343,12 +355,9 @@
             resident((chip_width, projection_weight.shape[1])),
             resident((2 * rank_cols, chip_width)),
         ],
-        [got, other_weight, other_adapters, projection_weight, down, up, requests],
-        far=4,
-        scratch_shapes=[
-            pltpu.VMEM(requests.shape, i32),
-            pltpu.SemaphoreType.DMA((chips + 3,)),
-        ],
+        [got, near_requests, other_weight, other_adapters, adapters, projection_weight],
+        far=1,
+        scratch_shapes=[pltpu.SemaphoreType.DMA((BANDS,))],
     )
     message, state = call(
         functools.partial(next_products, kept),

time: 88.3 us -> 87.6 us (level)
  starting transfers between devices: 29 us -> 26.2 us
  waiting for transfers between devices: 2.61 us -> 4.84 us
    all_to_all x1, starting transfers between devices: 24.7 us -> 21.8 us  [move(): lax.all_to_all(value, ('rep', 'c'), split_axis=0, concat_axis=0, axis_ind...]
    all_to_all x1, waiting for transfers between devices: 0.01 us -> 2.23 us  [move(): lax.all_to_all(value, ('rep', 'c'), split_axis=0, concat_axis=0, axis_ind...]
  transfers between devices with their start and end apart: 3 -> 3, of which waited for: 1 -> 2; matrix products, arithmetic and copies ran while one was open for 0% -> 0% of each run, Pallas kernels for 0% -> 0%
where the time goes in v10:
time: 87.6 us; the launch traced here: 87.2 us
  blocking collectives  48.1 us (55%)
  starting transfers between devices  26.2 us (30%)
  Pallas kernels  7.9 us (9%)
  waiting for transfers between devices  4.84 us (6%)
    all_to_all x1, blocking collectives, move(): lax.all_to_all(value, ('rep', 'c'), split_axis=0, concat_axis=0, axis_ind...  27.6 us
    all_to_all x1, starting transfers between devices, move(): lax.all_to_all(value, ('rep', 'c'), split_axis=0, concat_axis=0, axis_ind...  21.8 us
    all_to_all x2, blocking collectives, exchange(): lax.all_to_all(message, 'y', split_axis=0, concat_axis=0, axis_index_grou...  20.5 us
    pallas_call x6, Pallas kernels, call(): pl.pallas_call(kernel, out_shape=outs, in_specs=[pl.BlockSpec(memory_spac...  7.9 us
    ppermute x2, starting transfers between devices, shards(): lax.ppermute(value, 'c', sibling)  4.33 us
    ppermute x2, waiting for transfers between devices, shards(): lax.ppermute(value, 'c', sibling)  2.61 us
    all_to_all x1, waiting for transfers between devices, move(): lax.all_to_all(value, ('rep', 'c'), split_axis=0, concat_axis=0, axis_ind...  2.23 us
  transfers between devices with their start and end apart: 3, of which 2 were waited for; matrix products, arithmetic and copies ran while one was open for 0% of the time, Pallas kernels for 0%

profile of v10, /device:TPU:1, one launch (start us, length us, event | category | flops | bytes accessed | tf_op | source)
XLA Modules:
  0.0 87.2 jit_solution(13140125970354957558)
XLA Ops:
  0.0 2.0 %shard_map.64 = (bf16[512,128]{1,0:T(8,128)(2,1)}, bf16[512,384]{1,0:T(8,128)(2,1)S(1)}, s32[64,64]{1,0:T(8,128)S(1)}) custom-call(s32[64,64]{1,0:T(8,128)} %requests_ref.1, bf16[128,384]{1,0:T(8,128)(2,1)} %x_hbm.1, f32[3,128]{1,0:T(4,128)} %bitcast.14, bf16[256,384]{1,0:T(8,128)(2,1)} %bitcast.12, bf16[256,384]{1,0:T(8,128)(2,1)} %bitcast.13), custom_call_target="tpu_custom_call" | custom-call | tf_op jit(solution)/shard_map/pallas_call | solution.py:279
  2.0 21.8 %all-to-all-start = ((bf16[128,4,128]{2,1,0:T(4,128)(2,1)}), bf16[128,4,128]{2,1,0:T(4,128)(2,1)S(1)}, u32[]{:S(2)}, u32[]{:S(2)}) async-start(bf16[128,4,128]{2,1,0:T(4,128)(2,1)} %bitcast.4), calls=%async_computation | async-start | bytes 262144 | tf_op jit(solution)/shard_map/all_to_all | solution.py:324
  23.9 2.3 %collective-permute-start = (bf16[384,3072]{1,0:T(8,128)(2,1)}, bf16[384,3072]{1,0:T(8,128)(2,1)S(1)}, u32[]{:S(2)}, u32[]{:S(2)}) collective-permute-start(bf16[384,3072]{1,0:T(8,128)(2,1)} %weight_hbm.1), channel_id=1, source_target_pairs={{0,1},{1,0},{2,3},{3,2},{4,5},{5,4},{6,7},{7,6},{8,9},{9,8},{10,11... | collective-permute-start | bytes 7077896 | tf_op jit(solution)/shard_map/ppermute | solution.py:343
  26.2 2.1 %collective-permute-start.1 = (bf16[512,384]{1,0:T(8,128)(2,1)S(1)}, bf16[512,384]{1,0:T(8,128)(2,1)S(1)}, u32[]{:S(2)}, u32[]{:S(2)}) collective-permute-start(bf16[512,384]{1,0:T(8,128)(2,1)S(1)} %shard_map.65.own), channel_id=1, source_target_pairs={{0,1},{1,0},{2,3},{3,2},{4,5},{5,4},{6,7},{7,6},{8,9},{9,8},{10,11... | collective-permute-start | bytes 1179656 | tf_op jit(solution)/shard_map/ppermute | solution.py:343
  28.3 2.6 %collective-permute-done.1.others = bf16[512,384]{1,0:T(8,128)(2,1)S(1)} collective-permute-done((bf16[512,384]{1,0:T(8,128)(2,1)S(1)}, bf16[512,384]{1,0:T(8,128)(2,1)S(1)}, u32[]{:S(2)}, u32[]{:S(2)}) %collective-permute-start.1) | collective-permute-done | bytes 393248 | tf_op jit(solution)/shard_map/ppermute | solution.py:343
  30.9 2.2 %all-to-all-done = bf16[128,4,128]{2,1,0:T(4,128)(2,1)S(1)} async-done(((bf16[128,4,128]{2,1,0:T(4,128)(2,1)}), bf16[128,4,128]{2,1,0:T(4,128)(2,1)S(1)}, u32[]{:S(2)}, u32[]{:S(2)}) %all-to-all-start) | async-done | bytes 131104 | tf_op jit(solution)/shard_map/all_to_all | solution.py:324
  33.1 0.0 collective-permute-done.other_weight
  33.1 2.9 %shard_map.66 = (bf16[4,64,896]{2,1,0:T(8,128)(2,1)S(1)}, bf16[64,768]{1,0:T(8,128)(2,1)S(1)}, f32[1,768]{1,0:T(1,128)S(1)}, s32[64,128]{1,0:T(8,128)S(1)}, bf16...) custom-call(bf16[512,128]{1,0:T(8,128)(2,1)S(1)} %bitcast.10, s32[64,64]{1,0:T(8,128)S(1)} %get-tuple-element.17.requests_ref, ...), custom_call_target="tpu_custom_call" | custom-call | tf_op jit(solution)/shard_map/pallas_call | solution.py:279
  36.0 11.0 %all_to_all.20.got_ref = bf16[4,64,896]{2,1,0:T(8,128)(2,1)S(1)} all-to-all(bf16[4,64,896]{2,1,0:T(8,128)(2,1)S(1)} %get-tuple-element.20), channel_id=1, replica_groups={{4,6,0,2},{5,7,1,3},{12,14,8,10},{13,15,9,11},{20,22,16,18},{21,23,17,1..., dimensions={0} | all-to-all | bytes 917504 | tf_op jit(solution)/shard_map/all_to_all | solution.py:329
  47.0 1.3 %shard_map.67 = (bf16[4,64,896]{2,1,0:T(8,128)(2,1)S(1)}, bf16[64,768]{1,0:T(8,128)(2,1)S(1)}) custom-call(bf16[64,768]{1,0:T(8,128)(2,1)S(1)} %get-tuple-element.19.wide_ref, bf16[4,64,896]{2,1,0:T(8,128)(2,1)S(1)} %all_to_all.20.got_ref, s32[64,128]{1,0:T(8,128)S(1)} %get-tuple-element.21.held_ref, f32[1,768]{1,0:T(1,128)S(1)} %get-tuple-element.22.scale_ref, ...), custom_call_target="tpu_custom_call" | custom-call | tf_op jit(solution)/shard_map/pallas_call | solution.py:279
  48.3 0.0 copy-start
  48.3 9.5 %all_to_all.21.got_ref = bf16[4,64,896]{2,1,0:T(8,128)(2,1)S(1)} all-to-all(bf16[4,64,896]{2,1,0:T(8,128)(2,1)S(1)} %get-tuple-element.26), channel_id=1, replica_groups={{4,6,0,2},{5,7,1,3},{12,14,8,10},{13,15,9,11},{20,22,16,18},{21,23,17,1..., dimensions={0} | all-to-all | bytes 917504 | tf_op jit(solution)/shard_map/all_to_all | solution.py:329
  57.9 0.6 shard_map.68
  58.5 0.1 reshape.26
  58.5 27.6 %all_to_all.22 = bf16[128,2,384]{2,1,0:T(2,128)(2,1)S(1)} all-to-all(bf16[128,2,384]{2,1,0:T(2,128)(2,1)S(1)} %reshape.26), channel_id=1, replica_groups={{368,369,376,377,384,385,392,393,400,401,408,409,416,417,424,425,432,43..., dimensions={0} | all-to-all | bytes 393216 | tf_op jit(solution)/shard_map/all_to_all | solution.py:324
  86.1 0.0 copy-done
  86.1 1.1 %shard_map.69 = bf16[2,128,384]{2,1,0:T(8,128)(2,1)} custom-call(s32[64,64]{1,0:T(8,128)S(1)} %copy-done, bf16[128,768]{1,0:T(8,128)(2,1)S(1)} %bitcast.9), custom_call_target="tpu_custom_call" | custom-call | tf_op jit(solution)/shard_map/pallas_call | solution.py:279
  (2 shorter events, 0.1 us)
Async XLA Ops:
  2.0 31.1 %all-to-all-start = ((bf16[128,4,128]{2,1,0:T(4,128)(2,1)}), bf16[128,4,128]{2,1,0:T(4,128)(2,1)S(1)}, u32[]{:S(2)}, u32[]{:S(2)}) async-start(bf16[128,4,128]{2,1,0:T(4,128)(2,1)} %bitcast.4), calls=%async_computation | async-start | bytes 262144 | tf_op jit(solution)/shard_map/all_to_all | solution.py:324
  23.9 9.2 %collective-permute-start = (bf16[384,3072]{1,0:T(8,128)(2,1)}, bf16[384,3072]{1,0:T(8,128)(2,1)S(1)}, u32[]{:S(2)}, u32[]{:S(2)}) collective-permute-start(bf16[384,3072]{1,0:T(8,128)(2,1)} %weight_hbm.1), channel_id=1, source_target_pairs={{0,1},{1,0},{2,3},{3,2},{4,5},{5,4},{6,7},{7,6},{8,9},{9,8},{10,11... | collective-permute-start | bytes 7077896 | tf_op jit(solution)/shard_map/ppermute | solution.py:343
  26.2 4.7 %collective-permute-start.1 = (bf16[512,384]{1,0:T(8,128)(2,1)S(1)}, bf16[512,384]{1,0:T(8,128)(2,1)S(1)}, u32[]{:S(2)}, u32[]{:S(2)}) collective-permute-start(bf16[512,384]{1,0:T(8,128)(2,1)S(1)} %shard_map.65.own), channel_id=1, source_target_pairs={{0,1},{1,0},{2,3},{3,2},{4,5},{5,4},{6,7},{7,6},{8,9},{9,8},{10,11... | collective-permute-start | bytes 1179656 | tf_op jit(solution)/shard_map/ppermute | solution.py:343
  48.3 37.8 %copy-start = (s32[64,64]{1,0:T(8,128)S(1)}, s32[64,64]{1,0:T(8,128)}, u32[]{:S(2)}) copy-start(s32[64,64]{1,0:T(8,128)} %requests_ref.1) | copy-start | bytes 49156

commit v11 on v10

--- a/solution.py
+++ b/solution.py
@@ -13,7 +13,6 @@
 TURN = 46
 TURN_Y = 2
 HINT = 6 * 10**10
-BANDS = 2
 SLOT = 4
 
 bf16, f32, i32 = jnp.bfloat16, jnp.float32, jnp.int32
@@ -54,9 +53,7 @@
     return high, middle, values - high - middle
 
 
-def permute_in(kept, requests_hbm, x_hbm, scale_hbm, down_hbm, up_hbm, *refs):
-    sent_ref, adapters_ref, requests_ref, x_ref, scale_ref, sems = refs
-    rank_cols = down_hbm.shape[0]
+def permute_in(kept, requests_hbm, x_hbm, scale_hbm, sent_ref, requests_ref, x_ref, scale_ref, sems):
     copies = [
         pltpu.make_async_copy(source, target, sems.at[index])
         for index, (source, target) in enumerate(
@@ -64,8 +61,6 @@
                 (x_hbm, x_ref),
                 (requests_hbm, requests_ref),
                 (scale_hbm, scale_ref),
-                (down_hbm, adapters_ref.at[:rank_cols]),
-                (up_hbm, adapters_ref.at[rank_cols:]),
             )
         )
     ]
@@ -105,8 +100,6 @@
         ]
     )
     sent_ref[...] = jnp.where(padding, gain, mm(lay_out, stacked)).astype(bf16)
-    for copy in copies[3:]:
-        copy.wait()
 
 
 def permute_out(kept, requests_ref, home_ref, out_ref):
@@ -138,8 +131,16 @@
     return jnp.concatenate(picks)
 
 
-def pass_on(value_ref, out_ref):
-    out_ref[...] = value_ref[...]
+def pack(down_hbm, up_hbm, out_ref, sems):
+    rank_cols = down_hbm.shape[0]
+    copies = [
+        pltpu.make_async_copy(down_hbm, out_ref.at[:rank_cols], sems.at[0]),
+        pltpu.make_async_copy(up_hbm, out_ref.at[rank_cols:], sems.at[1]),
+    ]
+    for copy in copies:
+        copy.start()
+    for copy in copies:
+        copy.wait()
 
 
 def find_held(requests, kept):
@@ -197,17 +198,16 @@
     my_place = pl.ds(pl.multiple_of(jnp.where(first, 0, width), LANES), width)
     other_place = pl.ds(pl.multiple_of(jnp.where(first, width, 0), LANES), width)
     columns = [pl.ds(chip * chip_width, chip_width) for chip in range(chips)]
-    band = width // BANDS
+    half = chips // 2 * chip_width
     copies = [
         pltpu.make_async_copy(
-            weight_hbm.at[pl.ds(index * band, band), :],
-            weight.at[pl.ds(pl.multiple_of(jnp.where(first, 0, width) + index * band, 16), band), :],
-            sems.at[index],
+            weight_hbm.at[:, pl.ds(start, half)],
+            weight.at[my_place, pl.ds(start, half)],
+            sems.at[start // half],
         )
-        for index in range(BANDS)
+        for start in (0, half)
     ]
-    for copy in copies:
-        copy.start()
+    copies[0].start()
 
     rows = mm(unpack_picks(groups), x_ref[...])
     parts = 2 * (SLOT - 1)
@@ -232,10 +232,11 @@
     adapters[:, other_place] = others[...]
     for cols in columns:
         weight[other_place, cols] = other_weight[:, cols]
-    for copy in copies:
-        copy.wait()
+    copies[1].start()
     for chip, cols in enumerate(columns):
         place = within(chip + chips - TURN_Y, chips)
+        if chip % (chips // 2) == 0:
+            copies[chip * 2 // chips].wait()
         product = sums[chip] + mm(mine, weight[my_place, cols])
         message_ref[place, :, :chip_width] = product.astype(bf16)
         message_ref[place, :, chip_width:] = small
@@ -302,19 +303,18 @@
 
     down = jnp.transpose(down_weights, (0, 2, 1)).reshape(rank_cols, width)
     up = up_weights.reshape(rank_cols, width)
-    sent, adapters, near_requests = call(
+    sent, near_requests = call(
         functools.partial(permute_in, kept),
         [
             resident((SLOT * rows, LANES)),
-            resident((2 * rank_cols, width)),
             resident(requests.shape, i32),
         ],
-        [requests, first_hidden_rows, norm_scale.reshape(-1, LANES), down, up],
-        far=5,
+        [requests, first_hidden_rows, norm_scale.reshape(-1, LANES)],
+        far=3,
         scratch_shapes=[
             pltpu.VMEM((rows, width), bf16),
             pltpu.VMEM((width // LANES, LANES), f32),
-            pltpu.SemaphoreType.DMA((5,)),
+            pltpu.SemaphoreType.DMA((3,)),
         ],
     )
     movers = [[(place + TURN * cores) % rows for place in range(rows)]]
@@ -333,9 +333,11 @@
     got = move(sent.reshape(rows, SLOT, LANES)).reshape(SLOT * rows, LANES)
 
     (adapters,) = call(
-        pass_on,
-        [resident(adapters.shape)],
-        [adapters],
+        pack,
+        [resident((2 * rank_cols, width))],
+        [down, up],
+        far=2,
+        scratch_shapes=[pltpu.SemaphoreType.DMA((2,))],
         cost_estimate=pl.CostEstimate(flops=HINT, bytes_accessed=0, transcendentals=0),
     )
     sibling = [(core, cores - 1 - core) for core in range(cores)]
@@ -357,7 +359,7 @@
         ],
         [got, near_requests, other_weight, other_adapters, adapters, projection_weight],
         far=1,
-        scratch_shapes=[pltpu.SemaphoreType.DMA((BANDS,))],
+        scratch_shapes=[pltpu.SemaphoreType.DMA((2,))],
     )
     message, state = call(
         functools.partial(next_products, kept),

time: 87.6 us -> 87.7 us (level)
  Pallas kernels: 7.9 us -> 8.92 us
  waiting for transfers between devices: 4.84 us -> 3.83 us
    pallas_call x6, Pallas kernels: 7.9 us -> 8.92 us  [call(): pl.pallas_call(kernel, out_shape=outs, in_specs=[pl.BlockSpec(memory_spac...]
    ppermute x2, waiting for transfers between devices: 2.61 us -> 1.6 us  [shards(): lax.ppermute(value, 'c', sibling)]
  transfers between devices with their start and end apart: 3 -> 3, of which waited for: 2 -> 2; matrix products, arithmetic and copies ran while one was open for 0% -> 0% of each run, Pallas kernels for 0% -> 1%
where the time goes in v11:
time: 87.7 us; the launch traced here: 87.2 us
  blocking collectives  48.1 us (55%)
  starting transfers between devices  26.2 us (30%)
  Pallas kernels  8.92 us (10%)
  waiting for transfers between devices  3.83 us (4%)
    all_to_all x1, blocking collectives, move(): lax.all_to_all(value, ('rep', 'c'), split_axis=0, concat_axis=0, axis_ind...  27.6 us
    all_to_all x1, starting transfers between devices, move(): lax.all_to_all(value, ('rep', 'c'), split_axis=0, concat_axis=0, axis_ind...  21.8 us
    all_to_all x2, blocking collectives, exchange(): lax.all_to_all(message, 'y', split_axis=0, concat_axis=0, axis_index_grou...  20.5 us
    pallas_call x6, Pallas kernels, call(): pl.pallas_call(kernel, out_shape=outs, in_specs=[pl.BlockSpec(memory_spac...  8.92 us
    ppermute x2, starting transfers between devices, shards(): lax.ppermute(value, 'c', sibling)  4.33 us
    all_to_all x1, waiting for transfers between devices, move(): lax.all_to_all(value, ('rep', 'c'), split_axis=0, concat_axis=0, axis_ind...  2.23 us
  transfers between devices with their start and end apart: 3, of which 2 were waited for; matrix products, arithmetic and copies ran while one was open for 0% of the time, Pallas kernels for 1%

profile of v11, /device:TPU:1, one launch (start us, length us, event | category | flops | bytes accessed | tf_op | source)
XLA Modules:
  0.0 87.2 jit_solution(11686491404456930564)
XLA Ops:
  0.0 2.0 %shard_map.64 = (bf16[512,128]{1,0:T(8,128)(2,1)}, s32[64,64]{1,0:T(8,128)S(1)}) custom-call(s32[64,64]{1,0:T(8,128)} %requests_ref.1, bf16[128,384]{1,0:T(8,128)(2,1)} %x_hbm.1, f32[3,128]{1,0:T(4,128)} %bitcast.12), custom_call_target="tpu_custom_call" | custom-call | tf_op jit(solution)/shard_map/pallas_call | solution.py:280
  2.0 21.8 %all-to-all-start = ((bf16[128,4,128]{2,1,0:T(4,128)(2,1)}), bf16[128,4,128]{2,1,0:T(4,128)(2,1)S(1)}, u32[]{:S(2)}, u32[]{:S(2)}) async-start(bf16[128,4,128]{2,1,0:T(4,128)(2,1)} %bitcast.1), calls=%async_computation | async-start | bytes 262144 | tf_op jit(solution)/shard_map/all_to_all | solution.py:324
  23.9 2.3 %collective-permute-start = (bf16[384,3072]{1,0:T(8,128)(2,1)}, bf16[384,3072]{1,0:T(8,128)(2,1)S(1)}, u32[]{:S(2)}, u32[]{:S(2)}) collective-permute-start(bf16[384,3072]{1,0:T(8,128)(2,1)} %weight_hbm.1), channel_id=1, source_target_pairs={{0,1},{1,0},{2,3},{3,2},{4,5},{5,4},{6,7},{7,6},{8,9},{9,8},{10,11... | collective-permute-start | bytes 7077896 | tf_op jit(solution)/shard_map/ppermute | solution.py:345
  26.1 1.0 %shard_map.65.own = bf16[512,384]{1,0:T(8,128)(2,1)S(1)} custom-call(bf16[256,384]{1,0:T(8,128)(2,1)} %bitcast.13, bf16[256,384]{1,0:T(8,128)(2,1)} %bitcast.14), custom_call_target="tpu_custom_call" | custom-call | flops 60000002048 | tf_op jit(solution)/shard_map/pallas_call | solution.py:280
  27.2 2.1 %collective-permute-start.1 = (bf16[512,384]{1,0:T(8,128)(2,1)S(1)}, bf16[512,384]{1,0:T(8,128)(2,1)S(1)}, u32[]{:S(2)}, u32[]{:S(2)}) collective-permute-start(bf16[512,384]{1,0:T(8,128)(2,1)S(1)} %shard_map.65.own), channel_id=1, source_target_pairs={{0,1},{1,0},{2,3},{3,2},{4,5},{5,4},{6,7},{7,6},{8,9},{9,8},{10,11... | collective-permute-start | bytes 1179656 | tf_op jit(solution)/shard_map/ppermute | solution.py:345
  29.3 1.6 %collective-permute-done.1.others = bf16[512,384]{1,0:T(8,128)(2,1)S(1)} collective-permute-done((bf16[512,384]{1,0:T(8,128)(2,1)S(1)}, bf16[512,384]{1,0:T(8,128)(2,1)S(1)}, u32[]{:S(2)}, u32[]{:S(2)}) %collective-permute-start.1) | collective-permute-done | bytes 393248 | tf_op jit(solution)/shard_map/ppermute | solution.py:345
  30.9 2.2 %all-to-all-done = bf16[128,4,128]{2,1,0:T(4,128)(2,1)S(1)} async-done(((bf16[128,4,128]{2,1,0:T(4,128)(2,1)}), bf16[128,4,128]{2,1,0:T(4,128)(2,1)S(1)}, u32[]{:S(2)}, u32[]{:S(2)}) %all-to-all-start) | async-done | bytes 131104 | tf_op jit(solution)/shard_map/all_to_all | solution.py:324
  33.1 0.0 collective-permute-done.other_weight
  33.1 2.9 %shard_map.66 = (bf16[4,64,896]{2,1,0:T(8,128)(2,1)S(1)}, bf16[64,768]{1,0:T(8,128)(2,1)S(1)}, f32[1,768]{1,0:T(1,128)S(1)}, s32[64,128]{1,0:T(8,128)S(1)}, bf16...) custom-call(bf16[512,128]{1,0:T(8,128)(2,1)S(1)} %bitcast.10, s32[64,64]{1,0:T(8,128)S(1)} %get-tuple-element.16.requests_ref, ...), custom_call_target="tpu_custom_call" | custom-call | tf_op jit(solution)/shard_map/pallas_call | solution.py:280
  36.0 11.0 %all_to_all.20.got_ref = bf16[4,64,896]{2,1,0:T(8,128)(2,1)S(1)} all-to-all(bf16[4,64,896]{2,1,0:T(8,128)(2,1)S(1)} %get-tuple-element.18), channel_id=1, replica_groups={{4,6,0,2},{5,7,1,3},{12,14,8,10},{13,15,9,11},{20,22,16,18},{21,23,17,1..., dimensions={0} | all-to-all | bytes 917504 | tf_op jit(solution)/shard_map/all_to_all | solution.py:329
  47.0 1.3 %shard_map.67 = (bf16[4,64,896]{2,1,0:T(8,128)(2,1)S(1)}, bf16[64,768]{1,0:T(8,128)(2,1)S(1)}) custom-call(bf16[64,768]{1,0:T(8,128)(2,1)S(1)} %get-tuple-element.17.wide_ref, bf16[4,64,896]{2,1,0:T(8,128)(2,1)S(1)} %all_to_all.20.got_ref, s32[64,128]{1,0:T(8,128)S(1)} %get-tuple-element.19.held_ref, f32[1,768]{1,0:T(1,128)S(1)} %get-tuple-element.20.scale_ref, ...), custom_call_target="tpu_custom_call" | custom-call | tf_op jit(solution)/shard_map/pallas_call | solution.py:280
  48.4 0.0 copy-start
  48.4 9.5 %all_to_all.21.got_ref = bf16[4,64,896]{2,1,0:T(8,128)(2,1)S(1)} all-to-all(bf16[4,64,896]{2,1,0:T(8,128)(2,1)S(1)} %get-tuple-element.24), channel_id=1, replica_groups={{4,6,0,2},{5,7,1,3},{12,14,8,10},{13,15,9,11},{20,22,16,18},{21,23,17,1..., dimensions={0} | all-to-all | bytes 917504 | tf_op jit(solution)/shard_map/all_to_all | solution.py:329
  57.9 0.6 shard_map.68
  58.5 0.1 reshape.26
  58.5 27.6 %all_to_all.22 = bf16[128,2,384]{2,1,0:T(2,128)(2,1)S(1)} all-to-all(bf16[128,2,384]{2,1,0:T(2,128)(2,1)S(1)} %reshape.26), channel_id=1, replica_groups={{368,369,376,377,384,385,392,393,400,401,408,409,416,417,424,425,432,43..., dimensions={0} | all-to-all | bytes 393216 | tf_op jit(solution)/shard_map/all_to_all | solution.py:324
  86.2 0.0 copy-done
  86.2 1.1 %shard_map.69 = bf16[2,128,384]{2,1,0:T(8,128)(2,1)} custom-call(s32[64,64]{1,0:T(8,128)S(1)} %copy-done, bf16[128,768]{1,0:T(8,128)(2,1)S(1)} %bitcast.9), custom_call_target="tpu_custom_call" | custom-call | tf_op jit(solution)/shard_map/pallas_call | solution.py:280
  (1 shorter events, 0.0 us)
Async XLA Ops:
  2.0 31.1 %all-to-all-start = ((bf16[128,4,128]{2,1,0:T(4,128)(2,1)}), bf16[128,4,128]{2,1,0:T(4,128)(2,1)S(1)}, u32[]{:S(2)}, u32[]{:S(2)}) async-start(bf16[128,4,128]{2,1,0:T(4,128)(2,1)} %bitcast.1), calls=%async_computation | async-start | bytes 262144 | tf_op jit(solution)/shard_map/all_to_all | solution.py:324
  23.9 9.2 %collective-permute-start = (bf16[384,3072]{1,0:T(8,128)(2,1)}, bf16[384,3072]{1,0:T(8,128)(2,1)S(1)}, u32[]{:S(2)}, u32[]{:S(2)}) collective-permute-start(bf16[384,3072]{1,0:T(8,128)(2,1)} %weight_hbm.1), channel_id=1, source_target_pairs={{0,1},{1,0},{2,3},{3,2},{4,5},{5,4},{6,7},{7,6},{8,9},{9,8},{10,11... | collective-permute-start | bytes 7077896 | tf_op jit(solution)/shard_map/ppermute | solution.py:345
  27.2 3.7 %collective-permute-start.1 = (bf16[512,384]{1,0:T(8,128)(2,1)S(1)}, bf16[512,384]{1,0:T(8,128)(2,1)S(1)}, u32[]{:S(2)}, u32[]{:S(2)}) collective-permute-start(bf16[512,384]{1,0:T(8,128)(2,1)S(1)} %shard_map.65.own), channel_id=1, source_target_pairs={{0,1},{1,0},{2,3},{3,2},{4,5},{5,4},{6,7},{7,6},{8,9},{9,8},{10,11... | collective-permute-start | bytes 1179656 | tf_op jit(solution)/shard_map/ppermute | solution.py:345
  48.4 37.8 %copy-start = (s32[64,64]{1,0:T(8,128)S(1)}, s32[64,64]{1,0:T(8,128)}, u32[]{:S(2)}) copy-start(s32[64,64]{1,0:T(8,128)} %requests_ref.1) | copy-start | bytes 49156
